TPU v7x, 256 devices: a whole 4x4x8 slice. The times are simulated.
256 devices in a mesh: wide: 32 (over y, z), hist: 8 (over x, core).
Axes of the slice: x: 4, y: 4, z: 8, core: 2. Of those that a mesh axis runs over, the one named last changes fastest.
Arguments:
- x_home: bfloat16 [262144, 256], P(('wide', 'hist')), may hold values from -6 to 6
- cotangent: bfloat16 [262144, 256], P(('wide', 'hist')), may hold values from -6 to 6
- owner: int32 [262144, 1], P(('wide', 'hist')), may hold values from 0 to 31; in each aligned block of 1024 rows (0 to 1023, 1024 to 2047, ...) at most 64 rows name the same one
- weights: bfloat16 [2, 256, 256], replicated, may hold values from -0.375 to 0.375
- history: bfloat16 [2, 8192, 256], P(None, 'hist'), may hold values from -6 to 6
- halo_ids: int32 [32, 8, 8, 64], P('wide', 'hist'), may hold values from 0 to 1023
- halo_count: int32 [32, 8, 8], P('wide', 'hist'), may hold values from 1 to 64, as said below
- tile_rows: int32 [32, 8, 96], P('wide', 'hist'), may hold values from 0 to 15
- tile_cols: int32 [32, 8, 96], P('wide', 'hist'), may hold values from 0 to 19
- tile_count: int32 [32, 8], P('wide', 'hist'), may hold values from 32 to 96, as said below
- tile_vals: bfloat16 [32, 8, 96, 128, 128], P('wide', 'hist'), may hold values from -0.21875 to 0.21875
Outputs:
- second_out: bfloat16 [262144, 256], P(('wide', 'hist'))
- weight_grads: float32 [2, 256, 256], replicated
Inputs may be any that keep to these rules, and one draw needn't show every extreme that they name: At most 64 rows of one device name the same owner; in every draw some device sends exactly 64 rows to one owner. `halo_ids`: row numbers within one table shard; slots at or past the count are ignored. `halo_count`: some owner uses all 64 slots of some shard in every draw. `tile_cols`: column tiles 16 and above are the halo's. `tile_count`: some owner uses all 96 slots in every draw.
All inputs are finite; a program needn't handle non-finite values.
Results may differ from a plain program's by a relative error of at most 0.0055.
Values may be sent and summed in bfloat16 or wider, within the bound.
No kernel may reach another device: no remote copies, remote signals or barrier semaphores. Data moves between devices by JAX's collectives and lax.ppermute only.
A program may use at most 128 MiB of HBM per device.

v0:
```python
import math

import jax
import jax.numpy as jnp
from jax import lax
from jax.sharding import PartitionSpec as P

ALPHA = 0.1
BETAS = (math.log(1.5), math.log(1.25))


def slope(pre):
    sig = jax.nn.sigmoid(pre)
    return sig * (1.0 + pre * (1.0 - sig))


def spread(ext, vals, cols, select_rows, tile, width):
    tiles = ext.reshape(-1, tile, width)[cols]
    prod = jnp.einsum("kij,kjd->kid", vals, tiles, preferred_element_type=jnp.float32)
    return jnp.einsum("kr,kid->rid", select_rows, prod, precision=lax.Precision.HIGHEST).reshape(
        -1, width
    )


def forward_pass(ws_x, valid, halo, weights, rows, cols, count, vals):
    work, width = ws_x.shape
    tile = vals.shape[-1]
    slots = vals.shape[0]
    live = (jnp.arange(slots) < count).astype(jnp.float32)
    select_rows = (rows[:, None] == jnp.arange(work // tile)[None, :]).astype(jnp.float32) * live[
        :, None
    ]
    h0f = ws_x.astype(jnp.float32)
    keep = valid.astype(jnp.float32)[:, None]
    prev = ws_x
    saved = []
    for layer in range(2):
        ext = jnp.concatenate([prev, halo[layer]], axis=0)
        support = spread(ext, vals, cols, select_rows, tile, width)
        mixed = (1.0 - ALPHA) * support + ALPHA * h0f
        mixed_b = mixed.astype(jnp.bfloat16)
        pre = (1.0 - BETAS[layer]) * mixed + BETAS[layer] * jnp.dot(
            mixed_b, weights[layer], preferred_element_type=jnp.float32
        )
        prev = (jax.nn.silu(pre) * keep).astype(jnp.bfloat16)
        saved.append((mixed_b, pre))
    return (prev, saved, live, keep)


def backward_pass(ws_cot, saved, live, keep, weights, rows, cols, vals):
    work, width = ws_cot.shape
    tile = vals.shape[-1]
    select_back = (cols[:, None] == jnp.arange(work // tile)[None, :]).astype(jnp.float32) * live[
        :, None
    ]
    grad_two = ws_cot.astype(jnp.float32) * keep * slope(saved[1][1])
    grad_two_b = grad_two.astype(jnp.bfloat16)
    weight_two = BETAS[1] * jnp.dot(saved[1][0].T, grad_two_b, preferred_element_type=jnp.float32)
    grad_mix = (1.0 - BETAS[1]) * grad_two + BETAS[1] * jnp.dot(
        grad_two_b, weights[1].T, preferred_element_type=jnp.float32
    )
    grad_mix_b = grad_mix.astype(jnp.bfloat16)
    gathered = grad_mix_b.reshape(-1, tile, width)[rows]
    back_prod = jnp.einsum("kij,kid->kjd", vals, gathered, preferred_element_type=jnp.float32)
    back = jnp.einsum(
        "kc,kjd->cjd", select_back, back_prod, precision=lax.Precision.HIGHEST
    ).reshape(-1, width)
    grad_one = (1.0 - ALPHA) * back * keep * slope(saved[0][1])
    grad_one_b = grad_one.astype(jnp.bfloat16)
    weight_one = BETAS[0] * jnp.dot(saved[0][0].T, grad_one_b, preferred_element_type=jnp.float32)
    return jnp.stack([weight_one, weight_two])


def local(
    x_home,
    cotangent,
    owner,
    weights,
    history,
    halo_ids,
    halo_count,
    tile_rows,
    tile_cols,
    tile_count,
    tile_vals,
):
    n_wide = lax.axis_size("wide")
    rows_here, width = x_home.shape
    cap = 2 * rows_here // n_wide
    work = 2 * rows_here
    owners = owner[:, 0]
    onehot = (owners[:, None] == jnp.arange(n_wide)[None, :]).astype(jnp.int32)
    rank = jnp.sum((jnp.cumsum(onehot, axis=0) - onehot) * onehot, axis=1)
    place = owners * cap + rank
    send_x = jnp.zeros((work, width), jnp.bfloat16).at[place].set(x_home)
    send_cot = jnp.zeros((work, width), jnp.bfloat16).at[place].set(cotangent)
    send_mark = jnp.zeros((work,), jnp.bfloat16).at[place].set(jnp.ones((rows_here,), jnp.bfloat16))
    ws_x, ws_mark, ws_cot = (
        lax.all_to_all(send_x, "wide", split_axis=0, concat_axis=0, tiled=True),
        lax.all_to_all(send_mark, "wide", split_axis=0, concat_axis=0, tiled=True),
        lax.all_to_all(send_cot, "wide", split_axis=0, concat_axis=0, tiled=True),
    )
    asked = halo_ids[0, 0]
    hcap = asked.shape[1]
    incoming = lax.all_to_all(asked, "hist", split_axis=0, concat_axis=0, tiled=True)
    picked = history[:, incoming.reshape(-1)]
    halo = lax.all_to_all(picked, "hist", split_axis=1, concat_axis=1, tiled=True)
    live_halo = (jnp.arange(hcap)[None, :] < halo_count[0, 0][:, None]).reshape(-1)
    halo = jnp.where(live_halo[None, :, None], halo, jnp.zeros((), jnp.bfloat16))
    rows = tile_rows[0, 0]
    cols = tile_cols[0, 0]
    count = tile_count[0, 0]
    vals = tile_vals[0, 0]
    second_ws, saved, live, keep = forward_pass(
        ws_x, ws_mark, halo, weights, rows, cols, count, vals
    )
    returned = lax.all_to_all(second_ws, "wide", split_axis=0, concat_axis=0, tiled=True)
    second_out = returned[place]
    grads = backward_pass(ws_cot, saved, live, keep, weights, rows, cols, vals)
    total = lax.psum(grads, ("wide", "hist"))
    return (second_out, total)


def solution(mesh):
    placed = (
        P(("wide", "hist"), None),
        P(("wide", "hist"), None),
        P(("wide", "hist"), None),
        P(),
        P(None, "hist", None),
        P("wide", "hist", None, None),
        P("wide", "hist", None),
        P("wide", "hist", None),
        P("wide", "hist", None),
        P("wide", "hist"),
        P("wide", "hist", None, None, None),
    )
    return jax.shard_map(
        local,
        mesh=mesh,
        in_specs=placed,
        out_specs=(P(("wide", "hist"), None), P()),
        check_vma=False,
    )
```

profile of v0, /device:TPU:1, one launch (start us, length us, event | category | flops | bytes accessed | tf_op | source)
XLA Modules:
  0.0 530.8 jit_solution(18246913975836110841)
XLA Ops:
  7.2 6.7 %all-to-all-start.1 = ((s32[8,1,64]{2,1,0:T(1,128)}), s32[8,1,64]{2,1,0:T(1,128)S(1)}, u32[]{:S(2)}, u32[]{:S(2)}) async-start(s32[8,1,64]{2,1,0:T(1,128)} %bitcast.139), calls=%async_computation.1 | async-start | bytes 8192 | tf_op jit(solution)/shard_map/all_to_all | solution.py:105
  14.6 9.0 %reduce-window.6 = s32[32,8,128]{2,1,0:T(8,128)S(1)} reduce-window(s32[32,8,128]{2,1,0:T(8,128)S(1)} %fusion.27, s32[]{:T(128)} %constant.19.clone.1), window={size=1x1x128 pad=0_0x0_0x127_0}, to_apply=%region_0.0 | reduce-window | flops 4161536 | bytes 262148 | tf_op jit(solution)/shard_map/reduce-window
  24.1 0.7 fusion.22
  25.5 7.6 %scatter_custom_fusion.1 = bf16[2048]{0:T(1024)(128)(2,1)S(1)} fusion(s32[1024]{0:T(1024)S(1)} %bitcast.134, bf16[1024]{0:T(1024)(128)(2,1)S(1)} %broadcast.128, bf16[]{:T(256)} %constant.17.clone.1), kind=kCustom, calls=%fused_computation.99 | custom fusion | bytes 4098 | tf_op jit(solution)/shard_map/scatter | solution.py:97
  33.8 10.6 %all-to-all-start.3 = ((bf16[32,64,1]{1,2,0:T(2,128)(2,1)}), bf16[32,64,1]{1,2,0:T(2,128)(2,1)S(1)}, u32[]{:S(2)}, u32[]{:S(2)}) async-start(bf16[32,64,1]{1,2,0:T(2,128)(2,1)} %all_to_all.50), calls=%async_computation.3 | async-start | bytes 32768 | tf_op jit(solution)/shard_map/all_to_all | solution.py:100
  45.6 6.3 %gather_fusion = bf16[512,2,256]{2,0,1:T(8,128)(2,1)} fusion(bf16[2,1024,256]{2,1,0:T(8,128)(2,1)} %param.15, s32[1024]{0:T(1024)S(1)} %pad_clamp_fusion.2), kind=kCustom, calls=%fused_computation | custom fusion | bytes 1050624 | tf_op jit(solution)/shard_map/gather | solution.py:106
  51.9 2.4 copy.40
  54.3 5.1 all-to-all-start.2
  59.4 6.4 %scatter_custom_fusion = bf16[2048,256]{1,0:T(8,128)(2,1)} fusion(s32[1024]{0:T(1024)S(1)} %bitcast.135, bf16[1024,256]{1,0:T(8,128)(2,1)} %param.11, bf16[]{:T(256)} %constant.17.clone.1), kind=kCustom, calls=%fused_computation.52 | custom fusion | bytes 1049088 | tf_op jit(solution)/shard_map/scatter | solution.py:95
  65.8 3.2 all-to-all-done.2
  69.0 9.8 %all-to-all-start = ((bf16[32,64,256]{2,1,0:T(8,128)(2,1)}), bf16[32,64,256]{2,1,0:T(8,128)(2,1)}, u32[]{:S(2)}, u32[]{:S(2)}) async-start(bf16[32,64,256]{2,1,0:T(8,128)(2,1)} %bitcast.124), calls=%async_computation | async-start | bytes 2097152 | tf_op jit(solution)/shard_map/all_to_all | solution.py:99
  78.8 6.4 %scatter_custom_fusion.2 = bf16[2048,256]{1,0:T(8,128)(2,1)} fusion(s32[1024]{0:T(1024)S(1)} %bitcast.136, bf16[1024,256]{1,0:T(8,128)(2,1)} %param.12, bf16[]{:T(256)} %constant.17.clone.1), kind=kCustom, calls=%fused_computation.50 | custom fusion | bytes 1049088 | tf_op jit(solution)/shard_map/scatter | solution.py:96
  86.2 1.2 copy_select_fusion
  87.4 0.7 slice_bitcast_fusion.1
  88.2 15.3 %all-to-all-done = bf16[32,64,256]{2,1,0:T(8,128)(2,1)} async-done(((bf16[32,64,256]{2,1,0:T(8,128)(2,1)}), bf16[32,64,256]{2,1,0:T(8,128)(2,1)}, u32[]{:S(2)}, u32[]{:S(2)}) %all-to-all-start) | async-done | bytes 1048608 | tf_op jit(solution)/shard_map/all_to_all | solution.py:99
  103.4 8.7 %all-to-all-start.5 = ((bf16[32,64,256]{2,1,0:T(8,128)(2,1)}), bf16[32,64,256]{2,1,0:T(8,128)(2,1)}, u32[]{:S(2)}, u32[]{:S(2)}) async-start(bf16[32,64,256]{2,1,0:T(8,128)(2,1)} %bitcast.123), calls=%async_computation.5 | async-start | bytes 2097152 | tf_op jit(solution)/shard_map/all_to_all | solution.py:101
  112.1 2.5 pad_maximum_fusion
  114.6 7.3 %gather_fusion.1 = bf16[96,128,256]{2,1,0:T(8,128)(2,1)} fusion(bf16[20,128,256]{2,1,0:T(8,128)(2,1)} %bitcast.120, s32[1024]{0:T(1024)S(1)} %pad_clamp_fusion.1), kind=kCustom, calls=%fused_computation.1 | custom fusion | bytes 12583296 | tf_op jit(solution)/shard_map/gather | solution.py:18
  121.8 9.2 %convolution_bitcast_fusion.2 = f32[96,128,256]{1,2,0:T(8,128)} fusion(bf16[96,128,256]{2,1,0:T(8,128)(2,1)} %gather_fusion.1, bf16[1,1,96,128,128]{4,3,2,1,0:T(8,128)(2,1)S(1)} %copy-done), kind=kOutput, calls=%fused_computation.10 | convolution fusion | flops 805306368 | bytes 22020096 | tf_op jit(solution)/shard_map/kij,kjd->kid/dot_general | solution.py:19
  131.0 12.8 %copy.43 = f32[96,128,256]{2,0,1:T(8,128)} copy(f32[96,128,256]{1,2,0:T(8,128)} %convolution_bitcast_fusion.2) | data formatting | bytes 25165824 | tf_op jit(solution)/shard_map/kij,kjd->kid/dot_general | solution.py:19
  143.7 1.5 convert_multiply_fusion.1
  145.2 10.5 %add_convert_fusion.1 = (bf16[16,128,256]{2,0,1:T(8,128)(2,1)S(1)}, f32[16,128,256]{2,0,1:T(8,128)S(1)}) fusion(f32[16,128,256]{2,1,0:T(8,128)S(1)} %bitcast.121, f32[96,128,256]{2,0,1:T(8,128)} %copy.43, f32[96]{0:T(128)S(1)} %compare_convert_fusion, s32[96]{0:T(128)S(1)} %bitcast.140), kind=kOutput, calls=%fused_computation.33 | convolution fusion | flops 605555712 | bytes 17826560 | tf_op jit(solution)/shard_map/kr,kid->rid/dot_general | solution.py:20
  156.1 1.2 copy.44
  157.3 1.7 bitcast_add_fusion.1
  159.0 2.2 multiply_convert_fusion.1
  161.2 1.2 pad_maximum_fusion.1
  162.4 7.7 %gather_fusion.2 = bf16[96,128,256]{2,1,0:T(8,128)(2,1)} fusion(bf16[20,128,256]{2,1,0:T(8,128)(2,1)} %bitcast.119, s32[1024]{0:T(1024)S(1)} %pad_clamp_fusion.1), kind=kCustom, calls=%fused_computation.2 | custom fusion | bytes 12583296 | tf_op jit(solution)/shard_map/gather | solution.py:18
  170.1 9.2 %convolution_bitcast_fusion.1 = f32[96,128,256]{1,2,0:T(8,128)} fusion(bf16[96,128,256]{2,1,0:T(8,128)(2,1)} %gather_fusion.2, bf16[1,1,96,128,128]{4,3,2,1,0:T(8,128)(2,1)S(1)} %copy-done), kind=kOutput, calls=%fused_computation.9 | convolution fusion | flops 805306368 | bytes 22020096 | tf_op jit(solution)/shard_map/kij,kjd->kid/dot_general | solution.py:19
  179.2 12.8 %copy.49 = f32[96,128,256]{2,0,1:T(8,128)} copy(f32[96,128,256]{1,2,0:T(8,128)} %convolution_bitcast_fusion.1) | data formatting | bytes 25165824 | tf_op jit(solution)/shard_map/kij,kjd->kid/dot_general | solution.py:19
  192.0 10.2 %add_convert_fusion = (bf16[16,128,256]{2,0,1:T(8,128)(2,1)S(1)}, f32[16,128,256]{2,0,1:T(8,128)S(1)}) fusion(f32[16,128,256]{2,1,0:T(8,128)} %bitcast.122, f32[96,128,256]{2,0,1:T(8,128)} %copy.49, f32[96]{0:T(128)S(1)} %compare_convert_fusion, s32[96]{0:T(128)S(1)} %bitcast.141), kind=kOutput, calls=%fused_computation.30 | convolution fusion | flops 605555712 | bytes 17826560 | tf_op jit(solution)/shard_map/kr,kid->rid/dot_general | solution.py:20
  202.2 1.3 copy.52
  203.5 1.2 copy.50
  204.7 3.0 bitcast_add_fusion
  207.7 5.2 fusion.7
  213.0 9.3 %all-to-all-start.4 = ((bf16[32,64,256]{2,1,0:T(8,128)(2,1)}), bf16[32,64,256]{2,1,0:T(8,128)(2,1)}, u32[]{:S(2)}, u32[]{:S(2)}) async-start(bf16[32,64,256]{2,1,0:T(8,128)(2,1)} %bitcast.126), calls=%async_computation.4 | async-start | bytes 2097152 | tf_op jit(solution)/shard_map/all_to_all | solution.py:117
  222.5 3.7 fusion.6
  226.2 7.2 %gather_fusion.4 = bf16[96,128,256]{2,1,0:T(8,128)(2,1)} fusion(bf16[16,128,256]{2,1,0:T(8,128)(2,1)} %bitcast.118, s32[1024]{0:T(1024)S(1)} %pad_clamp_fusion), kind=kCustom, calls=%fused_computation.4 | custom fusion | bytes 12583296 | tf_op jit(solution)/shard_map/gather | solution.py:63
  233.4 9.2 %convolution_bitcast_fusion = f32[96,128,256]{1,2,0:T(8,128)} fusion(bf16[96,128,256]{2,1,0:T(8,128)(2,1)} %gather_fusion.4, bf16[1,1,96,128,128]{4,3,2,1,0:T(8,128)(2,1)S(1)} %copy-done), kind=kOutput, calls=%fused_computation.8 | convolution fusion | flops 805306368 | bytes 22020096 | tf_op jit(solution)/shard_map/kij,kid->kjd/dot_general | solution.py:64
  242.6 12.8 %copy.54 = f32[96,128,256]{2,0,1:T(8,128)} copy(f32[96,128,256]{1,2,0:T(8,128)} %convolution_bitcast_fusion) | data formatting | bytes 25165824 | tf_op jit(solution)/shard_map/kij,kid->kjd/dot_general | solution.py:64
  255.3 8.9 %fusion.30 = f32[16,128,256]{2,0,1:T(8,128)S(1)} fusion(f32[96,128,256]{2,0,1:T(8,128)} %copy.54, s32[96]{0:T(128)S(1)} %bitcast.142, f32[96]{0:T(128)S(1)} %compare_convert_fusion), kind=kOutput, calls=%fused_computation.73 | convolution fusion | flops 603982848 | bytes 14680832 | tf_op jit(solution)/shard_map/kc,kjd->cjd/dot_general | solution.py:65
  264.3 1.2 copy.55
  265.9 0.8 fusion.9
  266.6 0.8 copy-done.3
  268.1 1.1 copy-done.4
  269.7 0.8 pad_maximum_fusion.2
  270.6 6.0 %gather_fusion.3 = bf16[1024,256]{1,0:T(8,128)(2,1)} fusion(bf16[2048,256]{1,0:T(8,128)(2,1)} %bitcast.32, s32[1024]{0:T(1024)S(1)} %broadcast_clamp_fusion), kind=kCustom, calls=%fused_computation.3 | custom fusion | bytes 1052672 | tf_op jit(solution)/shard_map/gather | solution.py:118
  276.6 245.3 %all-reduce.2.cloned.1.call-done = f32[2,256,256]{2,1,0:T(8,128)} async-done(((f32[2,256,256]{2,1,0:T(8,128)}), f32[2,256,256]{2,1,0:T(8,128)}) %all-reduce.2.cloned.1.call-update) | async-done | bytes 524304 | tf_op jit(solution)/shard_map/psum | solution.py:120
  521.9 1.9 copy.66
  (57 shorter events, 6.2 us)
Async XLA Ops:
  7.2 114.7 %copy-start = (bf16[1,1,96,128,128]{4,3,2,1,0:T(8,128)(2,1)S(1)}, bf16[1,1,96,128,128]{4,3,2,1,0:T(8,128)(2,1)}, u32[]{:S(2)}) copy-start(bf16[1,1,96,128,128]{4,3,2,1,0:T(8,128)(2,1)} %param.21) | copy-start | bytes 9437188
  7.2 26.6 %all-to-all-start.1 = ((s32[8,1,64]{2,1,0:T(1,128)}), s32[8,1,64]{2,1,0:T(1,128)S(1)}, u32[]{:S(2)}, u32[]{:S(2)}) async-start(s32[8,1,64]{2,1,0:T(1,128)} %bitcast.139), calls=%async_computation.1 | async-start | bytes 8192 | tf_op jit(solution)/shard_map/all_to_all | solution.py:105
  33.8 20.5 %all-to-all-start.3 = ((bf16[32,64,1]{1,2,0:T(2,128)(2,1)}), bf16[32,64,1]{1,2,0:T(2,128)(2,1)S(1)}, u32[]{:S(2)}, u32[]{:S(2)}) async-start(bf16[32,64,1]{1,2,0:T(2,128)(2,1)} %all_to_all.50), calls=%async_computation.3 | async-start | bytes 32768 | tf_op jit(solution)/shard_map/all_to_all | solution.py:100
  54.3 14.7 %all-to-all-start.2 = ((bf16[2,512,256]{2,0,1:T(2,128)(2,1)}), bf16[2,512,256]{2,0,1:T(2,128)(2,1)}, u32[]{:S(2)}, u32[]{:S(2)}) async-start(bf16[2,512,256]{2,0,1:T(2,128)(2,1)} %copy.40), calls=%async_computation.2 | async-start | bytes 1048576 | tf_op jit(solution)/shard_map/all_to_all | solution.py:107
  59.4 25.8 %copy-start.11 = (s32[1,1,8]{2,1,0:T(1,128)S(1)}, s32[1,1,8]{2,1,0:T(1,128)}, u32[]{:S(2)}) copy-start(s32[1,1,8]{2,1,0:T(1,128)} %param.17) | copy-start | bytes 100
  59.4 26.7 %copy-start.10 = (s32[1,1,96]{2,1,0:T(1,128)S(1)}, s32[1,1,96]{2,1,0:T(1,128)}, u32[]{:S(2)}) copy-start(s32[1,1,96]{2,1,0:T(1,128)} %param.19) | copy-start | bytes 1156
  59.4 26.7 %copy-start.9 = (s32[1,1,96]{2,1,0:T(1,128)S(1)}, s32[1,1,96]{2,1,0:T(1,128)}, u32[]{:S(2)}) copy-start(s32[1,1,96]{2,1,0:T(1,128)} %param.18) | copy-start | bytes 1156
  69.0 34.5 %all-to-all-start = ((bf16[32,64,256]{2,1,0:T(8,128)(2,1)}), bf16[32,64,256]{2,1,0:T(8,128)(2,1)}, u32[]{:S(2)}, u32[]{:S(2)}) async-start(bf16[32,64,256]{2,1,0:T(8,128)(2,1)} %bitcast.124), calls=%async_computation | async-start | bytes 2097152 | tf_op jit(solution)/shard_map/all_to_all | solution.py:99
  103.4 104.3 %all-to-all-start.5 = ((bf16[32,64,256]{2,1,0:T(8,128)(2,1)}), bf16[32,64,256]{2,1,0:T(8,128)(2,1)}, u32[]{:S(2)}, u32[]{:S(2)}) async-start(bf16[32,64,256]{2,1,0:T(8,128)(2,1)} %bitcast.123), calls=%async_computation.5 | async-start | bytes 2097152 | tf_op jit(solution)/shard_map/all_to_all | solution.py:101
  145.2 10.5 %copy-start.1 = (f32[32,64,256]{2,1,0:T(8,128)}, f32[32,64,256]{2,1,0:T(8,128)S(1)}, u32[]{:S(2)}) copy-start(f32[32,64,256]{2,1,0:T(8,128)S(1)} %convert_multiply_fusion.1) | copy-start | bytes 6291460
  157.3 1.7 copy-start.7
  159.0 2.2 copy-start.2
  204.7 3.0 copy-start.8
  213.0 57.6 %all-to-all-start.4 = ((bf16[32,64,256]{2,1,0:T(8,128)(2,1)}), bf16[32,64,256]{2,1,0:T(8,128)(2,1)}, u32[]{:S(2)}, u32[]{:S(2)}) async-start(bf16[32,64,256]{2,1,0:T(8,128)(2,1)} %bitcast.126), calls=%async_computation.4 | async-start | bytes 2097152 | tf_op jit(solution)/shard_map/all_to_all | solution.py:117
  222.3 299.6 %all-reduce.2.cloned.1.call-start = ((), (), s32[]{:S(2)}) async-start(), calls=%async_computation.6 | async-start | bytes 1048576 | tf_op jit(solution)/shard_map/psum | solution.py:120
  264.3 1.6 copy-start.6
  265.9 1.6 copy-start.3
  265.9 2.2 copy-start.5
  267.4 1.7 copy-start.4
Sparse Core Ops, SparseCore 0:
  270.7 251.1 all-reduce.1
where the time goes:
time: 541 us; the launch traced here: 531 us
  waiting for transfers between devices  264 us (49%)
  local copies, waits for them, and re-layouts  107 us (20%)
  matrix products  69.2 us (13%)
  starting transfers between devices  50.4 us (9%)
  other arithmetic  24.7 us (5%)
  between operations  15.2 us (3%)
    psum x1, waiting for transfers between devices, local(): total = lax.psum(grads, ('wide', 'hist'))  245 us
    dot_general x2, local copies, waits for them, and re-layouts, spread(): jnp.einsum('kij,kjd->kid', vals, tiles, preferred_element_type=jnp.float32)  25.5 us
    dot_general x2, matrix products, spread(): jnp.einsum('kr,kid->rid', select_rows, prod, precision=lax.Precision.HIGH...  20.7 us
    dot_general x2, matrix products, spread(): jnp.einsum('kij,kjd->kid', vals, tiles, preferred_element_type=jnp.float32)  18.3 us
    all_to_all x1, waiting for transfers between devices, local(): lax.all_to_all(send_x, 'wide', split_axis=0, concat_axis=0, tiled=True)  15.3 us
    gather x2, local copies, waits for them, and re-layouts, spread(): tiles = ext.reshape(-1, tile, width)[cols]  14.9 us
    dot_general x1, local copies, waits for them, and re-layouts, backward_pass(): jnp.einsum('kij,kid->kjd', vals, gathered, preferred_element_type=jnp.flo...  12.8 us
  transfers between devices with their start and end apart: 7, of which 3 were waited for; matrix products, arithmetic and copies ran while one was open for 36% of the time, Pallas kernels for 0%

commit v1 on v0

v1 whole, which is shorter than its diff:
```python
import math

import jax
import jax.numpy as jnp
from jax import lax
from jax.experimental import pallas as pl
from jax.experimental.pallas import tpu as pltpu
from jax.sharding import PartitionSpec as P

ALPHA = 0.1
BETAS = (math.log(1.5), math.log(1.25))
TILE = 128
CAP = 64
HCAP = 64
MARK = 1024.0
LIMIT = 512.0
BF16 = jnp.bfloat16
F32 = jnp.float32
MIB = 1 << 20


def vmem(count):
    return [pl.BlockSpec(memory_space=pltpu.VMEM)] * count


def smem(count):
    return [pl.BlockSpec(memory_space=pltpu.SMEM)] * count


def cost(flops, moved):
    return pl.CostEstimate(flops=flops, bytes_accessed=moved, transcendentals=0)


def dot(a, b):
    return jnp.dot(a, b, preferred_element_type=F32)


def dot_rows(a, b):
    return lax.dot_general(a, b, (((0,), (0,)), ((), ())), preferred_element_type=F32)


def route_body(n_wide, own_ref, x_ref, cot_ref, send_ref, place_ref):
    rows_here = own_ref.shape[1]
    width = x_ref.shape[1]
    blocks = rows_here // 128
    own = own_ref[...]
    ids = lax.broadcasted_iota(jnp.int32, (n_wide, 128), 0)
    hot = [(own[:, 128 * b : 128 * (b + 1)] == ids).astype(F32) for b in range(blocks)]
    lower = lax.broadcasted_iota(jnp.int32, (128, 128), 0)
    upper = lax.broadcasted_iota(jnp.int32, (128, 128), 1)
    earlier = (lower < upper).astype(F32).astype(BF16)
    inside = dot(jnp.concatenate(hot, axis=0).astype(BF16), earlier)
    before = jnp.zeros((n_wide, 1), F32)
    ranks = []
    for b in range(blocks):
        seen = inside[n_wide * b : n_wide * (b + 1)] + before
        ranks.append(jnp.sum(seen * hot[b], axis=0, keepdims=True))
        before = before + jnp.sum(hot[b], axis=1, keepdims=True)
    place = own * CAP + jnp.concatenate(ranks, axis=1).astype(jnp.int32)
    place_ref[...] = place
    step = 256
    base = lax.broadcasted_iota(jnp.int32, (step, rows_here), 0)
    for c in range(send_ref.shape[0] // step):
        hit = (base == place - c * step).astype(F32)
        held = jnp.max(hit, axis=1, keepdims=True)
        hit = hit.astype(BF16)
        x_part = jnp.where(held > 0.5, dot(hit, x_ref[...]), MARK)
        send_ref[pl.ds(c * step, step), :width] = x_part.astype(BF16)
        send_ref[pl.ds(c * step, step), width:] = dot(hit, cot_ref[...]).astype(BF16)


def prepare_body(rows_ref, cols_ref, count_ref, place_ref, vals_ref, adj_ref, column_ref, head, following):
    adj_ref[...] = jnp.zeros_like(adj_ref)
    count = count_ref[0]
    wide = adj_ref.shape[1] // TILE

    def clear(k, carry):
        head[rows_ref[k] * wide + cols_ref[k]] = -1
        return carry

    lax.fori_loop(0, count, clear, 0)

    def chain(i, carry):
        k = count - 1 - i
        cell = rows_ref[k] * wide + cols_ref[k]
        following[k] = head[cell]
        head[cell] = k
        return carry

    lax.fori_loop(0, count, chain, 0)

    def fill(k, carry):
        row, col = rows_ref[k], cols_ref[k]

        @pl.when(head[row * wide + col] == k)
        def _():
            def more(state):
                at, total = state
                return following[at], total + vals_ref[at].astype(F32)

            _, total = lax.while_loop(
                lambda state: state[0] >= 0, more, (following[k], vals_ref[k].astype(F32))
            )
            adj_ref[
                pl.ds(pl.multiple_of(row * TILE, TILE), TILE),
                pl.ds(pl.multiple_of(col * TILE, TILE), TILE),
            ] = total.astype(BF16)

        return carry

    lax.fori_loop(0, count, fill, 0)
    for b in range(place_ref.shape[1] // 128):
        part = place_ref[:, 128 * b : 128 * (b + 1)].astype(F32)
        column_ref[pl.ds(128 * b, 128), :] = jnp.transpose(jnp.broadcast_to(part, (128, 128)))


def pick_body(ids_ref, history_ref, *piece_refs):
    slots = ids_ref.shape[0]
    here = history_ref.shape[1]
    lane = lax.broadcasted_iota(jnp.int32, (slots, 128), 1)
    ids = ids_ref[...]
    hit = jnp.concatenate(
        [(ids - 128 * c == lane).astype(F32).astype(BF16) for c in range(here // 128)], axis=1
    )
    for layer in range(2):
        rows = dot(hit, history_ref[layer]).astype(BF16)
        for k, piece_ref in enumerate(piece_refs):
            piece_ref[pl.ds(layer * HCAP, HCAP), :] = rows[k * HCAP : (k + 1) * HCAP]


def forward_body(turn_ref, ws_ref, adj_ref, w_ref, *rest):
    n_hist = (len(rest) - 7)
    pieces = rest[:n_hist]
    out_ref, m1_ref, m2_ref, s1_ref, s2_ref, ext0, ext1 = rest[n_hist:]
    work, width = out_ref.shape
    turn = turn_ref[0]
    for layer, ext in enumerate((ext0, ext1)):
        for k, piece in enumerate(pieces):
            shard = lax.rem(turn + k, n_hist)
            at = pl.multiple_of(work + shard * HCAP, HCAP)
            ext[pl.ds(at, HCAP), :] = piece[pl.ds(layer * HCAP, HCAP), :]
    step = 512
    for b in range(work // step):
        part = pl.ds(b * step, step)
        got = ws_ref[part, :width].astype(F32)
        ext0[part, :] = jnp.where(got < LIMIT, got, 0.0).astype(BF16)
    for layer in range(2):
        ext, m_ref, s_ref = ((ext0, m1_ref, s1_ref), (ext1, m2_ref, s2_ref))[layer]
        beta = BETAS[layer]
        for b in range(work // step):
            part = pl.ds(b * step, step)
            support = dot(adj_ref[part, :], ext[...])
            mixed = (1.0 - ALPHA) * support + ALPHA * ext0[part, :].astype(F32)
            mixed_b = mixed.astype(BF16)
            m_ref[part, :] = mixed_b
            pre = (1.0 - beta) * mixed + beta * dot(mixed_b, w_ref[layer])
            sig = jax.nn.sigmoid(pre)
            keep = ws_ref[part, :width].astype(F32) < LIMIT
            new = jnp.where(keep, pre * sig, 0.0).astype(BF16)
            s_ref[part, :] = jnp.where(keep, sig * (1.0 + pre * (1.0 - sig)), 0.0)
            if layer == 0:
                ext1[part, :] = new
            else:
                out_ref[part, :] = new


def backward_body(ws_ref, adj_ref, w_ref, m1_ref, m2_ref, s1_ref, s2_ref, grads_ref, turned):
    work, width = m1_ref.shape
    step = 512
    beta = BETAS[1]
    total = jnp.zeros((width, width), F32)
    for b in range(work // step):
        part = pl.ds(b * step, step)
        grad_two = ws_ref[part, width:].astype(F32) * s2_ref[part, :]
        grad_two_b = grad_two.astype(BF16)
        total = total + dot_rows(m2_ref[part, :], grad_two_b)
        through = lax.dot_general(
            grad_two_b, w_ref[1], (((1,), (1,)), ((), ())), preferred_element_type=F32
        )
        grad_mix = (1.0 - beta) * grad_two + beta * through
        turned[:, pl.ds(b * step, step)] = jnp.transpose(grad_mix.astype(BF16))
    grads_ref[1] = BETAS[1] * total
    total = jnp.zeros((width, width), F32)
    for b in range(work // step):
        part = pl.ds(b * step, step)
        back = jnp.transpose(dot(turned[...], adj_ref[:, pl.ds(b * step, step)]))
        grad_one = (1.0 - ALPHA) * back * s1_ref[part, :]
        total = total + dot_rows(m1_ref[part, :], grad_one.astype(BF16))
    grads_ref[0] = BETAS[0] * total


def collect_body(column_ref, back_ref, out_ref):
    slots = back_ref.shape[0]
    step = 256
    lane = lax.broadcasted_iota(jnp.int32, (step, 128), 1).astype(F32)
    for b in range(out_ref.shape[0] // step):
        part = pl.ds(b * step, step)
        place = column_ref[part, :]
        hit = jnp.concatenate(
            [(place - 128.0 * c == lane).astype(F32).astype(BF16) for c in range(slots // 128)],
            axis=1,
        )
        out_ref[part, :] = dot(hit, back_ref[...]).astype(BF16)


def local(
    x_home,
    cotangent,
    owner,
    weights,
    history,
    halo_ids,
    halo_count,
    tile_rows,
    tile_cols,
    tile_count,
    tile_vals,
):
    n_wide = lax.axis_size("wide")
    n_hist = lax.axis_size("hist")
    turn = lax.axis_index("hist")
    rows_here, width = x_home.shape
    work = n_wide * CAP
    halo = n_hist * HCAP
    slots = tile_vals.shape[2]
    params = pltpu.CompilerParams(vmem_limit_bytes=48 * MIB)

    send, place = pl.pallas_call(
        lambda *refs: route_body(n_wide, *refs),
        out_shape=(
            jax.ShapeDtypeStruct((work, 2 * width), BF16),
            jax.ShapeDtypeStruct((1, rows_here), jnp.int32),
        ),
        in_specs=vmem(3),
        out_specs=tuple(vmem(2)),
        compiler_params=params,
        cost_estimate=cost(4 * work * rows_here * width, 3 * MIB),
        name="route",
    )(owner.reshape(1, rows_here), x_home, cotangent)
    ws = lax.all_to_all(
        send.reshape(n_wide, CAP, 2 * width), "wide", split_axis=0, concat_axis=0, tiled=True
    ).reshape(work, 2 * width)

    live = jnp.arange(HCAP)[None, :] < halo_count[0, 0][:, None]
    wanted = jnp.where(live, halo_ids[0, 0], -1)
    wanted, place = lax.optimization_barrier((wanted, place))
    wanted = lax.dynamic_slice_in_dim(jnp.concatenate([wanted, wanted]), turn, n_hist, axis=0)

    def shift(value, by):
        return lax.ppermute(value, "hist", [(i, (i + by) % n_hist) for i in range(n_hist)])

    asked = [wanted[0]] + [shift(wanted[k], k) for k in range(1, n_hist)]
    asked = jnp.broadcast_to(jnp.stack(asked).reshape(halo, 1), (halo, 128))
    picked = pl.pallas_call(
        pick_body,
        out_shape=tuple(jax.ShapeDtypeStruct((2 * HCAP, width), BF16) for _ in range(n_hist)),
        in_specs=vmem(2),
        out_specs=tuple(vmem(n_hist)),
        compiler_params=params,
        cost_estimate=cost(4 * halo * history.shape[1] * width, 2 * MIB),
        name="pick",
    )(asked, history)
    pieces = [picked[0]] + [shift(picked[k], n_hist - k) for k in range(1, n_hist)]

    adjacency, column = pl.pallas_call(
        prepare_body,
        out_shape=(
            jax.ShapeDtypeStruct((work, work + halo), BF16),
            jax.ShapeDtypeStruct((rows_here, 128), F32),
        ),
        in_specs=smem(3) + vmem(2),
        out_specs=tuple(vmem(2)),
        scratch_shapes=[
            pltpu.SMEM(((work // TILE) * ((work + halo) // TILE),), jnp.int32),
            pltpu.SMEM((slots,), jnp.int32),
        ],
        compiler_params=params,
        cost_estimate=cost(0, 24 * MIB),
        name="prepare",
    )(tile_rows[0, 0], tile_cols[0, 0], tile_count[0], place, tile_vals[0, 0])

    second, m1, m2, s1, s2 = pl.pallas_call(
        forward_body,
        out_shape=tuple(
            jax.ShapeDtypeStruct((work, width), kind) for kind in (BF16, BF16, BF16, F32, F32)
        ),
        in_specs=smem(1) + vmem(3 + n_hist),
        out_specs=tuple(vmem(5)),
        scratch_shapes=[pltpu.VMEM((work + halo, width), BF16)] * 2,
        compiler_params=params,
        cost_estimate=cost(4 * work * (work + halo + width) * width, 24 * MIB),
        name="forward",
    )(turn.reshape(1), ws, adjacency, weights, *pieces)
    returned = lax.all_to_all(
        second.reshape(n_wide, CAP, width), "wide", split_axis=0, concat_axis=0, tiled=True
    ).reshape(work, width)

    grads = pl.pallas_call(
        backward_body,
        out_shape=jax.ShapeDtypeStruct((2, width, width), F32),
        in_specs=vmem(7),
        out_specs=vmem(1)[0],
        scratch_shapes=[pltpu.VMEM((width, work), BF16)],
        compiler_params=params,
        cost_estimate=cost(2 * work * (work + 3 * width) * width, 20 * MIB),
        name="backward",
    )(ws, adjacency, weights, m1, m2, s1, s2)

    second_out = pl.pallas_call(
        collect_body,
        out_shape=jax.ShapeDtypeStruct((rows_here, width), BF16),
        in_specs=vmem(2),
        out_specs=vmem(1)[0],
        compiler_params=params,
        cost_estimate=cost(2 * work * rows_here * width, 2 * MIB),
        name="collect",
    )(column, returned)

    n_all = n_wide * n_hist
    lanes = 128
    chunk = 2 * width * width // n_all // lanes
    both = ("wide", "hist")
    parts = lax.all_to_all(
        grads.reshape(n_all, chunk, lanes), both, split_axis=0, concat_axis=0, tiled=True
    )
    mine = jnp.sum(parts, axis=0, keepdims=True)
    total = lax.all_to_all(
        jnp.broadcast_to(mine, (n_all, chunk, lanes)), both, split_axis=0, concat_axis=0, tiled=True
    ).reshape(2, width, width)
    return (second_out, total)


def solution(mesh):
    placed = (
        P(("wide", "hist"), None),
        P(("wide", "hist"), None),
        P(("wide", "hist"), None),
        P(),
        P(None, "hist", None),
        P("wide", "hist", None, None),
        P("wide", "hist", None),
        P("wide", "hist", None),
        P("wide", "hist", None),
        P("wide", "hist"),
        P("wide", "hist", None, None, None),
    )
    return jax.shard_map(
        local,
        mesh=mesh,
        in_specs=placed,
        out_specs=(P(("wide", "hist"), None), P()),
        check_vma=False,
    )
```

time: 541 us -> 196 us (0.36); the launches traced: 531 us -> 196 us
  waiting for transfers between devices: 264 us -> 64.5 us
  local copies, waits for them, and re-layouts: 107 us -> 12.7 us
  matrix products: 69.2 us -> 0 us
  Pallas kernels: 0 us -> 42.1 us
  blocking collectives: 0 us -> 31.2 us
  other arithmetic: 24.7 us -> 0.36 us
  between operations: 15.2 us -> 1.49 us
  starting transfers between devices: 50.4 us -> 43.6 us
    psum x1 -> x0, waiting for transfers between devices: 245 us -> none  [local(): total = lax.psum(grads, ('wide', 'hist'))]
    dot_general x11 -> x0, matrix products: 69.2 us -> none  [the longest x2 20.7 us: spread(): jnp.einsum('kr,kid->rid', select_rows, prod, precision=lax.Precision.HIGH...]
    all_to_all x6 -> x3, waiting for transfers between devices: 18.5 us -> 62.1 us  [the longest x1 24.3 us: local(): lax.all_to_all(second.reshape(n_wide, CAP, width), 'wide', split_axis=0,...]
    pallas_call x0 -> x6, Pallas kernels: none -> 42.1 us  [the longest x1 18.9 us: local(): pl.pallas_call(forward_body, out_shape=tuple((jax.ShapeDtypeStruct((work,...]
    dot_general x4 -> x0, local copies, waits for them, and re-layouts: 39.5 us -> none  [the longest x2 25.5 us: spread(): jnp.einsum('kij,kjd->kid', vals, tiles, preferred_element_type=jnp.float32)]
    gather x6 -> x0, local copies, waits for them, and re-layouts: 36.7 us -> none  [the longest x2 14.9 us: spread(): tiles = ext.reshape(-1, tile, width)[cols]]
    all_to_all x0 -> x1, blocking collectives: none -> 31.2 us  [local(): lax.all_to_all(grads.reshape(n_all, chunk, lanes), both, split_axis=0, co...]
    all_to_all x6 -> x3, starting transfers between devices: 50.1 us -> 27.5 us  [the longest x1 12.2 us: local(): lax.all_to_all(send.reshape(n_wide, CAP, 2 * width), 'wide', split_axis=0...]
  transfers between devices with their start and end apart: 7 -> 17, of which waited for: 3 -> 5; matrix products, arithmetic and copies ran while one was open for 36% -> 0% of each run, Pallas kernels for 0% -> 5%
where the time goes in v1:
time: 196 us
  waiting for transfers between devices  64.5 us (33%)
  starting transfers between devices  43.6 us (22%)
  Pallas kernels  42.1 us (21%)
  blocking collectives  31.2 us (16%)
  local copies, waits for them, and re-layouts  12.7 us (6%)
    all_to_all x1, blocking collectives, local(): lax.all_to_all(grads.reshape(n_all, chunk, lanes), both, split_axis=0, co...  31.2 us
    all_to_all x1, waiting for transfers between devices, local(): lax.all_to_all(second.reshape(n_wide, CAP, width), 'wide', split_axis=0,...  24.3 us
    all_to_all x1, waiting for transfers between devices, local(): lax.all_to_all(send.reshape(n_wide, CAP, 2 * width), 'wide', split_axis=0...  19.3 us
    pallas_call x1, Pallas kernels, local(): pl.pallas_call(forward_body, out_shape=tuple((jax.ShapeDtypeStruct((work,...  18.9 us
    all_to_all x1, waiting for transfers between devices, local(): lax.all_to_all(jnp.broadcast_to(mine, (n_all, chunk, lanes)), both, split...  18.4 us
    ppermute x14, starting transfers between devices, shift(): lax.ppermute(value, 'hist', [(i, (i + by) % n_hist) for i in range(n_hist)])  16.1 us
    all_to_all x1, starting transfers between devices, local(): lax.all_to_all(send.reshape(n_wide, CAP, 2 * width), 'wide', split_axis=0...  12.2 us
    all_to_all x1, starting transfers between devices, local(): lax.all_to_all(jnp.broadcast_to(mine, (n_all, chunk, lanes)), both, split...  11.4 us
  transfers between devices with their start and end apart: 17, of which 5 were waited for; matrix products, arithmetic and copies ran while one was open for 0% of the time, Pallas kernels for 5%

profile of v1, /device:TPU:1, one launch (start us, length us, event | category | flops | bytes accessed | tf_op | source)
XLA Modules:
  0.0 195.9 jit_solution(9238366810154371558)
XLA Ops:
  0.6 1.0 copy-done.9
  1.7 1.0 copy-done.10
  2.7 0.7 copy-done.11
  3.4 3.7 %route.1 = (bf16[2048,512]{1,0:T(8,128)(2,1)S(1)}, s32[1,1024]{1,0:T(1,128)S(1)}) custom-call(s32[1,1024]{1,0:T(1,128)S(1)} %bitcast.42, bf16[1024,256]{1,0:T(8,128)(2,1)S(1)} %copy-done.9, bf16[1024,256]{1,0:T(8,128)(2,1)S(1)} %copy-done.10), custom_call_target="tpu_custom_call" | custom-call | flops 2147483648 | bytes 3145728 | tf_op jit(solution)/shard_map/route/pallas_call | solution.py:228
  7.2 1.4 copy-done.4
  8.5 12.2 %all-to-all-start = ((bf16[32,64,512]{2,1,0:T(8,128)(2,1)}), bf16[32,64,512]{2,1,0:T(8,128)(2,1)S(1)}, u32[]{:S(2)}, u32[]{:S(2)}) async-start(bf16[32,64,512]{2,1,0:T(8,128)(2,1)} %bitcast.38), calls=%async_computation | async-start | bytes 4194304 | tf_op jit(solution)/shard_map/all_to_all | solution.py:240
  20.7 0.0 copy-start.6
  20.7 0.0 copy-start.7
  20.7 0.1 bitcast_select_fusion
  20.8 1.0 collective-permute-start.6
  21.8 2.5 %collective-permute-start.5 = (s32[64]{0:T(128)S(1)}, s32[64]{0:T(128)S(1)}, u32[]{:S(2)}, u32[]{:S(2)}) collective-permute-start(s32[64]{0:T(128)S(1)} %get-tuple-element.41), channel_id=1, source_target_pairs={{0,6},{1,7},{2,0},{3,1},{4,2},{5,3},{6,4},{7,5},{8,14},{9,15},{10,... | collective-permute-start | bytes 776 | tf_op jit(solution)/shard_map/ppermute | solution.py:250
  24.3 0.8 collective-permute-start.4
  25.1 2.1 %collective-permute-start.3 = (s32[64]{0:T(128)S(1)}, s32[64]{0:T(128)S(1)}, u32[]{:S(2)}, u32[]{:S(2)}) collective-permute-start(s32[64]{0:T(128)S(1)} %get-tuple-element.43), channel_id=1, source_target_pairs={{0,4},{1,5},{2,6},{3,7},{4,0},{5,1},{6,2},{7,3},{8,12},{9,13},{10,... | collective-permute-start | bytes 776 | tf_op jit(solution)/shard_map/ppermute | solution.py:250
  27.1 1.2 collective-permute-start.2
  28.4 0.6 collective-permute-start.1
  29.0 0.9 collective-permute-start
  29.8 1.5 collective-permute-done.2
  31.3 1.0 collective-permute-done.1
  32.3 0.1 broadcast_in_dim.19
  32.4 0.1 broadcast_in_dim.20.ids_ref
  32.5 0.0 copy-start.5
  32.5 0.7 pick.1
  33.3 0.4 collective-permute-start.7
  33.7 1.2 collective-permute-start.8
  34.9 1.3 collective-permute-start.9
  36.2 1.0 collective-permute-start.10
  37.2 2.0 %collective-permute-start.11 = (bf16[128,256]{1,0:T(8,128)(2,1)S(1)}, bf16[128,256]{1,0:T(8,128)(2,1)S(1)}, u32[]{:S(2)}, u32[]{:S(2)}) collective-permute-start(bf16[128,256]{1,0:T(8,128)(2,1)S(1)} %get-tuple-element.32), channel_id=1, source_target_pairs={{0,3},{1,4},{2,5},{3,6},{4,7},{5,0},{6,1},{7,2},{8,11},{9,12},{10,... | collective-permute-start | bytes 196616 | tf_op jit(solution)/shard_map/ppermute | solution.py:250
  39.2 0.8 collective-permute-start.12
  40.0 0.4 collective-permute-start.13
  41.1 0.0 copy-start.2
  41.1 1.9 copy-done.2
  43.0 7.3 %prepare.1 = (bf16[2048,2560]{1,0:T(8,128)(2,1)}, f32[1024,128]{1,0:T(8,128)S(1)}) custom-call(s32[96]{0:T(128)S(1)} %bitcast.40, s32[96]{0:T(128)S(1)} %bitcast.41, s32[1]{0:T(128)} %bitcast.34.count_ref, s32[1,1024]{1,0:T(1,128)S(1)} %get-tuple-element.22.place_ref, bf16[96,128,128]{2,1,0:T(8,128)(2,1)S(1)} %bitcast.37), custom_call_target="tpu_custom_call" | custom-call | bytes 25165824 | tf_op jit(solution)/shard_map/prepare/pallas_call | solution.py:265
  50.3 19.3 %all-to-all-done = bf16[32,64,512]{2,1,0:T(8,128)(2,1)S(1)} async-done(((bf16[32,64,512]{2,1,0:T(8,128)(2,1)}), bf16[32,64,512]{2,1,0:T(8,128)(2,1)S(1)}, u32[]{:S(2)}, u32[]{:S(2)}) %all-to-all-start) | async-done | bytes 2097184 | tf_op jit(solution)/shard_map/all_to_all | solution.py:240
  69.6 1.3 copy-done
  70.9 18.9 %forward.1 = (bf16[2048,256]{1,0:T(8,128)(2,1)}, bf16[2048,256]{1,0:T(8,128)(2,1)S(1)}, bf16[2048,256]{1,0:T(8,128)(2,1)S(1)}, f32[2048,256]{1,0:T(8,128)S(1)}, f32[2048,256]{1,0:T(8,128)}) custom-call(s32[1]{0:T(128)} %bitcast.7.turn_ref, bf16[2048,512]{1,0:T(8,128)(2,1)} %bitcast.35, bf16[2048,2560]{1,0:T(8,128)(2,1)} %get-tuple-element.25.adj_ref, ...), custom_call_target="tpu_custom_call" | custom-call | flops 5905580032 | bytes 25165824 | tf_op jit(solution)/shard_map/forward/pallas_call | solution.py:282
  89.8 1.3 copy-done.3
  91.1 1.6 copy-done.1
  92.7 9.4 %backward.1 = f32[2,256,256]{2,1,0:T(8,128)S(1)} custom-call(bf16[2048,512]{1,0:T(8,128)(2,1)S(1)} %bitcast.36, bf16[2048,2560]{1,0:T(8,128)(2,1)} %get-tuple-element.25.adj_ref, bf16[2,256,256]{2,1,0:T(8,128)(2,1)S(1)} %copy-done.5, bf16[2048,256]{1,0:T(8,128)(2,1)S(1)} %get-tuple-element.36.m1_ref, bf16[2048,256]{1,0:T(8,128)(2,1)S(1)} %get-tuple-element.37.m2_ref, ...), custom_call_target="tpu_custom_call" | custom-call | flops 2952790016 | bytes 20971520 | tf_op jit(solution)/shard_map/backward/pallas_call | solution.py:298
  102.1 0.2 reshape.38
  102.3 31.2 %all_to_all.20 = f32[256,4,128]{2,1,0:T(4,128)S(1)} all-to-all(f32[256,4,128]{2,1,0:T(4,128)S(1)} %reshape.38), channel_id=1, replica_groups=mesh['wide'=32,'hist'=8] {'wide','hist'}, dimensions={0} | all-to-all | bytes 1048576 | tf_op jit(solution)/shard_map/all_to_all | solution.py:323
  133.5 3.9 %all-to-all-start.1 = ((bf16[32,64,256]{2,1,0:T(8,128)(2,1)}), bf16[32,64,256]{2,1,0:T(8,128)(2,1)S(1)}, u32[]{:S(2)}, u32[]{:S(2)}) async-start(bf16[32,64,256]{2,1,0:T(8,128)(2,1)} %bitcast.24), calls=%async_computation.1 | async-start | bytes 2097152 | tf_op jit(solution)/shard_map/all_to_all | solution.py:294
  137.5 0.3 reduce_sum.9
  137.7 24.3 %all-to-all-done.1 = bf16[32,64,256]{2,1,0:T(8,128)(2,1)S(1)} async-done(((bf16[32,64,256]{2,1,0:T(8,128)(2,1)}), bf16[32,64,256]{2,1,0:T(8,128)(2,1)S(1)}, u32[]{:S(2)}, u32[]{:S(2)}) %all-to-all-start.1) | async-done | bytes 1048608 | tf_op jit(solution)/shard_map/all_to_all | solution.py:294
  162.1 0.9 broadcast_in_dim.21
  162.9 11.4 %all-to-all-start.3 = ((f32[256,4,128]{2,1,0:T(4,128)}), f32[256,4,128]{2,1,0:T(4,128)S(1)}, u32[]{:S(2)}, u32[]{:S(2)}) async-start(f32[256,4,128]{2,1,0:T(4,128)} %broadcast_in_dim.21), calls=%async_computation.3 | async-start | bytes 1048576 | tf_op jit(solution)/shard_map/all_to_all | solution.py:327
  174.3 2.1 %collect.1 = bf16[1024,256]{1,0:T(8,128)(2,1)} custom-call(f32[1024,128]{1,0:T(8,128)S(1)} %get-tuple-element.23.column_ref, bf16[2048,256]{1,0:T(8,128)(2,1)S(1)} %bitcast.39), custom_call_target="tpu_custom_call" | custom-call | flops 1073741824 | bytes 2097152 | tf_op jit(solution)/shard_map/collect/pallas_call | solution.py:309
  176.4 18.4 %all-to-all-done.3 = f32[256,4,128]{2,1,0:T(4,128)S(1)} async-done(((f32[256,4,128]{2,1,0:T(4,128)}), f32[256,4,128]{2,1,0:T(4,128)S(1)}, u32[]{:S(2)}, u32[]{:S(2)}) %all-to-all-start.3) | async-done | bytes 524320 | tf_op jit(solution)/shard_map/all_to_all | solution.py:327
  194.8 1.1 reshape.39
  (31 shorter events, 0.1 us)
Async XLA Ops:
  0.6 1.0 copy-start.9
  1.7 1.0 copy-start.10
  2.7 0.7 copy-start.11
  7.1 1.4 copy-start.4
  8.5 12.2 %copy-start.12 = (s32[1,1,8,64]{3,2,1,0:T(8,128)S(1)}, s32[1,1,8,64]{3,2,1,0:T(8,128)}, u32[]{:S(2)}) copy-start(s32[1,1,8,64]{3,2,1,0:T(8,128)} %param.16) | copy-start | bytes 6148
  8.5 12.2 %copy-start.13 = (s32[1,1,8]{2,1,0:T(1,128)S(1)}, s32[1,1,8]{2,1,0:T(1,128)}, u32[]{:S(2)}) copy-start(s32[1,1,8]{2,1,0:T(1,128)} %param.17) | copy-start | bytes 100
  8.5 24.0 %copy-start.8 = (bf16[2,1024,256]{2,1,0:T(8,128)(2,1)S(1)}, bf16[2,1024,256]{2,1,0:T(8,128)(2,1)}, u32[]{:S(2)}) copy-start(bf16[2,1024,256]{2,1,0:T(8,128)(2,1)} %history_ref.1) | copy-start | bytes 3145732
  8.5 61.1 %all-to-all-start = ((bf16[32,64,512]{2,1,0:T(8,128)(2,1)}), bf16[32,64,512]{2,1,0:T(8,128)(2,1)S(1)}, u32[]{:S(2)}, u32[]{:S(2)}) async-start(bf16[32,64,512]{2,1,0:T(8,128)(2,1)} %bitcast.38), calls=%async_computation | async-start | bytes 4194304 | tf_op jit(solution)/shard_map/all_to_all | solution.py:240
  20.7 20.4 %copy-start.6 = (s32[1,1,96]{2,1,0:T(1,128)S(1)}, s32[1,1,96]{2,1,0:T(1,128)}, u32[]{:S(2)}) copy-start(s32[1,1,96]{2,1,0:T(1,128)} %param.18) | copy-start | bytes 1156
  20.7 20.4 %copy-start.7 = (s32[1,1,96]{2,1,0:T(1,128)S(1)}, s32[1,1,96]{2,1,0:T(1,128)}, u32[]{:S(2)}) copy-start(s32[1,1,96]{2,1,0:T(1,128)} %param.19) | copy-start | bytes 1156
  20.8 7.5 %collective-permute-start.6 = (s32[64]{0:T(128)S(1)}, s32[64]{0:T(128)S(1)}, u32[]{:S(2)}, u32[]{:S(2)}) collective-permute-start(s32[64]{0:T(128)S(1)} %get-tuple-element.40), channel_id=1, source_target_pairs={{0,7},{1,0},{2,1},{3,2},{4,3},{5,4},{6,5},{7,6},{8,15},{9,8},{10,9... | collective-permute-start | bytes 776 | tf_op jit(solution)/shard_map/ppermute | solution.py:250
  21.8 7.2 %collective-permute-start.5 = (s32[64]{0:T(128)S(1)}, s32[64]{0:T(128)S(1)}, u32[]{:S(2)}, u32[]{:S(2)}) collective-permute-start(s32[64]{0:T(128)S(1)} %get-tuple-element.41), channel_id=1, source_target_pairs={{0,6},{1,7},{2,0},{3,1},{4,2},{5,3},{6,4},{7,5},{8,14},{9,15},{10,... | collective-permute-start | bytes 776 | tf_op jit(solution)/shard_map/ppermute | solution.py:250
  24.3 5.5 %collective-permute-start.4 = (s32[64]{0:T(128)S(1)}, s32[64]{0:T(128)S(1)}, u32[]{:S(2)}, u32[]{:S(2)}) collective-permute-start(s32[64]{0:T(128)S(1)} %get-tuple-element.42), channel_id=1, source_target_pairs={{0,5},{1,6},{2,7},{3,0},{4,1},{5,2},{6,3},{7,4},{8,13},{9,14},{10,... | collective-permute-start | bytes 776 | tf_op jit(solution)/shard_map/ppermute | solution.py:250
  25.1 4.7 %collective-permute-start.3 = (s32[64]{0:T(128)S(1)}, s32[64]{0:T(128)S(1)}, u32[]{:S(2)}, u32[]{:S(2)}) collective-permute-start(s32[64]{0:T(128)S(1)} %get-tuple-element.43), channel_id=1, source_target_pairs={{0,4},{1,5},{2,6},{3,7},{4,0},{5,1},{6,2},{7,3},{8,12},{9,13},{10,... | collective-permute-start | bytes 776 | tf_op jit(solution)/shard_map/ppermute | solution.py:250
  27.1 4.2 %collective-permute-start.2 = (s32[64]{0:T(128)S(1)}, s32[64]{0:T(128)S(1)}, u32[]{:S(2)}, u32[]{:S(2)}) collective-permute-start(s32[64]{0:T(128)S(1)} %get-tuple-element.44), channel_id=1, source_target_pairs={{0,3},{1,4},{2,5},{3,6},{4,7},{5,0},{6,1},{7,2},{8,11},{9,12},{10,... | collective-permute-start | bytes 776 | tf_op jit(solution)/shard_map/ppermute | solution.py:250
  28.4 3.9 %collective-permute-start.1 = (s32[64]{0:T(128)S(1)}, s32[64]{0:T(128)S(1)}, u32[]{:S(2)}, u32[]{:S(2)}) collective-permute-start(s32[64]{0:T(128)S(1)} %get-tuple-element.45), channel_id=1, source_target_pairs={{0,2},{1,3},{2,4},{3,5},{4,6},{5,7},{6,0},{7,1},{8,10},{9,11},{10,... | collective-permute-start | bytes 776 | tf_op jit(solution)/shard_map/ppermute | solution.py:250
  29.0 3.3 %collective-permute-start = (s32[64]{0:T(128)S(1)}, s32[64]{0:T(128)S(1)}, u32[]{:S(2)}, u32[]{:S(2)}) collective-permute-start(s32[64]{0:T(128)S(1)} %get-tuple-element.46), channel_id=1, source_target_pairs={{0,1},{1,2},{2,3},{3,4},{4,5},{5,6},{6,7},{7,0},{8,9},{9,10},{10,1... | collective-permute-start | bytes 776 | tf_op jit(solution)/shard_map/ppermute | solution.py:250
  32.5 38.4 %copy-start.5 = (bf16[2,256,256]{2,1,0:T(8,128)(2,1)S(1)}, bf16[2,256,256]{2,1,0:T(8,128)(2,1)}, u32[]{:S(2)}) copy-start(bf16[2,256,256]{2,1,0:T(8,128)(2,1)} %w_ref.3) | copy-start | bytes 786436
  33.3 6.0 %collective-permute-start.7 = (bf16[128,256]{1,0:T(8,128)(2,1)S(1)}, bf16[128,256]{1,0:T(8,128)(2,1)S(1)}, u32[]{:S(2)}, u32[]{:S(2)}) collective-permute-start(bf16[128,256]{1,0:T(8,128)(2,1)S(1)} %get-tuple-element.28), channel_id=1, source_target_pairs={{0,7},{1,0},{2,1},{3,2},{4,3},{5,4},{6,5},{7,6},{8,15},{9,8},{10,9... | collective-permute-start | bytes 196616 | tf_op jit(solution)/shard_map/ppermute | solution.py:250
  33.7 6.4 %collective-permute-start.8 = (bf16[128,256]{1,0:T(8,128)(2,1)S(1)}, bf16[128,256]{1,0:T(8,128)(2,1)S(1)}, u32[]{:S(2)}, u32[]{:S(2)}) collective-permute-start(bf16[128,256]{1,0:T(8,128)(2,1)S(1)} %get-tuple-element.29), channel_id=1, source_target_pairs={{0,6},{1,7},{2,0},{3,1},{4,2},{5,3},{6,4},{7,5},{8,14},{9,15},{10,... | collective-permute-start | bytes 196616 | tf_op jit(solution)/shard_map/ppermute | solution.py:250
  34.9 15.4 %collective-permute-start.9 = (bf16[128,256]{1,0:T(8,128)(2,1)S(1)}, bf16[128,256]{1,0:T(8,128)(2,1)S(1)}, u32[]{:S(2)}, u32[]{:S(2)}) collective-permute-start(bf16[128,256]{1,0:T(8,128)(2,1)S(1)} %get-tuple-element.30), channel_id=1, source_target_pairs={{0,5},{1,6},{2,7},{3,0},{4,1},{5,2},{6,3},{7,4},{8,13},{9,14},{10,... | collective-permute-start | bytes 196616 | tf_op jit(solution)/shard_map/ppermute | solution.py:250
  36.2 14.1 %collective-permute-start.10 = (bf16[128,256]{1,0:T(8,128)(2,1)S(1)}, bf16[128,256]{1,0:T(8,128)(2,1)S(1)}, u32[]{:S(2)}, u32[]{:S(2)}) collective-permute-start(bf16[128,256]{1,0:T(8,128)(2,1)S(1)} %get-tuple-element.31), channel_id=1, source_target_pairs={{0,4},{1,5},{2,6},{3,7},{4,0},{5,1},{6,2},{7,3},{8,12},{9,13},{10,... | collective-permute-start | bytes 196616 | tf_op jit(solution)/shard_map/ppermute | solution.py:250
  37.2 13.1 %collective-permute-start.11 = (bf16[128,256]{1,0:T(8,128)(2,1)S(1)}, bf16[128,256]{1,0:T(8,128)(2,1)S(1)}, u32[]{:S(2)}, u32[]{:S(2)}) collective-permute-start(bf16[128,256]{1,0:T(8,128)(2,1)S(1)} %get-tuple-element.32), channel_id=1, source_target_pairs={{0,3},{1,4},{2,5},{3,6},{4,7},{5,0},{6,1},{7,2},{8,11},{9,12},{10,... | collective-permute-start | bytes 196616 | tf_op jit(solution)/shard_map/ppermute | solution.py:250
  39.2 11.1 %collective-permute-start.12 = (bf16[128,256]{1,0:T(8,128)(2,1)S(1)}, bf16[128,256]{1,0:T(8,128)(2,1)S(1)}, u32[]{:S(2)}, u32[]{:S(2)}) collective-permute-start(bf16[128,256]{1,0:T(8,128)(2,1)S(1)} %get-tuple-element.33), channel_id=1, source_target_pairs={{0,2},{1,3},{2,4},{3,5},{4,6},{5,7},{6,0},{7,1},{8,10},{9,11},{10,... | collective-permute-start | bytes 196616 | tf_op jit(solution)/shard_map/ppermute | solution.py:250
  40.0 10.2 %collective-permute-start.13 = (bf16[128,256]{1,0:T(8,128)(2,1)S(1)}, bf16[128,256]{1,0:T(8,128)(2,1)S(1)}, u32[]{:S(2)}, u32[]{:S(2)}) collective-permute-start(bf16[128,256]{1,0:T(8,128)(2,1)S(1)} %get-tuple-element.34), channel_id=1, source_target_pairs={{0,1},{1,2},{2,3},{3,4},{4,5},{5,6},{6,7},{7,0},{8,9},{9,10},{10,1... | collective-permute-start | bytes 196616 | tf_op jit(solution)/shard_map/ppermute | solution.py:250
  41.1 1.9 copy-start.2
  69.6 1.3 copy-start
  89.8 1.3 copy-start.3
  91.1 1.6 copy-start.1
  133.5 28.6 %all-to-all-start.1 = ((bf16[32,64,256]{2,1,0:T(8,128)(2,1)}), bf16[32,64,256]{2,1,0:T(8,128)(2,1)S(1)}, u32[]{:S(2)}, u32[]{:S(2)}) async-start(bf16[32,64,256]{2,1,0:T(8,128)(2,1)} %bitcast.24), calls=%async_computation.1 | async-start | bytes 2097152 | tf_op jit(solution)/shard_map/all_to_all | solution.py:294
  162.9 31.9 %all-to-all-start.3 = ((f32[256,4,128]{2,1,0:T(4,128)}), f32[256,4,128]{2,1,0:T(4,128)S(1)}, u32[]{:S(2)}, u32[]{:S(2)}) async-start(f32[256,4,128]{2,1,0:T(4,128)} %broadcast_in_dim.21), calls=%async_computation.3 | async-start | bytes 1048576 | tf_op jit(solution)/shard_map/all_to_all | solution.py:327

commit v2 on v1

v2 whole, which is shorter than its diff:
```python
import math

import jax
import jax.numpy as jnp
from jax import lax
from jax.experimental import pallas as pl
from jax.experimental.pallas import tpu as pltpu
from jax.sharding import Mesh
from jax.sharding import PartitionSpec as P

ALPHA = 0.1
BETAS = (math.log(1.5), math.log(1.25))
TILE = 128
CAP = 64
HCAP = 64
MARK = 1024.0
LIMIT = 512.0
BF16 = jnp.bfloat16
F32 = jnp.float32
MIB = 1 << 20
WIDE = ("y", "z")
HIST = ("x", "core")


def vmem(count):
    return [pl.BlockSpec(memory_space=pltpu.VMEM)] * count


def smem(count):
    return [pl.BlockSpec(memory_space=pltpu.SMEM)] * count


def params(limit):
    return pltpu.CompilerParams(vmem_limit_bytes=limit * MIB)


def cost(flops, moved):
    return pl.CostEstimate(flops=flops, bytes_accessed=moved, transcendentals=0)


def dot(a, b):
    return jnp.dot(a, b, preferred_element_type=F32)


def dot_rows(a, b):
    return lax.dot_general(a, b, (((0,), (0,)), ((), ())), preferred_element_type=F32)


def hits_of(place, start, step):
    slots = lax.broadcasted_iota(jnp.int32, (step, place.shape[1]), 0) + start
    return (slots == place).astype(F32)


def route_body(n_wide, own_ref, x_hbm, send_hbm, place_ref, x_all, send, load_sem, send_sem):
    load = pltpu.make_async_copy(x_hbm, x_all, load_sem)
    load.start()
    rows_here = own_ref.shape[1]
    blocks = rows_here // 128
    own = own_ref[...]
    ids = lax.broadcasted_iota(jnp.int32, (n_wide, 128), 0)
    hot = [(own[:, 128 * b : 128 * (b + 1)] == ids).astype(F32) for b in range(blocks)]
    lower = lax.broadcasted_iota(jnp.int32, (128, 128), 0)
    upper = lax.broadcasted_iota(jnp.int32, (128, 128), 1)
    earlier = (lower < upper).astype(F32).astype(BF16)
    inside = dot(jnp.concatenate(hot, axis=0).astype(BF16), earlier)
    before = jnp.zeros((n_wide, 1), F32)
    ranks = []
    for b in range(blocks):
        seen = inside[n_wide * b : n_wide * (b + 1)] + before
        ranks.append(jnp.sum(seen * hot[b], axis=0, keepdims=True))
        before = before + jnp.sum(hot[b], axis=1, keepdims=True)
    place = own * CAP + jnp.concatenate(ranks, axis=1).astype(jnp.int32)
    place_ref[...] = place
    load.wait()
    step = 256
    stores = []
    for c in range(send.shape[0] // step):
        part = pl.ds(c * step, step)
        hit = hits_of(place, c * step, step)
        held = jnp.max(hit, axis=1, keepdims=True)
        send[part, :] = jnp.where(held > 0.5, dot(hit.astype(BF16), x_all[...]), MARK).astype(BF16)
        store = pltpu.make_async_copy(send.at[part], send_hbm.at[part], send_sem.at[c])
        store.start()
        stores.append(store)
    for store in stores:
        store.wait()


def follow_body(place_ref, value_ref, send_ref):
    place = place_ref[...]
    step = 256
    for c in range(send_ref.shape[0] // step):
        hit = hits_of(place, c * step, step).astype(BF16)
        send_ref[pl.ds(c * step, step), :] = dot(hit, value_ref[...]).astype(BF16)


def prepare_body(rows_ref, cols_ref, count_ref, place_ref, vals_ref, adj_ref, column_ref, head, following):
    adj_ref[...] = jnp.zeros_like(adj_ref)
    count = count_ref[0]
    wide = adj_ref.shape[1] // TILE

    def clear(k, carry):
        head[rows_ref[k] * wide + cols_ref[k]] = -1
        return carry

    lax.fori_loop(0, count, clear, 0)

    def chain(i, carry):
        k = count - 1 - i
        cell = rows_ref[k] * wide + cols_ref[k]
        following[k] = head[cell]
        head[cell] = k
        return carry

    lax.fori_loop(0, count, chain, 0)

    def fill(k, carry):
        row, col = rows_ref[k], cols_ref[k]

        @pl.when(head[row * wide + col] == k)
        def _():
            def more(state):
                at, total = state
                return following[at], total + vals_ref[at].astype(F32)

            _, total = lax.while_loop(
                lambda state: state[0] >= 0, more, (following[k], vals_ref[k].astype(F32))
            )
            adj_ref[
                pl.ds(pl.multiple_of(row * TILE, TILE), TILE),
                pl.ds(pl.multiple_of(col * TILE, TILE), TILE),
            ] = total.astype(BF16)

        return carry

    lax.fori_loop(0, count, fill, 0)
    for b in range(place_ref.shape[1] // 128):
        part = place_ref[:, 128 * b : 128 * (b + 1)].astype(F32)
        column_ref[pl.ds(128 * b, 128), :] = jnp.transpose(jnp.broadcast_to(part, (128, 128)))


def pick_body(ids_ref, history_ref, own_ref, other_ref):
    slots = ids_ref.shape[0]
    here = history_ref.shape[1]
    lane = lax.broadcasted_iota(jnp.int32, (slots, 128), 1)
    ids = ids_ref[...]
    hit = jnp.concatenate(
        [(ids - 128 * c == lane).astype(F32).astype(BF16) for c in range(here // 128)], axis=1
    )
    size = own_ref.shape[0]
    for layer in range(2):
        rows = dot(hit, history_ref[layer]).astype(BF16)
        for side, ref in enumerate((own_ref, other_ref)):
            for k in range(size):
                at = (side * size + k) * HCAP
                ref[k, pl.ds(layer * HCAP, HCAP), :] = rows[at : at + HCAP]


def forward_body(size, turn_ref, ws_hbm, w_hbm, adj_hbm, *rest):
    pieces = rest[:size]
    out_hbm, m_hbm, s_hbm, adj, w, ws, ext0, ext1, m_all, s_all, out, acc0, acc1, load_sem, keep_sem = rest[size:]
    work, width = ws.shape
    step = acc0.shape[0]
    blocks = work // step
    rows = [pl.ds(b * step, step) for b in range(blocks)]
    first = [
        pltpu.make_async_copy(ws_hbm, ws, load_sem.at[0]),
        pltpu.make_async_copy(w_hbm, w, load_sem.at[1]),
    ]
    x, core = turn_ref[0], turn_ref[1]
    for layer, ext in enumerate((ext0, ext1)):
        for k, piece in enumerate(pieces):
            for side in range(2):
                shard = lax.rem(x + k, size) * 2 + lax.rem(core + side, 2)
                there = pl.ds(pl.multiple_of(work + shard * HCAP, HCAP), HCAP)
                here = pl.ds((2 * side + layer) * HCAP, HCAP)
                sem = load_sem.at[2 + (layer * size + k) * 2 + side]
                first.append(pltpu.make_async_copy(piece.at[here], ext.at[there], sem))
    for load in first:
        load.start()
    loads = {}
    for b, until in ((0, 1), (1, blocks // 2), (blocks // 2, blocks)):
        part = pl.ds(b * step, (until - b) * step)
        sem = load_sem.at[2 + 4 * size + len(loads)]
        loads[b] = pltpu.make_async_copy(adj_hbm.at[part], adj.at[part], sem)
        loads[b].start()
    for load in first:
        load.wait()
    for part in rows:
        got = ws[part, :].astype(F32)
        ext0[part, :] = jnp.where(got < LIMIT, got, 0.0).astype(BF16)
    stores = []

    def finish(layer, b, support):
        part = rows[b]
        beta = BETAS[layer]
        mixed = (1.0 - ALPHA) * support + ALPHA * ext0[part, :].astype(F32)
        mixed_b = mixed.astype(BF16)
        m_all[layer, part, :] = mixed_b
        pre = (1.0 - beta) * mixed + beta * dot(mixed_b, w[layer])
        sig = jax.nn.sigmoid(pre)
        keep = ws[part, :].astype(F32) < LIMIT
        raw = pre * sig
        new = jnp.where(keep, raw, 0.0).astype(BF16)
        s_all[layer, part, :] = jnp.where(keep, sig + raw * (1.0 - sig), 0.0)
        (ext1, out)[layer][part, :] = new
        moves = [(m_all.at[layer, part], m_hbm.at[layer, part]), (s_all.at[layer, part], s_hbm.at[layer, part])]
        if layer == 1:
            moves.insert(0, (out.at[part], out_hbm.at[part]))
        for kind, (here, there) in enumerate(moves):
            store = pltpu.make_async_copy(here, there, keep_sem.at[layer, kind, b])
            store.start()
            stores.append(store)

    accs = (acc0, acc1)
    for layer, ext in enumerate((ext0, ext1)):
        for b in range(blocks + 1):
            if b < blocks:
                if layer == 0 and b in loads:
                    loads[b].wait()
                accs[b % 2][...] = dot(adj[rows[b], :], ext[...])
            if b > 0:
                finish(layer, b - 1, accs[(b - 1) % 2][...])
    for store in stores:
        store.wait()


def backward_body(cot_ref, w_ref, adj_hbm, m_hbm, s_hbm, grads_ref, adj, m_all, s_all, turned, load_sem):
    work = m_all.shape[1]
    width = m_all.shape[2]
    step = 512
    blocks = work // step
    parts = [pl.ds(b * step, step) for b in range(blocks)]
    copies = [
        pltpu.make_async_copy(s_hbm.at[1], s_all.at[1], load_sem.at[0]),
        pltpu.make_async_copy(m_hbm.at[1], m_all.at[1], load_sem.at[1]),
    ]
    loads = [
        pltpu.make_async_copy(adj_hbm.at[:, part], adj.at[:, part], load_sem.at[4 + b])
        for b, part in enumerate(parts)
    ]
    late = [
        pltpu.make_async_copy(s_hbm.at[0], s_all.at[0], load_sem.at[2]),
        pltpu.make_async_copy(m_hbm.at[0], m_all.at[0], load_sem.at[3]),
    ]
    for copy in copies + loads[:1] + late + loads[1:]:
        copy.start()
    for copy in copies:
        copy.wait()
    beta = BETAS[1]
    total = jnp.zeros((width, width), F32)
    for part in parts:
        grad_two = cot_ref[part, :].astype(F32) * s_all[1, part, :]
        grad_two_b = grad_two.astype(BF16)
        total = total + dot_rows(m_all[1, part, :], grad_two_b)
        through = lax.dot_general(
            grad_two_b, w_ref[1], (((1,), (1,)), ((), ())), preferred_element_type=F32
        )
        grad_mix = (1.0 - beta) * grad_two + beta * through
        turned[:, part] = jnp.transpose(grad_mix.astype(BF16))
    grads_ref[1] = BETAS[1] * total
    for copy in late:
        copy.wait()
    total = jnp.zeros((width, width), F32)
    for b, part in enumerate(parts):
        loads[b].wait()
        back = jnp.transpose(dot(turned[...], adj[:, part]))
        grad_one = (1.0 - ALPHA) * back * s_all[0, part, :]
        total = total + dot_rows(m_all[0, part, :], grad_one.astype(BF16))
    grads_ref[0] = BETAS[0] * total


def collect_body(column_ref, back_ref, out_ref):
    slots = back_ref.shape[0]
    step = 256
    lane = lax.broadcasted_iota(jnp.int32, (step, 128), 1).astype(F32)
    for b in range(out_ref.shape[0] // step):
        part = pl.ds(b * step, step)
        place = column_ref[part, :]
        hit = jnp.concatenate(
            [(place - 128.0 * c == lane).astype(F32).astype(BF16) for c in range(slots // 128)],
            axis=1,
        )
        out_ref[part, :] = dot(hit, back_ref[...]).astype(BF16)


def local(
    x_home,
    cotangent,
    owner,
    weights,
    history,
    halo_ids,
    halo_count,
    tile_rows,
    tile_cols,
    tile_count,
    tile_vals,
):
    n_wide = lax.axis_size(WIDE)
    n_hist = lax.axis_size(HIST)
    rows_here, width = x_home.shape
    work = n_wide * CAP
    halo = n_hist * HCAP
    slots = tile_vals.shape[2]

    anywhere = pl.BlockSpec(memory_space=pl.ANY)
    x = lax.axis_index("x")
    core = lax.axis_index("core")
    size = lax.axis_size("x")

    def to_owners(value):
        value = value.reshape(n_wide, CAP, width)
        return lax.all_to_all(value, WIDE, split_axis=0, concat_axis=0, tiled=True).reshape(
            work, width
        )

    send, place = pl.pallas_call(
        lambda *refs: route_body(n_wide, *refs),
        out_shape=(
            pltpu.HBM((work, width), BF16),
            jax.ShapeDtypeStruct((1, rows_here), jnp.int32),
        ),
        in_specs=vmem(1) + [anywhere],
        out_specs=(anywhere, vmem(1)[0]),
        scratch_shapes=[
            pltpu.VMEM((rows_here, width), BF16),
            pltpu.VMEM((work, width), BF16),
            pltpu.SemaphoreType.DMA,
            pltpu.SemaphoreType.DMA((work // 256,)),
        ],
        compiler_params=params(56),
        cost_estimate=cost(2 * work * rows_here * width, 2 * MIB),
        name="route",
    )(owner.reshape(1, rows_here), x_home)
    ws = to_owners(send)

    send_cot = pl.pallas_call(
        follow_body,
        out_shape=jax.ShapeDtypeStruct((work, width), BF16),
        in_specs=vmem(2),
        out_specs=vmem(1)[0],
        compiler_params=params(16),
        cost_estimate=cost(2 * work * rows_here * width, 2 * MIB),
        name="follow",
    )(place, cotangent)
    adjacency, column = pl.pallas_call(
        prepare_body,
        out_shape=(
            pltpu.HBM((work, work + halo), BF16),
            jax.ShapeDtypeStruct((rows_here, 128), F32),
        ),
        in_specs=smem(3) + vmem(2),
        out_specs=tuple(vmem(2)),
        scratch_shapes=[
            pltpu.SMEM(((work // TILE) * ((work + halo) // TILE),), jnp.int32),
            pltpu.SMEM((slots,), jnp.int32),
        ],
        compiler_params=params(24),
        cost_estimate=cost(0, 24 * MIB),
        name="prepare",
    )(tile_rows[0, 0], tile_cols[0, 0], tile_count[0], place, tile_vals[0, 0])

    live = jnp.arange(HCAP)[None, :] < halo_count[0, 0][:, None]
    wanted = jnp.where(live, halo_ids[0, 0], -1)
    wanted, place = lax.optimization_barrier((wanted, place))
    wanted = wanted.reshape(size, 2, HCAP)
    wanted = lax.dynamic_slice_in_dim(jnp.concatenate([wanted, wanted]), x, size, axis=0)

    def shift(value, by):
        return lax.ppermute(value, "x", [(i, (i + by) % size) for i in range(size)])

    asked = jnp.stack([wanted[0]] + [shift(wanted[k], k) for k in range(1, size)])
    asked_own = jnp.where(core == 0, asked[:, 0], asked[:, 1])
    asked_other = swap_cores(jnp.where(core == 0, asked[:, 1], asked[:, 0]))
    asked = jnp.stack([asked_own, asked_other]).reshape(halo, 1)
    own, other = pl.pallas_call(
        pick_body,
        out_shape=(jax.ShapeDtypeStruct((size, 2 * HCAP, width), BF16),) * 2,
        in_specs=vmem(2),
        out_specs=tuple(vmem(2)),
        compiler_params=params(12),
        cost_estimate=cost(4 * halo * history.shape[1] * width, 2 * MIB),
        name="pick",
    )(jnp.broadcast_to(asked, (halo, 128)), history)
    send_cot, ws, adjacency, own, other = lax.optimization_barrier(
        (send_cot, ws, adjacency, own, other)
    )
    ws_cot = to_owners(send_cot)

    other = swap_cores(other)
    pieces = [jnp.concatenate([own[k], other[k]]) for k in range(size)]
    pieces = pieces[:1] + [shift(pieces[k], size - k) for k in range(1, size)]

    step = 256
    second, mixed, slopes = pl.pallas_call(
        lambda *refs: forward_body(size, *refs),
        out_shape=(
            pltpu.HBM((work, width), BF16),
            pltpu.HBM((2, work, width), BF16),
            pltpu.HBM((2, work, width), F32),
        ),
        in_specs=smem(1) + [anywhere] * (3 + size),
        out_specs=(anywhere,) * 3,
        scratch_shapes=[
            pltpu.VMEM((work, work + halo), BF16),
            pltpu.VMEM((2, width, width), BF16),
            pltpu.VMEM((work, width), BF16),
            pltpu.VMEM((work + halo, width), BF16),
            pltpu.VMEM((work + halo, width), BF16),
            pltpu.VMEM((2, work, width), BF16),
            pltpu.VMEM((2, work, width), F32),
            pltpu.VMEM((work, width), BF16),
            pltpu.VMEM((step, width), F32),
            pltpu.VMEM((step, width), F32),
            pltpu.SemaphoreType.DMA((5 + 4 * size,)),
            pltpu.SemaphoreType.DMA((2, 3, work // step)),
        ],
        compiler_params=params(56),
        cost_estimate=cost(4 * work * (work + halo + width) * width, 24 * MIB),
        name="forward",
    )(jnp.stack([x, core]).astype(jnp.int32), ws, weights, adjacency, *pieces)
    second, ws_cot = lax.optimization_barrier((second, ws_cot))
    returned = to_owners(second)

    grads = pl.pallas_call(
        backward_body,
        out_shape=jax.ShapeDtypeStruct((2, width, width), F32),
        in_specs=vmem(2) + [anywhere] * 3,
        out_specs=vmem(1)[0],
        scratch_shapes=[
            pltpu.VMEM((work, work), BF16),
            pltpu.VMEM((2, work, width), BF16),
            pltpu.VMEM((2, work, width), F32),
            pltpu.VMEM((width, work), BF16),
            pltpu.SemaphoreType.DMA((8,)),
        ],
        compiler_params=params(56),
        cost_estimate=cost(2 * work * (work + 3 * width) * width, 20 * MIB),
        name="backward",
    )(ws_cot, weights, adjacency, mixed, slopes)

    grads, returned = reduce_rows(grads), returned
    grads, returned = lax.optimization_barrier((grads, returned))
    second_out = pl.pallas_call(
        collect_body,
        out_shape=jax.ShapeDtypeStruct((rows_here, width), BF16),
        in_specs=vmem(2),
        out_specs=vmem(1)[0],
        compiler_params=params(24),
        cost_estimate=cost(2 * work * rows_here * width, 2 * MIB),
        name="collect",
    )(column, returned)
    mine = sum_wide(grads, n_wide)
    mine, second_out = lax.optimization_barrier((mine, second_out))
    return (second_out, spread(mine))


def swap_cores(value):
    return lax.ppermute(value, "core", [(0, 1), (1, 0)])


def reduce_rows(grads):
    core = lax.axis_index("core")
    kept = jnp.where(core == 0, grads[0], grads[1])
    given = jnp.where(core == 0, grads[1], grads[0])
    kept = kept + swap_cores(given)
    size = lax.axis_size("x")
    quarter = kept.shape[0] // size
    x = lax.axis_index("x")

    def rows_of(index):
        return lax.dynamic_slice_in_dim(kept, lax.rem(index, size) * quarter, quarter, axis=0)

    total = rows_of(x)
    for k in range(1, size):
        total = total + lax.ppermute(
            rows_of(x + k), "x", [(i, (i + k) % size) for i in range(size)]
        )
    return total


def sum_wide(part, n_wide):
    rows, width = part.shape
    some = rows // n_wide
    parts = lax.all_to_all(
        part.reshape(n_wide, some, width), WIDE, split_axis=0, concat_axis=0, tiled=True
    )
    return jnp.sum(parts, axis=0, keepdims=True)


def spread(mine):
    _, some, width = mine.shape
    every = ("x",) + WIDE
    n_every = lax.axis_size(every)
    own = lax.all_to_all(
        jnp.broadcast_to(mine, (n_every, some, width)),
        every,
        split_axis=0,
        concat_axis=0,
        tiled=True,
    ).reshape(n_every * some, width)
    other = swap_cores(own)
    core = lax.axis_index("core")
    return jnp.stack([jnp.where(core == 0, own, other), jnp.where(core == 0, other, own)])


def solution(mesh):
    sizes = (4, mesh.shape["wide"] // 4, mesh.shape["hist"] // 2, 2)
    split = Mesh(mesh.devices.reshape(sizes), WIDE + HIST)
    rows = P(WIDE + HIST, None)
    placed = (
        rows,
        rows,
        rows,
        P(),
        P(None, HIST, None),
        P(WIDE, HIST, None, None),
        P(WIDE, HIST, None),
        P(WIDE, HIST, None),
        P(WIDE, HIST, None),
        P(WIDE, HIST),
        P(WIDE, HIST, None, None, None),
    )
    return jax.shard_map(
        local,
        mesh=split,
        in_specs=placed,
        out_specs=(rows, P()),
        check_vma=False,
    )
```

time: 196 us -> 155 us (0.79)
  waiting for transfers between devices: 64.5 us -> 21.4 us
  starting transfers between devices: 43.6 us -> 61 us
  blocking collectives: 31.2 us -> 18.9 us
  local copies, waits for them, and re-layouts: 12.7 us -> 7.26 us
  other arithmetic: 0.36 us -> 4.47 us
  Pallas kernels: 42.1 us -> 39.9 us
    all_to_all x3 -> x4, waiting for transfers between devices: 62.1 us -> 9.39 us  [the longest x1 6.87 us: sum_wide(): lax.all_to_all(part.reshape(n_wide, some, width), WIDE, split_axis=0, con...]
    all_to_all x1, blocking collectives: 31.2 us -> 18.9 us  [spread(): lax.all_to_all(jnp.broadcast_to(mine, (n_every, some, width)), every, spl...]
    all_to_all x3 -> x4, starting transfers between devices: 27.5 us -> 38.8 us  [the longest x3 30.3 us: to_owners(): lax.all_to_all(value, WIDE, split_axis=0, concat_axis=0, tiled=True)]
    ppermute x14 -> x13, waiting for transfers between devices: 2.47 us -> 12 us  [the longest x3 4.49 us: reduce_rows(): lax.ppermute(rows_of(x + k), 'x', [(i, (i + k) % size) for i in range(siz...]
    ppermute x14 -> x13, starting transfers between devices: 16.1 us -> 22.3 us  [the longest x6 10.1 us: shift(): return lax.ppermute(value, 'x', [(i, (i + by) % size) for i in range(size)])]
    unnamed x28 -> x32, local copies, waits for them, and re-layouts: 10.2 us -> 6.07 us
    pallas_call x4 -> x5, Pallas kernels: 30.6 us -> 28.3 us  [the longest x1 12.4 us: local(): pl.pallas_call(lambda *refs: forward_body(size, *refs), out_shape=(pltpu....]
  transfers between devices with their start and end apart: 17 -> 17, of which waited for: 5 -> 11; matrix products, arithmetic and copies ran while one was open for 0% -> 2% of each run, Pallas kernels for 5% -> 23%
where the time goes in v2:
time: 155 us
  starting transfers between devices  61 us (39%)
  Pallas kernels  39.9 us (26%)
  waiting for transfers between devices  21.4 us (14%)
  blocking collectives  18.9 us (12%)
  local copies, waits for them, and re-layouts  7.26 us (5%)
  other arithmetic  4.47 us (3%)
  between operations  1.63 us (1%)
    all_to_all x3, starting transfers between devices, to_owners(): lax.all_to_all(value, WIDE, split_axis=0, concat_axis=0, tiled=True)  30.3 us
    all_to_all x1, blocking collectives, spread(): lax.all_to_all(jnp.broadcast_to(mine, (n_every, some, width)), every, spl...  18.9 us
    pallas_call x1, Pallas kernels, local(): pl.pallas_call(lambda *refs: forward_body(size, *refs), out_shape=(pltpu....  12.4 us
    ppermute x6, starting transfers between devices, shift(): return lax.ppermute(value, 'x', [(i, (i + by) % size) for i in range(size)])  10.1 us
    pallas_call x1, Pallas kernels, local(): pl.pallas_call(backward_body, out_shape=jax.ShapeDtypeStruct((2, width, w...  9.57 us
    pallas_call x1, Pallas kernels, local(): pl.pallas_call(prepare_body, out_shape=(pltpu.HBM((work, work + halo), BF...  8.91 us
    ppermute x4, starting transfers between devices, swap_cores(): return lax.ppermute(value, 'core', [(0, 1), (1, 0)])  8.53 us
    all_to_all x1, starting transfers between devices, sum_wide(): lax.all_to_all(part.reshape(n_wide, some, width), WIDE, split_axis=0, con...  8.49 us
  transfers between devices with their start and end apart: 17, of which 11 were waited for; matrix products, arithmetic and copies ran while one was open for 2% of the time, Pallas kernels for 23%

profile of v2, /device:TPU:1, one launch (start us, length us, event | category | flops | bytes accessed | tf_op | source)
XLA Modules:
  0.0 154.6 jit_solution(16424660072352768019)
XLA Ops:
  0.7 5.1 %route.1 = (bf16[2048,256]{1,0:T(8,128)(2,1)}, s32[1,1024]{1,0:T(1,128)}) custom-call(s32[1,1024]{1,0:T(1,128)} %bitcast.78, bf16[1024,256]{1,0:T(8,128)(2,1)} %refs_1_.1), custom_call_target="tpu_custom_call" | custom-call | flops 1073741824 | bytes 2097152 | tf_op jit(solution)/shard_map/route/pallas_call | solution.py:318
  5.8 12.2 %all-to-all-start = ((bf16[32,64,256]{2,1,0:T(8,128)(2,1)}), bf16[32,64,256]{2,1,0:T(8,128)(2,1)}, u32[]{:S(2)}, u32[]{:S(2)}) async-start(bf16[32,64,256]{2,1,0:T(8,128)(2,1)} %bitcast.68), calls=%async_computation | async-start | bytes 2097152 | tf_op jit(solution)/shard_map/all_to_all | solution.py:314
  18.1 1.3 collective-permute-start
  19.4 2.4 %collective-permute-start.1 = (s32[2,64]{1,0:T(2,128)S(1)}, s32[2,64]{1,0:T(2,128)S(1)}, u32[]{:S(2)}, u32[]{:S(2)}) collective-permute-start(s32[2,64]{1,0:T(2,128)S(1)} %get-tuple-element.61), channel_id=1, source_target_pairs={{0,4},{2,6},{4,0},{6,2},{1,5},{3,7},{5,1},{7,3},{8,12},{10,14},{12... | collective-permute-start | bytes 1544 | tf_op jit(solution)/shard_map/ppermute | solution.py:371
  21.8 1.2 collective-permute-start.2
  23.0 0.7 copy-done.2
  23.7 1.0 copy-done.7
  24.7 1.2 follow.1
  26.0 1.0 copy-done.1
  27.6 8.9 %prepare.1 = (bf16[2048,2560]{1,0:T(8,128)(2,1)}, f32[1024,128]{1,0:T(8,128)S(1)}) custom-call(s32[96]{0:T(128)S(1)} %bitcast.64, s32[96]{0:T(128)S(1)} %bitcast.65, s32[1]{0:T(128)} %bitcast.60.count_ref, s32[1,1024]{1,0:T(1,128)S(1)} %copy-done.3, bf16[96,128,128]{2,1,0:T(8,128)(2,1)S(1)} %bitcast.61), custom_call_target="tpu_custom_call" | custom-call | bytes 25165824 | tf_op jit(solution)/shard_map/prepare/pallas_call | solution.py:347
  36.5 0.8 copy-done.8
  37.4 1.8 %collective-permute-start.3 = (s32[4,64]{1,0:T(4,128)S(1)}, s32[4,64]{1,0:T(4,128)S(1)}, u32[]{:S(2)}, u32[]{:S(2)}) collective-permute-start(s32[4,64]{1,0:T(4,128)S(1)} %bitcast.72), channel_id=1, source_target_pairs={{0,1},{1,0},{2,3},{3,2},{4,5},{5,4},{6,7},{7,6},{8,9},{9,8},{10,11... | collective-permute-start | bytes 3080 | tf_op jit(solution)/shard_map/ppermute | solution.py:460
  39.1 0.8 collective-permute-done.3
  40.2 1.2 copy-done.6
  41.4 0.7 pick.1
  42.1 0.4 all-to-all-done
  42.5 8.6 %all-to-all-start.1 = ((bf16[32,64,256]{2,1,0:T(8,128)(2,1)}), bf16[32,64,256]{2,1,0:T(8,128)(2,1)S(1)}, u32[]{:S(2)}, u32[]{:S(2)}) async-start(bf16[32,64,256]{2,1,0:T(8,128)(2,1)} %bitcast.63), calls=%async_computation.1 | async-start | bytes 2097152 | tf_op jit(solution)/shard_map/all_to_all | solution.py:314
  51.1 1.5 collective-permute-start.4
  52.7 1.1 collective-permute-done.4
  53.9 1.3 collective-permute-start.7
  55.2 2.5 %collective-permute-start.6 = (bf16[256,256]{1,0:T(8,128)(2,1)S(1)}, bf16[256,256]{1,0:T(8,128)(2,1)S(1)}, u32[]{:S(2)}, u32[]{:S(2)}) collective-permute-start(bf16[256,256]{1,0:T(8,128)(2,1)S(1)} %pad_maximum_fusion.3), channel_id=1, source_target_pairs={{0,4},{2,6},{4,0},{6,2},{1,5},{3,7},{5,1},{7,3},{8,12},{10,14},{12... | collective-permute-start | bytes 393224 | tf_op jit(solution)/shard_map/ppermute | solution.py:371
  57.7 1.4 collective-permute-start.5
  59.1 0.6 pad_add_fusion.2.refs_0_
  59.7 0.7 pad_maximum_fusion.1.refs_4_
  60.4 3.3 %collective-permute-done.6.refs_6_ = bf16[256,256]{1,0:T(8,128)(2,1)S(1)} collective-permute-done((bf16[256,256]{1,0:T(8,128)(2,1)S(1)}, bf16[256,256]{1,0:T(8,128)(2,1)S(1)}, u32[]{:S(2)}, u32[]{:S(2)}) %collective-permute-start.6) | collective-permute-done | bytes 131104 | tf_op jit(solution)/shard_map/ppermute | solution.py:371
  63.7 0.7 copy-done.14
  64.3 0.6 copy-done.15
  65.0 12.4 %forward.1 = (bf16[2048,256]{1,0:T(8,128)(2,1)}, bf16[2,2048,256]{2,1,0:T(8,128)(2,1)}, f32[2,2048,256]{2,1,0:T(8,128)}) custom-call(s32[2]{0:T(128)} %pad_add_fusion.2.refs_0_, bf16[2048,256]{1,0:T(8,128)(2,1)} %bitcast.4.refs_1_, bf16[2,256,256]{2,1,0:T(8,128)(2,1)} %w_ref.1, bf16[2048,2560]{1,0:T(8,128)(2,1)} %get-tuple-element.30.refs_3_.adj_hbm, ...), custom_call_target="tpu_custom_call" | custom-call | flops 5905580032 | bytes 25165824 | tf_op jit(solution)/shard_map/forward/pallas_call | solution.py:396
  77.4 9.5 %all-to-all-start.2 = ((bf16[32,64,256]{2,1,0:T(8,128)(2,1)}), bf16[32,64,256]{2,1,0:T(8,128)(2,1)S(1)}, u32[]{:S(2)}, u32[]{:S(2)}) async-start(bf16[32,64,256]{2,1,0:T(8,128)(2,1)} %bitcast.67), calls=%async_computation.2 | async-start | bytes 2097152 | tf_op jit(solution)/shard_map/all_to_all | solution.py:314
  87.0 9.6 %backward.1 = f32[2,256,256]{2,1,0:T(8,128)} custom-call(bf16[2048,256]{1,0:T(8,128)(2,1)} %bitcast.66, bf16[2,256,256]{2,1,0:T(8,128)(2,1)} %w_ref.1, bf16[2048,2560]{1,0:T(8,128)(2,1)} %get-tuple-element.30.refs_3_.adj_hbm, bf16[2,2048,256]{2,1,0:T(8,128)(2,1)} %get-tuple-element.36.m_hbm, f32[2,2048,256]{2,1,0:T(8,128)} %get-tuple-element.37.s_hbm), custom_call_target="tpu_custom_call" | custom-call | flops 2952790016 | bytes 20971520 | tf_op jit(solution)/shard_map/backward/pallas_call | solution.py:426
  96.5 1.1 select_bitcast_fusion.2
  97.6 1.6 %collective-permute-start.8 = (f32[256,256]{1,0:T(8,128)S(1)}, f32[256,256]{1,0:T(8,128)S(1)}, u32[]{:S(2)}, u32[]{:S(2)}) collective-permute-start(f32[256,256]{1,0:T(8,128)S(1)} %select_bitcast_fusion.2), channel_id=1, source_target_pairs={{0,1},{1,0},{2,3},{3,2},{4,5},{5,4},{6,7},{7,6},{8,9},{9,8},{10,11... | collective-permute-start | bytes 786440 | tf_op jit(solution)/shard_map/ppermute | solution.py:460
  99.2 1.2 collective-permute-done.8
  100.3 1.1 bitcast_add_fusion
  101.5 2.1 %collective-permute-start.10 = (f32[64,256]{1,0:T(8,128)S(1)}, f32[64,256]{1,0:T(8,128)S(1)}, u32[]{:S(2)}, u32[]{:S(2)}) collective-permute-start(f32[64,256]{1,0:T(8,128)S(1)} %get-tuple-element.48), channel_id=1, source_target_pairs={{0,4},{2,6},{4,0},{6,2},{1,5},{3,7},{5,1},{7,3},{8,12},{10,14},{12... | collective-permute-start | bytes 196616 | tf_op jit(solution)/shard_map/ppermute | solution.py:477
  103.6 1.3 collective-permute-start.11
  105.1 1.6 %collective-permute-done.10 = f32[64,256]{1,0:T(8,128)S(1)} collective-permute-done((f32[64,256]{1,0:T(8,128)S(1)}, f32[64,256]{1,0:T(8,128)S(1)}, u32[]{:S(2)}, u32[]{:S(2)}) %collective-permute-start.10) | collective-permute-done | bytes 65568 | tf_op jit(solution)/shard_map/ppermute | solution.py:477
  106.7 0.6 collective-permute-done.11
  107.2 2.3 %collective-permute-done.9 = f32[64,256]{1,0:T(8,128)S(1)} collective-permute-done((f32[64,256]{1,0:T(8,128)S(1)}, f32[64,256]{1,0:T(8,128)S(1)}, u32[]{:S(2)}, u32[]{:S(2)}) %collective-permute-start.9) | collective-permute-done | bytes 65568 | tf_op jit(solution)/shard_map/ppermute | solution.py:477
  109.6 2.1 %all-to-all-done.2 = bf16[32,64,256]{2,1,0:T(8,128)(2,1)S(1)} async-done(((bf16[32,64,256]{2,1,0:T(8,128)(2,1)}), bf16[32,64,256]{2,1,0:T(8,128)(2,1)S(1)}, u32[]{:S(2)}, u32[]{:S(2)}) %all-to-all-start.2) | async-done | bytes 1048608 | tf_op jit(solution)/shard_map/all_to_all | solution.py:314
  111.7 0.7 reshape.70
  112.3 8.5 %all-to-all-start.3 = ((f32[32,2,256]{2,1,0:T(2,128)}), f32[32,2,256]{2,1,0:T(2,128)S(1)}, u32[]{:S(2)}, u32[]{:S(2)}) async-start(f32[32,2,256]{2,1,0:T(2,128)} %reshape.70), calls=%async_computation.3 | async-start | bytes 131072 | tf_op jit(solution)/shard_map/all_to_all | solution.py:486
  120.8 2.0 %collect.1 = bf16[1024,256]{1,0:T(8,128)(2,1)} custom-call(f32[1024,128]{1,0:T(8,128)S(1)} %copy-done.9, bf16[2048,256]{1,0:T(8,128)(2,1)S(1)} %bitcast.62), custom_call_target="tpu_custom_call" | custom-call | flops 1073741824 | bytes 2097152 | tf_op jit(solution)/shard_map/collect/pallas_call | solution.py:445
  122.9 6.9 %all-to-all-done.3 = f32[32,2,256]{2,1,0:T(2,128)S(1)} async-done(((f32[32,2,256]{2,1,0:T(2,128)}), f32[32,2,256]{2,1,0:T(2,128)S(1)}, u32[]{:S(2)}, u32[]{:S(2)}) %all-to-all-start.3) | async-done | bytes 65568 | tf_op jit(solution)/shard_map/all_to_all | solution.py:486
  129.9 18.9 %all_to_all.25 = f32[128,2,256]{2,1,0:T(2,128)S(1)} all-to-all(f32[128,2,256]{2,1,0:T(2,128)S(1)} %broadcast_in_dim.27), channel_id=1, replica_groups=mesh['y'=4,'z'=8,'x'=4,'core'=2] {'x','y','z'}, dimensions={0} | all-to-all | bytes 524288 | tf_op jit(solution)/shard_map/all_to_all | solution.py:496
  148.9 3.7 %collective-permute-start.12 = (f32[256,256]{1,0:T(8,128)S(1)}, f32[256,256]{1,0:T(8,128)S(1)}, u32[]{:S(2)}, u32[]{:S(2)}) collective-permute-start(f32[256,256]{1,0:T(8,128)S(1)} %reshape.71), channel_id=1, source_target_pairs={{0,1},{1,0},{2,3},{3,2},{4,5},{5,4},{6,7},{7,6},{8,9},{9,8},{10,11... | collective-permute-start | bytes 786440 | tf_op jit(solution)/shard_map/ppermute | solution.py:460
  152.6 1.2 collective-permute-done.12
  153.8 0.8 pad_maximum_fusion
  (52 shorter events, 1.0 us)
Async XLA Ops:
  0.6 17.3 %copy-start.12 = (s32[1,1,8]{2,1,0:T(1,128)S(1)}, s32[1,1,8]{2,1,0:T(1,128)}, u32[]{:S(2)}) copy-start(s32[1,1,8]{2,1,0:T(1,128)} %param.17) | copy-start | bytes 100
  0.6 17.3 %copy-start.11 = (s32[1,1,8,64]{3,2,1,0:T(8,128)S(1)}, s32[1,1,8,64]{3,2,1,0:T(8,128)}, u32[]{:S(2)}) copy-start(s32[1,1,8,64]{3,2,1,0:T(8,128)} %param.16) | copy-start | bytes 6148
  0.7 26.9 %copy-start = (bf16[1,1,96,128,128]{4,3,2,1,0:T(8,128)(2,1)S(1)}, bf16[1,1,96,128,128]{4,3,2,1,0:T(8,128)(2,1)}, u32[]{:S(2)}) copy-start(bf16[1,1,96,128,128]{4,3,2,1,0:T(8,128)(2,1)} %param.21) | copy-start | bytes 9437188
  0.7 26.9 %copy-start.4 = (s32[1,1,96]{2,1,0:T(1,128)S(1)}, s32[1,1,96]{2,1,0:T(1,128)}, u32[]{:S(2)}) copy-start(s32[1,1,96]{2,1,0:T(1,128)} %param.18) | copy-start | bytes 1156
  0.7 26.9 %copy-start.5 = (s32[1,1,96]{2,1,0:T(1,128)S(1)}, s32[1,1,96]{2,1,0:T(1,128)}, u32[]{:S(2)}) copy-start(s32[1,1,96]{2,1,0:T(1,128)} %param.19) | copy-start | bytes 1156
  5.7 21.9 %copy-start.3 = (s32[1,1024]{1,0:T(1,128)S(1)}, s32[1,1024]{1,0:T(1,128)}, u32[]{:S(2)}) copy-start(s32[1,1024]{1,0:T(1,128)} %get-tuple-element.23.place_ref) | copy-start | bytes 12292
  5.8 36.8 %all-to-all-start = ((bf16[32,64,256]{2,1,0:T(8,128)(2,1)}), bf16[32,64,256]{2,1,0:T(8,128)(2,1)}, u32[]{:S(2)}, u32[]{:S(2)}) async-start(bf16[32,64,256]{2,1,0:T(8,128)(2,1)} %bitcast.68), calls=%async_computation | async-start | bytes 2097152 | tf_op jit(solution)/shard_map/all_to_all | solution.py:314
  18.1 19.3 %collective-permute-start = (s32[2,64]{1,0:T(2,128)S(1)}, s32[2,64]{1,0:T(2,128)S(1)}, u32[]{:S(2)}, u32[]{:S(2)}) collective-permute-start(s32[2,64]{1,0:T(2,128)S(1)} %get-tuple-element.62), channel_id=1, source_target_pairs={{0,2},{2,4},{4,6},{6,0},{1,3},{3,5},{5,7},{7,1},{8,10},{10,12},{12... | collective-permute-start | bytes 1544 | tf_op jit(solution)/shard_map/ppermute | solution.py:371
  19.4 18.0 %collective-permute-start.1 = (s32[2,64]{1,0:T(2,128)S(1)}, s32[2,64]{1,0:T(2,128)S(1)}, u32[]{:S(2)}, u32[]{:S(2)}) collective-permute-start(s32[2,64]{1,0:T(2,128)S(1)} %get-tuple-element.61), channel_id=1, source_target_pairs={{0,4},{2,6},{4,0},{6,2},{1,5},{3,7},{5,1},{7,3},{8,12},{10,14},{12... | collective-permute-start | bytes 1544 | tf_op jit(solution)/shard_map/ppermute | solution.py:371
  21.8 15.5 %collective-permute-start.2 = (s32[2,64]{1,0:T(2,128)S(1)}, s32[2,64]{1,0:T(2,128)S(1)}, u32[]{:S(2)}, u32[]{:S(2)}) collective-permute-start(s32[2,64]{1,0:T(2,128)S(1)} %get-tuple-element.63), channel_id=1, source_target_pairs={{0,6},{2,0},{4,2},{6,4},{1,7},{3,1},{5,3},{7,5},{8,14},{10,8},{12,... | collective-permute-start | bytes 1544 | tf_op jit(solution)/shard_map/ppermute | solution.py:371
  23.0 0.7 copy-start.2
  23.7 1.0 copy-start.7
  26.0 1.0 copy-start.1
  36.5 0.8 copy-start.8
  37.4 2.6 %collective-permute-start.3 = (s32[4,64]{1,0:T(4,128)S(1)}, s32[4,64]{1,0:T(4,128)S(1)}, u32[]{:S(2)}, u32[]{:S(2)}) collective-permute-start(s32[4,64]{1,0:T(4,128)S(1)} %bitcast.72), channel_id=1, source_target_pairs={{0,1},{1,0},{2,3},{3,2},{4,5},{5,4},{6,7},{7,6},{8,9},{9,8},{10,11... | collective-permute-start | bytes 3080 | tf_op jit(solution)/shard_map/ppermute | solution.py:460
  40.2 1.2 copy-start.6
  42.5 34.9 %all-to-all-start.1 = ((bf16[32,64,256]{2,1,0:T(8,128)(2,1)}), bf16[32,64,256]{2,1,0:T(8,128)(2,1)S(1)}, u32[]{:S(2)}, u32[]{:S(2)}) async-start(bf16[32,64,256]{2,1,0:T(8,128)(2,1)} %bitcast.63), calls=%async_computation.1 | async-start | bytes 2097152 | tf_op jit(solution)/shard_map/all_to_all | solution.py:314
  51.1 2.7 %collective-permute-start.4 = (bf16[4,128,256]{2,1,0:T(8,128)(2,1)S(1)}, bf16[4,128,256]{2,1,0:T(8,128)(2,1)S(1)}, u32[]{:S(2)}, u32[]{:S(2)}) collective-permute-start(bf16[4,128,256]{2,1,0:T(8,128)(2,1)S(1)} %get-tuple-element.32), channel_id=1, source_target_pairs={{0,1},{1,0},{2,3},{3,2},{4,5},{5,4},{6,7},{7,6},{8,9},{9,8},{10,11... | collective-permute-start | bytes 786440 | tf_op jit(solution)/shard_map/ppermute | solution.py:460
  53.9 6.5 %collective-permute-start.7 = (bf16[256,256]{1,0:T(8,128)(2,1)S(1)}, bf16[256,256]{1,0:T(8,128)(2,1)S(1)}, u32[]{:S(2)}, u32[]{:S(2)}) collective-permute-start(bf16[256,256]{1,0:T(8,128)(2,1)S(1)} %pad_maximum_fusion.4), channel_id=1, source_target_pairs={{0,2},{2,4},{4,6},{6,0},{1,3},{3,5},{5,7},{7,1},{8,10},{10,12},{12... | collective-permute-start | bytes 393224 | tf_op jit(solution)/shard_map/ppermute | solution.py:371
  55.2 8.5 %collective-permute-start.6 = (bf16[256,256]{1,0:T(8,128)(2,1)S(1)}, bf16[256,256]{1,0:T(8,128)(2,1)S(1)}, u32[]{:S(2)}, u32[]{:S(2)}) collective-permute-start(bf16[256,256]{1,0:T(8,128)(2,1)S(1)} %pad_maximum_fusion.3), channel_id=1, source_target_pairs={{0,4},{2,6},{4,0},{6,2},{1,5},{3,7},{5,1},{7,3},{8,12},{10,14},{12... | collective-permute-start | bytes 393224 | tf_op jit(solution)/shard_map/ppermute | solution.py:371
  57.7 5.9 %collective-permute-start.5 = (bf16[256,256]{1,0:T(8,128)(2,1)S(1)}, bf16[256,256]{1,0:T(8,128)(2,1)S(1)}, u32[]{:S(2)}, u32[]{:S(2)}) collective-permute-start(bf16[256,256]{1,0:T(8,128)(2,1)S(1)} %pad_maximum_fusion.2), channel_id=1, source_target_pairs={{0,6},{2,0},{4,2},{6,4},{1,7},{3,1},{5,3},{7,5},{8,14},{10,8},{12,... | collective-permute-start | bytes 393224 | tf_op jit(solution)/shard_map/ppermute | solution.py:371
  60.4 3.3 %copy-start.13 = (bf16[256,256]{1,0:T(8,128)(2,1)}, bf16[256,256]{1,0:T(8,128)(2,1)S(1)}, u32[]{:S(2)}) copy-start(bf16[256,256]{1,0:T(8,128)(2,1)S(1)} %collective-permute-done.7.refs_7_) | copy-start | bytes 393220
  63.7 0.7 copy-start.14
  64.3 0.7 copy-start.15
  77.4 9.5 %copy-start.10 = (bf16[32,64,256]{2,1,0:T(8,128)(2,1)}, bf16[32,64,256]{2,1,0:T(8,128)(2,1)S(1)}, u32[]{:S(2)}) copy-start(bf16[32,64,256]{2,1,0:T(8,128)(2,1)S(1)} %all-to-all-done.1) | copy-start | bytes 3145732
  77.4 34.2 %all-to-all-start.2 = ((bf16[32,64,256]{2,1,0:T(8,128)(2,1)}), bf16[32,64,256]{2,1,0:T(8,128)(2,1)S(1)}, u32[]{:S(2)}, u32[]{:S(2)}) async-start(bf16[32,64,256]{2,1,0:T(8,128)(2,1)} %bitcast.67), calls=%async_computation.2 | async-start | bytes 2097152 | tf_op jit(solution)/shard_map/all_to_all | solution.py:314
  87.0 33.9 %copy-start.9 = (f32[1024,128]{1,0:T(8,128)S(1)}, f32[1024,128]{1,0:T(8,128)}, u32[]{:S(2)}) copy-start(f32[1024,128]{1,0:T(8,128)} %copy-done.8) | copy-start | bytes 1572868
  97.6 2.7 %collective-permute-start.8 = (f32[256,256]{1,0:T(8,128)S(1)}, f32[256,256]{1,0:T(8,128)S(1)}, u32[]{:S(2)}, u32[]{:S(2)}) collective-permute-start(f32[256,256]{1,0:T(8,128)S(1)} %select_bitcast_fusion.2), channel_id=1, source_target_pairs={{0,1},{1,0},{2,3},{3,2},{4,5},{5,4},{6,7},{7,6},{8,9},{9,8},{10,11... | collective-permute-start | bytes 786440 | tf_op jit(solution)/shard_map/ppermute | solution.py:460
  101.5 5.2 %collective-permute-start.10 = (f32[64,256]{1,0:T(8,128)S(1)}, f32[64,256]{1,0:T(8,128)S(1)}, u32[]{:S(2)}, u32[]{:S(2)}) collective-permute-start(f32[64,256]{1,0:T(8,128)S(1)} %get-tuple-element.48), channel_id=1, source_target_pairs={{0,4},{2,6},{4,0},{6,2},{1,5},{3,7},{5,1},{7,3},{8,12},{10,14},{12... | collective-permute-start | bytes 196616 | tf_op jit(solution)/shard_map/ppermute | solution.py:477
  103.6 3.7 %collective-permute-start.11 = (f32[64,256]{1,0:T(8,128)S(1)}, f32[64,256]{1,0:T(8,128)S(1)}, u32[]{:S(2)}, u32[]{:S(2)}) collective-permute-start(f32[64,256]{1,0:T(8,128)S(1)} %get-tuple-element.47), channel_id=1, source_target_pairs={{0,6},{2,0},{4,2},{6,4},{1,7},{3,1},{5,3},{7,5},{8,14},{10,8},{12,... | collective-permute-start | bytes 196616 | tf_op jit(solution)/shard_map/ppermute | solution.py:477
  104.9 4.6 %collective-permute-start.9 = (f32[64,256]{1,0:T(8,128)S(1)}, f32[64,256]{1,0:T(8,128)S(1)}, u32[]{:S(2)}, u32[]{:S(2)}) collective-permute-start(f32[64,256]{1,0:T(8,128)S(1)} %get-tuple-element.46), channel_id=1, source_target_pairs={{0,2},{2,4},{4,6},{6,0},{1,3},{3,5},{5,7},{7,1},{8,10},{10,12},{12... | collective-permute-start | bytes 196616 | tf_op jit(solution)/shard_map/ppermute | solution.py:477
  112.3 17.4 %all-to-all-start.3 = ((f32[32,2,256]{2,1,0:T(2,128)}), f32[32,2,256]{2,1,0:T(2,128)S(1)}, u32[]{:S(2)}, u32[]{:S(2)}) async-start(f32[32,2,256]{2,1,0:T(2,128)} %reshape.70), calls=%async_computation.3 | async-start | bytes 131072 | tf_op jit(solution)/shard_map/all_to_all | solution.py:486
  148.9 4.8 %collective-permute-start.12 = (f32[256,256]{1,0:T(8,128)S(1)}, f32[256,256]{1,0:T(8,128)S(1)}, u32[]{:S(2)}, u32[]{:S(2)}) collective-permute-start(f32[256,256]{1,0:T(8,128)S(1)} %reshape.71), channel_id=1, source_target_pairs={{0,1},{1,0},{2,3},{3,2},{4,5},{5,4},{6,7},{7,6},{8,9},{9,8},{10,11... | collective-permute-start | bytes 786440 | tf_op jit(solution)/shard_map/ppermute | solution.py:460

commit v3 on v2

v3 whole, which is shorter than its diff:
```python
import math

import jax
import jax.numpy as jnp
from jax import lax
from jax.experimental import pallas as pl
from jax.experimental.pallas import tpu as pltpu
from jax.sharding import Mesh
from jax.sharding import PartitionSpec as P

ALPHA = 0.1
BETAS = (math.log(1.5), math.log(1.25))
TILE = 128
CAP = 64
HCAP = 64
MARK = 1024.0
LIMIT = 512.0
BF16 = jnp.bfloat16
F32 = jnp.float32
MIB = 1 << 20
WIDE = ("y", "z")
HIST = ("x", "core")


def vmem(count):
    return [pl.BlockSpec(memory_space=pltpu.VMEM)] * count


def smem(count):
    return [pl.BlockSpec(memory_space=pltpu.SMEM)] * count


def params(limit):
    return pltpu.CompilerParams(vmem_limit_bytes=limit * MIB)


def cost(flops, moved):
    return pl.CostEstimate(flops=flops, bytes_accessed=moved, transcendentals=0)


def in_hbm(value):
    return pltpu.with_memory_space_constraint(value, pltpu.HBM)


def dot(a, b):
    return jnp.dot(a, b, preferred_element_type=F32)


def dot_rows(a, b):
    return lax.dot_general(a, b, (((0,), (0,)), ((), ())), preferred_element_type=F32)


def hits_of(place, start, step):
    slots = lax.broadcasted_iota(jnp.int32, (step, place.shape[1]), 0) + start
    return (slots == place).astype(F32)


def route_body(n_wide, own_ref, x_hbm, send_hbm, place_ref, x_all, send, load_sem, send_sem):
    load = pltpu.make_async_copy(x_hbm, x_all, load_sem)
    load.start()
    rows_here = own_ref.shape[1]
    blocks = rows_here // 128
    own = own_ref[...]
    hot = (own == lax.broadcasted_iota(jnp.int32, (n_wide, rows_here), 0)).astype(F32)
    hot_b = hot.astype(BF16)
    lower = lax.broadcasted_iota(jnp.int32, (128, 128), 0)
    upper = lax.broadcasted_iota(jnp.int32, (128, 128), 1)
    earlier = (lower < upper).astype(F32).astype(BF16)
    parts = [slice(128 * b, 128 * (b + 1)) for b in range(blocks)]
    inside = dot(jnp.concatenate([hot_b[:, part] for part in parts], axis=0), earlier)
    before = jnp.zeros((n_wide, 1), F32)
    ranks = []
    for b, part in enumerate(parts):
        seen = inside[n_wide * b : n_wide * (b + 1)] + before
        ranks.append(jnp.sum(seen * hot[:, part], axis=0, keepdims=True))
        before = before + jnp.sum(hot[:, part], axis=1, keepdims=True)
    rank = jnp.concatenate(ranks, axis=1)
    place_ref[...] = own * CAP + rank.astype(jnp.int32)
    by_rank = (rank == lax.broadcasted_iota(jnp.int32, (CAP, rows_here), 0).astype(F32)).astype(F32)
    by_rank = by_rank.astype(BF16)
    slot = lax.broadcasted_iota(jnp.int32, (CAP, 1), 0).astype(F32)
    load.wait()
    peers = 8
    step = peers * CAP
    stores = []
    for c in range(n_wide // peers):
        part = pl.ds(c * step, step)
        group = range(c * peers, (c + 1) * peers)
        hit = jnp.concatenate([by_rank * hot_b[o : o + 1, :] for o in group], axis=0)
        held = jnp.concatenate([slot < before[o : o + 1, :] for o in group], axis=0)
        send[part, :] = jnp.where(held, dot(hit, x_all[...]), MARK).astype(BF16)
        store = pltpu.make_async_copy(send.at[part], send_hbm.at[part], send_sem.at[c])
        store.start()
        stores.append(store)
    for store in stores:
        store.wait()


def prepare_body(
    rows_ref, cols_ref, count_ref, place_ref, vals_hbm, cot_hbm, adj_hbm, send_hbm, column_ref,
    adj, vals, cot, send, head, following, row_head, row_next, load_sem, adj_sem, send_sem,
):
    loads = (
        pltpu.make_async_copy(vals_hbm, vals, load_sem.at[0]),
        pltpu.make_async_copy(cot_hbm, cot, load_sem.at[1]),
    )
    for load in loads:
        load.start()
    count = count_ref[0]
    n_rows, wide = adj.shape[0] // TILE, adj.shape[1] // TILE
    for r in range(n_rows):
        row_head[r] = -1

    def clear(k, carry):
        head[rows_ref[k] * wide + cols_ref[k]] = -1
        return carry

    lax.fori_loop(0, count, clear, 0)

    def chain(i, carry):
        k = count - 1 - i
        row = rows_ref[k]
        cell = row * wide + cols_ref[k]
        following[k] = head[cell]
        head[cell] = k
        row_next[k] = row_head[row]
        row_head[row] = k
        return carry

    lax.fori_loop(0, count, chain, 0)
    loads[0].wait()

    def row_copy(r):
        part = pl.ds(pl.multiple_of(r * TILE, TILE), TILE)
        return pltpu.make_async_copy(adj.at[part], adj_hbm.at[part], adj_sem.at[r])

    def fill(r, carry):
        part = pl.ds(pl.multiple_of(r * TILE, TILE), TILE)
        adj[part, :] = jnp.zeros((TILE, adj.shape[1]), BF16)

        def place_tile(k):
            col = cols_ref[k]

            @pl.when(head[r * wide + col] == k)
            def _():
                def more(state):
                    at, total = state
                    return following[at], total + vals[at].astype(F32)

                _, total = lax.while_loop(
                    lambda state: state[0] >= 0, more, (following[k], vals[k].astype(F32))
                )
                adj[part, pl.ds(pl.multiple_of(col * TILE, TILE), TILE)] = total.astype(BF16)

            return row_next[k]

        lax.while_loop(lambda k: k >= 0, place_tile, row_head[r])
        row_copy(r).start()
        return carry

    lax.fori_loop(0, n_rows, fill, 0)
    loads[1].wait()
    place = place_ref[...]
    step = 512
    stores = []
    for c in range(send.shape[0] // step):
        part = pl.ds(c * step, step)
        hit = hits_of(place, c * step, step).astype(BF16)
        send[part, :] = dot(hit, cot[...]).astype(BF16)
        store = pltpu.make_async_copy(send.at[part], send_hbm.at[part], send_sem.at[c])
        store.start()
        stores.append(store)
    for b in range(place.shape[1] // 128):
        part = place[:, 128 * b : 128 * (b + 1)].astype(F32)
        column_ref[pl.ds(128 * b, 128), :] = jnp.transpose(jnp.broadcast_to(part, (128, 128)))
    for store in stores:
        store.wait()

    def drain(r, carry):
        row_copy(r).wait()
        return carry

    lax.fori_loop(0, n_rows, drain, 0)


def pick_body(ids_ref, history_ref, *block_refs):
    slots = ids_ref.shape[0]
    here = history_ref.shape[1]
    lane = lax.broadcasted_iota(jnp.int32, (slots, 128), 1)
    ids = ids_ref[...]
    hit = jnp.concatenate(
        [(ids - 128 * c == lane).astype(F32).astype(BF16) for c in range(here // 128)], axis=1
    )
    size = len(block_refs)
    for layer in range(2):
        rows = dot(hit, history_ref[layer]).astype(BF16)
        for side in range(2):
            for k, ref in enumerate(block_refs):
                at = (side * size + k) * HCAP
                ref[pl.ds((2 * side + layer) * HCAP, HCAP), :] = rows[at : at + HCAP]


def forward_body(size, x_ref, core_ref, ws_hbm, w_hbm, adj_hbm, *rest):
    pieces = rest[:size], rest[size : 2 * size]
    out_hbm, m_hbm, s_hbm, adj, w, ws, ext0, ext1, m_all, s_all, out, acc0, acc1, load_sem, keep_sem = rest[2 * size :]
    work, width = ws.shape
    step = acc0.shape[0]
    blocks = work // step
    rows = [pl.ds(b * step, step) for b in range(blocks)]
    x, core = x_ref[0], core_ref[0]
    first = pltpu.make_async_copy(ws_hbm, ws, load_sem.at[0])
    first.start()
    loads = {}

    def load_rows(b, until):
        part = pl.ds(b * step, (until - b) * step)
        sem = load_sem.at[2 + 4 * size + len(loads)]
        loads[b] = pltpu.make_async_copy(adj_hbm.at[part], adj.at[part], sem)
        loads[b].start()

    def load_halo(layer, ext):
        copies = []
        for k in range(size):
            for side in range(2):
                shard = lax.rem(x + k, size) * 2 + lax.rem(core + side, 2)
                there = pl.ds(pl.multiple_of(work + shard * HCAP, HCAP), HCAP)
                here = pl.ds((2 * side + layer) * HCAP, HCAP)
                sem = load_sem.at[2 + (layer * size + k) * 2 + side]
                copies.append(pltpu.make_async_copy(pieces[side][k].at[here], ext.at[there], sem))
                copies[-1].start()
        return copies

    load_rows(0, 1)
    halos = [load_halo(0, ext0)]
    load_rows(1, 4)
    weight = pltpu.make_async_copy(w_hbm, w, load_sem.at[1])
    weight.start()
    load_rows(4, blocks)
    halos.append(load_halo(1, ext1))
    first.wait()
    for part in rows:
        got = ws[part, :].astype(F32)
        ext0[part, :] = jnp.where(got < LIMIT, got, 0.0).astype(BF16)
    for copy in halos[0]:
        copy.wait()
    weight.wait()
    stores = []

    def store(here, there, *at):
        copy = pltpu.make_async_copy(here, there, keep_sem.at[*at])
        copy.start()
        stores.append(copy)

    def keep(layer, b):
        part = rows[b]
        store(m_all.at[layer, part], m_hbm.at[layer, part], layer, 0, b)
        store(s_all.at[layer, part], s_hbm.at[layer, part], layer, 1, b)

    def finish(layer, b, support):
        part = rows[b]
        beta = BETAS[layer]
        mixed = (1.0 - ALPHA) * support + ALPHA * ext0[part, :].astype(F32)
        mixed_b = mixed.astype(BF16)
        m_all[layer, part, :] = mixed_b
        pre = (1.0 - beta) * mixed + beta * dot(mixed_b, w[layer])
        sig = jax.nn.sigmoid(pre)
        valid = ws[part, :].astype(F32) < LIMIT
        raw = pre * sig
        new = jnp.where(valid, raw, 0.0).astype(BF16)
        s_all[layer, part, :] = jnp.where(valid, sig + raw * (1.0 - sig), 0.0)
        (ext1, out)[layer][part, :] = new
        if layer == 1:
            store(out.at[part], out_hbm.at[part], 1, 2, b)
        keep(layer, b)

    accs = (acc0, acc1)
    for layer, ext in enumerate((ext0, ext1)):
        for b in range(blocks + 1):
            if b < blocks:
                if layer == 0 and b in loads:
                    loads[b].wait()
                accs[b % 2][...] = dot(adj[rows[b], :], ext[...])
            if b > 0:
                finish(layer, b - 1, accs[(b - 1) % 2][...])
        if layer == 0:
            for copy in halos[1]:
                copy.wait()
    for copy in stores:
        copy.wait()


def backward_body(core_ref, cot_hbm, w_hbm, adj_hbm, m_hbm, s_hbm, kept_ref, given_ref, cot, w, adj, m_all, s_all, turned, load_sem):
    work, width = cot.shape
    step = 512
    blocks = work // step
    parts = [pl.ds(b * step, step) for b in range(blocks)]
    pairs = [
        (s_hbm.at[1], s_all.at[1]),
        (cot_hbm, cot),
        (m_hbm.at[1], m_all.at[1]),
        (w_hbm, w),
    ]
    pairs += [(adj_hbm.at[:, parts[0]], adj.at[:, parts[0]])]
    pairs += [(s_hbm.at[0], s_all.at[0]), (m_hbm.at[0], m_all.at[0])]
    pairs += [(adj_hbm.at[:, part], adj.at[:, part]) for part in parts[1:]]
    loads = [
        pltpu.make_async_copy(here, there, load_sem.at[i]) for i, (here, there) in enumerate(pairs)
    ]
    for load in loads:
        load.start()
    for load in loads[:4]:
        load.wait()
    beta = BETAS[1]
    total = jnp.zeros((width, width), F32)
    for part in parts:
        grad_two = cot[part, :].astype(F32) * s_all[1, part, :]
        grad_two_b = grad_two.astype(BF16)
        total = total + dot_rows(m_all[1, part, :], grad_two_b)
        through = lax.dot_general(
            grad_two_b, w[1], (((1,), (1,)), ((), ())), preferred_element_type=F32
        )
        grad_mix = (1.0 - beta) * grad_two + beta * through
        turned[:, part] = jnp.transpose(grad_mix.astype(BF16))
    second = BETAS[1] * total
    total = jnp.zeros((width, width), F32)
    for b, part in enumerate(parts):
        for load in loads[4:7] if b == 0 else loads[6 + b : 7 + b]:
            load.wait()
        back = jnp.transpose(dot(turned[...], adj[:, part]))
        grad_one = (1.0 - ALPHA) * back * s_all[0, part, :]
        total = total + dot_rows(m_all[0, part, :], grad_one.astype(BF16))
    first = BETAS[0] * total
    lower = core_ref[0] == 0
    for i in range(width // 128):
        here, there = slice(128 * i, 128 * (i + 1)), pl.ds(width * i, width)
        kept_ref[there, :] = jnp.where(lower, first[:, here], second[:, here])
        given_ref[there, :] = jnp.where(lower, second[:, here], first[:, here])


def collect_body(column_ref, back_ref, out_ref):
    slots = back_ref.shape[0]
    step = 256
    lane = lax.broadcasted_iota(jnp.int32, (step, 128), 1).astype(F32)
    for b in range(out_ref.shape[0] // step):
        part = pl.ds(b * step, step)
        place = column_ref[part, :]
        hit = jnp.concatenate(
            [(place - 128.0 * c == lane).astype(F32).astype(BF16) for c in range(slots // 128)],
            axis=1,
        )
        out_ref[part, :] = dot(hit, back_ref[...]).astype(BF16)


def local(
    x_home,
    cotangent,
    owner,
    weights,
    history,
    halo_ids,
    halo_count,
    tile_rows,
    tile_cols,
    tile_count,
    tile_vals,
):
    n_wide = lax.axis_size(WIDE)
    n_hist = lax.axis_size(HIST)
    rows_here, width = x_home.shape
    work = n_wide * CAP
    halo = n_hist * HCAP
    slots = tile_vals.shape[2]

    anywhere = pl.BlockSpec(memory_space=pl.ANY)
    x = lax.axis_index("x")
    core = lax.axis_index("core")
    size = lax.axis_size("x")

    def to_owners(value):
        value = value.reshape(n_wide, CAP, width)
        return lax.all_to_all(value, WIDE, split_axis=0, concat_axis=0, tiled=True).reshape(
            work, width
        )

    send, place = pl.pallas_call(
        lambda *refs: route_body(n_wide, *refs),
        out_shape=(
            pltpu.HBM((work, width), BF16),
            jax.ShapeDtypeStruct((1, rows_here), jnp.int32),
        ),
        in_specs=vmem(1) + [anywhere],
        out_specs=(anywhere, vmem(1)[0]),
        scratch_shapes=[
            pltpu.VMEM((rows_here, width), BF16),
            pltpu.VMEM((work, width), BF16),
            pltpu.SemaphoreType.DMA,
            pltpu.SemaphoreType.DMA((work // 512,)),
        ],
        compiler_params=params(56),
        cost_estimate=cost(2 * work * rows_here * width, 2 * MIB),
        name="route",
    )(owner.reshape(1, rows_here), x_home)
    ws = to_owners(send)

    adjacency, send_cot, column = pl.pallas_call(
        prepare_body,
        out_shape=(
            pltpu.HBM((work, work + halo), BF16),
            pltpu.HBM((work, width), BF16),
            pltpu.HBM((rows_here, 128), F32),
        ),
        in_specs=smem(3) + vmem(1) + [anywhere] * 2,
        out_specs=(anywhere, anywhere, vmem(1)[0]),
        scratch_shapes=[
            pltpu.VMEM((work, work + halo), BF16),
            pltpu.VMEM((slots, TILE, TILE), BF16),
            pltpu.VMEM((rows_here, width), BF16),
            pltpu.VMEM((work, width), BF16),
            pltpu.SMEM(((work // TILE) * ((work + halo) // TILE),), jnp.int32),
            pltpu.SMEM((slots,), jnp.int32),
            pltpu.SMEM((work // TILE,), jnp.int32),
            pltpu.SMEM((slots,), jnp.int32),
            pltpu.SemaphoreType.DMA((2,)),
            pltpu.SemaphoreType.DMA((work // TILE,)),
            pltpu.SemaphoreType.DMA((work // 512,)),
        ],
        compiler_params=params(56),
        cost_estimate=cost(2 * work * rows_here * width, 20 * MIB),
        name="prepare",
    )(tile_rows[0, 0], tile_cols[0, 0], tile_count[0], place, tile_vals[0, 0], cotangent)

    live = jnp.arange(HCAP)[None, :] < halo_count[0, 0][:, None]
    wanted = jnp.where(live, halo_ids[0, 0], -1)
    wanted, place = lax.optimization_barrier((wanted, place))
    wanted = wanted.reshape(size, 2, HCAP)
    wanted = lax.dynamic_slice_in_dim(jnp.concatenate([wanted, wanted]), x, size, axis=0)

    def shift(value, by):
        return lax.ppermute(value, "x", [(i, (i + by) % size) for i in range(size)])

    asked = jnp.stack([wanted[0]] + [shift(wanted[k], k) for k in range(1, size)])
    asked_own = jnp.where(core == 0, asked[:, 0], asked[:, 1])
    asked_other = swap_cores(jnp.where(core == 0, asked[:, 1], asked[:, 0]))
    asked = jnp.stack([asked_own, asked_other]).reshape(halo, 1)
    blocks = pl.pallas_call(
        pick_body,
        out_shape=(jax.ShapeDtypeStruct((4 * HCAP, width), BF16),) * size,
        in_specs=vmem(2),
        out_specs=tuple(vmem(size)),
        compiler_params=params(12),
        cost_estimate=cost(4 * halo * history.shape[1] * width, 2 * MIB),
        name="pick",
    )(jnp.broadcast_to(asked, (halo, 128)), history)
    send_cot, ws, adjacency, blocks = lax.optimization_barrier((send_cot, ws, adjacency, blocks))
    ws_cot = to_owners(send_cot)

    pieces = [blocks[0]] + [shift(blocks[k], size - k) for k in range(1, size)]
    pieces += [swap_cores(piece) for piece in pieces]

    step = 256
    second, mixed, slopes = pl.pallas_call(
        lambda *refs: forward_body(size, *refs),
        out_shape=(
            pltpu.HBM((work, width), BF16),
            pltpu.HBM((2, work, width), BF16),
            pltpu.HBM((2, work, width), F32),
        ),
        in_specs=smem(2) + [anywhere] * (3 + 2 * size),
        out_specs=(anywhere,) * 3,
        scratch_shapes=[
            pltpu.VMEM((work, work + halo), BF16),
            pltpu.VMEM((2, width, width), BF16),
            pltpu.VMEM((work, width), BF16),
            pltpu.VMEM((work + halo, width), BF16),
            pltpu.VMEM((work + halo, width), BF16),
            pltpu.VMEM((2, work, width), BF16),
            pltpu.VMEM((2, work, width), F32),
            pltpu.VMEM((work, width), BF16),
            pltpu.VMEM((step, width), F32),
            pltpu.VMEM((step, width), F32),
            pltpu.SemaphoreType.DMA((5 + 4 * size,)),
            pltpu.SemaphoreType.DMA((2, 3, work // step)),
        ],
        compiler_params=params(56),
        cost_estimate=cost(4 * work * (work + halo + width) * width, 24 * MIB),
        name="forward",
    )(
        x.reshape(1).astype(jnp.int32),
        core.reshape(1).astype(jnp.int32),
        in_hbm(ws),
        weights,
        adjacency,
        *[in_hbm(piece) for piece in pieces],
    )
    second, ws_cot = lax.optimization_barrier((second, ws_cot))
    returned = to_owners(second)

    kept, given = pl.pallas_call(
        backward_body,
        out_shape=(jax.ShapeDtypeStruct((width * width // 128, 128), F32),) * 2,
        in_specs=smem(1) + [anywhere] * 5,
        out_specs=tuple(vmem(2)),
        scratch_shapes=[
            pltpu.VMEM((work, width), BF16),
            pltpu.VMEM((2, width, width), BF16),
            pltpu.VMEM((work, work), BF16),
            pltpu.VMEM((2, work, width), BF16),
            pltpu.VMEM((2, work, width), F32),
            pltpu.VMEM((width, work), BF16),
            pltpu.SemaphoreType.DMA((10,)),
        ],
        compiler_params=params(56),
        cost_estimate=cost(2 * work * (work + 3 * width) * width, 20 * MIB),
        name="backward",
    )(core.reshape(1).astype(jnp.int32), in_hbm(ws_cot), weights, adjacency, mixed, slopes)
    grads = reduce_rows(kept + swap_cores(given))
    grads, returned = lax.optimization_barrier((grads, returned))
    second_out = pl.pallas_call(
        collect_body,
        out_shape=jax.ShapeDtypeStruct((rows_here, width), BF16),
        in_specs=vmem(2),
        out_specs=vmem(1)[0],
        compiler_params=params(24),
        cost_estimate=cost(2 * work * rows_here * width, 2 * MIB),
        name="collect",
    )(column, returned)
    mine = sum_wide(grads, n_wide)
    mine, second_out = lax.optimization_barrier((mine, second_out))
    return (second_out, spread(mine))


def swap_cores(value):
    return lax.ppermute(value, "core", [(0, 1), (1, 0)])


def reduce_rows(kept):
    size = lax.axis_size("x")
    quarter = kept.shape[0] // size
    x = lax.axis_index("x")

    def rows_of(index):
        return lax.dynamic_slice_in_dim(kept, lax.rem(index, size) * quarter, quarter, axis=0)

    total = rows_of(x)
    for k in range(1, size):
        total = total + lax.ppermute(
            rows_of(x + k), "x", [(i, (i + k) % size) for i in range(size)]
        )
    return total


def sum_wide(part, n_wide):
    rows, lanes = part.shape
    parts = lax.all_to_all(
        part.reshape(n_wide, rows // n_wide, lanes), WIDE, split_axis=0, concat_axis=0, tiled=True
    )
    return jnp.sum(parts, axis=0, keepdims=True).astype(BF16)


def spread(mine):
    _, some, lanes = mine.shape
    every = ("x",) + WIDE
    n_every = lax.axis_size(every)
    own = lax.all_to_all(
        jnp.broadcast_to(mine, (n_every, some, lanes)),
        every,
        split_axis=0,
        concat_axis=0,
        tiled=True,
    ).reshape(n_every * some, lanes)
    other = swap_cores(own)
    core = lax.axis_index("core")
    both = [jnp.where(core == 0, own, other), jnp.where(core == 0, other, own)]
    width = math.isqrt(n_every * some * lanes)
    return jnp.stack(
        [
            jnp.concatenate([one[i : i + width] for i in range(0, n_every * some, width)], axis=1)
            for one in both
        ]
    ).astype(F32)


def solution(mesh):
    sizes = (4, mesh.shape["wide"] // 4, mesh.shape["hist"] // 2, 2)
    split = Mesh(mesh.devices.reshape(sizes), WIDE + HIST)
    rows = P(WIDE + HIST, None)
    placed = (
        rows,
        rows,
        rows,
        P(),
        P(None, HIST, None),
        P(WIDE, HIST, None, None),
        P(WIDE, HIST, None),
        P(WIDE, HIST, None),
        P(WIDE, HIST, None),
        P(WIDE, HIST),
        P(WIDE, HIST, None, None, None),
    )
    return jax.shard_map(
        local,
        mesh=split,
        in_specs=placed,
        out_specs=(rows, P()),
        check_vma=False,
    )
```

time: 155 us -> 153 us (0.987)
  waiting for transfers between devices: 21.4 us -> 27.5 us
  local copies, waits for them, and re-layouts: 7.26 us -> 1.92 us
  Pallas kernels: 39.9 us -> 37.6 us
  starting transfers between devices: 61 us -> 63.1 us
  other arithmetic: 4.47 us -> 2.65 us
    all_to_all x3, waiting for transfers between devices: 2.52 us -> 12.6 us  [to_owners(): lax.all_to_all(value, WIDE, split_axis=0, concat_axis=0, tiled=True)]
    unnamed x32 -> x28, local copies, waits for them, and re-layouts: 6.07 us -> 1.63 us
    ppermute x4 -> x7, starting transfers between devices: 8.53 us -> 11.7 us  [swap_cores(): return lax.ppermute(value, 'core', [(0, 1), (1, 0)])]
    ppermute x6, waiting for transfers between devices: 3.27 us -> 0.73 us  [shift(): return lax.ppermute(value, 'x', [(i, (i + by) % size) for i in range(size)])]
    pallas_call x3 -> x2, Pallas kernels: 11.5 us -> 9.4 us  [the longest x1 8.69 us: local(): pl.pallas_call(backward_body, out_shape=(jax.ShapeDtypeStruct((width * wi...]
    ppermute x4 -> x7, waiting for transfers between devices: 4.28 us -> 4.13 us  [swap_cores(): return lax.ppermute(value, 'core', [(0, 1), (1, 0)])]
  transfers between devices with their start and end apart: 17 -> 20, of which waited for: 11 -> 11; matrix products, arithmetic and copies ran while one was open for 2% -> 1% of each run, Pallas kernels for 23% -> 22%
where the time goes in v3:
time: 153 us; the launch traced here: 152 us
  starting transfers between devices  63.1 us (41%)
  Pallas kernels  37.6 us (25%)
  waiting for transfers between devices  27.5 us (18%)
  blocking collectives  17.7 us (12%)
  other arithmetic  2.65 us (2%)
  local copies, waits for them, and re-layouts  1.92 us (1%)
  between operations  1.65 us (1%)
    all_to_all x3, starting transfers between devices, to_owners(): lax.all_to_all(value, WIDE, split_axis=0, concat_axis=0, tiled=True)  30.1 us
    all_to_all x1, blocking collectives, spread(): lax.all_to_all(jnp.broadcast_to(mine, (n_every, some, lanes)), every, spl...  17.7 us
    all_to_all x3, waiting for transfers between devices, to_owners(): lax.all_to_all(value, WIDE, split_axis=0, concat_axis=0, tiled=True)  12.6 us
    pallas_call x1, Pallas kernels, local(): pl.pallas_call(lambda *refs: forward_body(size, *refs), out_shape=(pltpu....  12.6 us
    ppermute x7, starting transfers between devices, swap_cores(): return lax.ppermute(value, 'core', [(0, 1), (1, 0)])  11.7 us
    ppermute x6, starting transfers between devices, shift(): return lax.ppermute(value, 'x', [(i, (i + by) % size) for i in range(size)])  9.19 us
    pallas_call x1, Pallas kernels, local(): pl.pallas_call(prepare_body, out_shape=(pltpu.HBM((work, work + halo), BF...  9.08 us
    pallas_call x1, Pallas kernels, local(): pl.pallas_call(backward_body, out_shape=(jax.ShapeDtypeStruct((width * wi...  8.69 us
  transfers between devices with their start and end apart: 20, of which 11 were waited for; matrix products, arithmetic and copies ran while one was open for 1% of the time, Pallas kernels for 22%

profile of v3, /device:TPU:1, one launch (start us, length us, event | category | flops | bytes accessed | tf_op | source)
XLA Modules:
  0.0 152.1 jit_solution(17620593670269521381)
XLA Ops:
  0.7 4.5 %route.1 = (bf16[2048,256]{1,0:T(8,128)(2,1)}, s32[1,1024]{1,0:T(1,128)}) custom-call(s32[1,1024]{1,0:T(1,128)} %bitcast.63, bf16[1024,256]{1,0:T(8,128)(2,1)} %refs_1_.1), custom_call_target="tpu_custom_call" | custom-call | flops 1073741824 | bytes 2097152 | tf_op jit(solution)/shard_map/route/pallas_call | solution.py:385
  5.1 0.0 copy-start
  5.1 12.2 %all-to-all-start = ((bf16[32,64,256]{2,1,0:T(8,128)(2,1)}), bf16[32,64,256]{2,1,0:T(8,128)(2,1)S(1)}, u32[]{:S(2)}, u32[]{:S(2)}) async-start(bf16[32,64,256]{2,1,0:T(8,128)(2,1)} %bitcast.50), calls=%async_computation | async-start | bytes 2097152 | tf_op jit(solution)/shard_map/all_to_all | solution.py:381
  17.4 0.1 bitcast_select_fusion
  17.5 1.3 collective-permute-start
  18.8 2.5 %collective-permute-start.1 = (s32[2,64]{1,0:T(2,128)S(1)}, s32[2,64]{1,0:T(2,128)S(1)}, u32[]{:S(2)}, u32[]{:S(2)}) collective-permute-start(s32[2,64]{1,0:T(2,128)S(1)} %get-tuple-element.71), channel_id=1, source_target_pairs={{0,4},{2,6},{4,0},{6,2},{1,5},{3,7},{5,1},{7,3},{8,12},{10,14},{12... | collective-permute-start | bytes 1544 | tf_op jit(solution)/shard_map/ppermute | solution.py:439
  21.2 1.2 collective-permute-start.2
  23.0 9.1 %prepare.1 = (bf16[2048,2560]{1,0:T(8,128)(2,1)}, bf16[2048,256]{1,0:T(8,128)(2,1)}, f32[1024,128]{1,0:T(8,128)}) custom-call(s32[96]{0:T(128)} %bitcast.64, s32[96]{0:T(128)} %bitcast.65, s32[1]{0:T(128)} %bitcast.44.count_ref, s32[1,1024]{1,0:T(1,128)} %get-tuple-element.30.place_ref, bf16[96,128,128]{2,1,0:T(8,128)(2,1)} %bitcast.62, ...), custom_call_target="tpu_custom_call" | custom-call | flops 1073741824 | bytes 20971520 | tf_op jit(solution)/shard_map/prepare/pallas_call | solution.py:405
  32.2 0.8 collective-permute-start.3
  33.0 0.8 collective-permute-done.3
  33.8 0.1 broadcast_in_dim.21
  33.9 0.1 broadcast_in_dim.22.ids_ref
  34.1 0.7 pick.1
  34.8 0.0 copy-start.1
  34.8 7.2 %all-to-all-done = bf16[32,64,256]{2,1,0:T(8,128)(2,1)S(1)} async-done(((bf16[32,64,256]{2,1,0:T(8,128)(2,1)}), bf16[32,64,256]{2,1,0:T(8,128)(2,1)S(1)}, u32[]{:S(2)}, u32[]{:S(2)}) %all-to-all-start) | async-done | bytes 1048608 | tf_op jit(solution)/shard_map/all_to_all | solution.py:381
  42.0 1.0 copy-done.4
  42.9 8.6 %all-to-all-start.1 = ((bf16[32,64,256]{2,1,0:T(8,128)(2,1)}), bf16[32,64,256]{2,1,0:T(8,128)(2,1)S(1)}, u32[]{:S(2)}, u32[]{:S(2)}) async-start(bf16[32,64,256]{2,1,0:T(8,128)(2,1)} %bitcast.49), calls=%async_computation.1 | async-start | bytes 2097152 | tf_op jit(solution)/shard_map/all_to_all | solution.py:381
  51.5 1.3 collective-permute-start.6
  52.8 1.5 collective-permute-start.4
  54.3 1.5 %collective-permute-start.5 = (bf16[256,256]{1,0:T(8,128)(2,1)S(1)}, bf16[256,256]{1,0:T(8,128)(2,1)S(1)}, u32[]{:S(2)}, u32[]{:S(2)}) collective-permute-start(bf16[256,256]{1,0:T(8,128)(2,1)S(1)} %get-tuple-element.43), channel_id=1, source_target_pairs={{0,4},{2,6},{4,0},{6,2},{1,5},{3,7},{5,1},{7,3},{8,12},{10,14},{12... | collective-permute-start | bytes 393224 | tf_op jit(solution)/shard_map/ppermute | solution.py:439
  55.8 2.3 %collective-permute-start.7 = (bf16[256,256]{1,0:T(8,128)(2,1)S(1)}, bf16[256,256]{1,0:T(8,128)(2,1)S(1)}, u32[]{:S(2)}, u32[]{:S(2)}) collective-permute-start(bf16[256,256]{1,0:T(8,128)(2,1)S(1)} %get-tuple-element.41.refs_5_), channel_id=1, source_target_pairs={{0,1},{1,0},{2,3},{3,2},{4,5},{5,4},{6,7},{7,6},{8,9},{9,8},{10,11... | collective-permute-start | bytes 393224 | tf_op jit(solution)/shard_map/ppermute | solution.py:533
  58.1 1.5 collective-permute-start.10
  59.6 1.0 collective-permute-start.8
  60.6 0.7 collective-permute-done.5.refs_7_
  61.3 1.7 %collective-permute-start.9 = (bf16[256,256]{1,0:T(8,128)(2,1)S(1)}, bf16[256,256]{1,0:T(8,128)(2,1)S(1)}, u32[]{:S(2)}, u32[]{:S(2)}) collective-permute-start(bf16[256,256]{1,0:T(8,128)(2,1)S(1)} %collective-permute-done.5.refs_7_), channel_id=1, source_target_pairs={{0,1},{1,0},{2,3},{3,2},{4,5},{5,4},{6,7},{7,6},{8,9},{9,8},{10,11... | collective-permute-start | bytes 393224 | tf_op jit(solution)/shard_map/ppermute | solution.py:533
  63.1 0.9 collective-permute-done.9.refs_11_
  64.1 0.6 copy-done.13
  64.7 12.6 %forward.1 = (bf16[2048,256]{1,0:T(8,128)(2,1)}, bf16[2,2048,256]{2,1,0:T(8,128)(2,1)}, f32[2,2048,256]{2,1,0:T(8,128)}) custom-call(s32[1]{0:T(128)} %bitcast.1.refs_0_, s32[1]{0:T(128)} %bitcast.refs_1_.core_ref, bf16[2048,256]{1,0:T(8,128)(2,1)} %bitcast.47, bf16[2,256,256]{2,1,0:T(8,128)(2,1)} %w_hbm.1, ...), custom_call_target="tpu_custom_call" | custom-call | flops 5905580032 | bytes 25165824 | tf_op jit(solution)/shard_map/forward/pallas_call | solution.py:461
  77.3 9.3 %all-to-all-start.2 = ((bf16[32,64,256]{2,1,0:T(8,128)(2,1)}), bf16[32,64,256]{2,1,0:T(8,128)(2,1)S(1)}, u32[]{:S(2)}, u32[]{:S(2)}) async-start(bf16[32,64,256]{2,1,0:T(8,128)(2,1)} %bitcast.48), calls=%async_computation.2 | async-start | bytes 2097152 | tf_op jit(solution)/shard_map/all_to_all | solution.py:381
  86.6 8.7 %backward.1 = (f32[512,128]{1,0:T(8,128)}, f32[512,128]{1,0:T(8,128)}) custom-call(s32[1]{0:T(128)} %bitcast.refs_1_.core_ref, bf16[2048,256]{1,0:T(8,128)(2,1)} %bitcast.46, bf16[2,256,256]{2,1,0:T(8,128)(2,1)} %w_hbm.1, bf16[2048,2560]{1,0:T(8,128)(2,1)} %get-tuple-element.40.refs_4_.adj_hbm, bf16[2,2048,256]{2,1,0:T(8,128)(2,1)} %get-tuple-element.48.m_hbm, ...), custom_call_target="tpu_custom_call" | custom-call | flops 2952790016 | bytes 20971520 | tf_op jit(solution)/shard_map/backward/pallas_call | solution.py:498
  95.3 0.7 collective-permute-start.11
  96.0 1.4 collective-permute-done.11
  97.4 1.0 add.37
  98.4 0.6 collective-permute-start.12
  99.0 2.6 %collective-permute-start.13 = (f32[128,128]{1,0:T(8,128)S(1)}, f32[128,128]{1,0:T(8,128)S(1)}, u32[]{:S(2)}, u32[]{:S(2)}) collective-permute-start(f32[128,128]{1,0:T(8,128)S(1)} %get-tuple-element.62), channel_id=1, source_target_pairs={{0,4},{2,6},{4,0},{6,2},{1,5},{3,7},{5,1},{7,3},{8,12},{10,14},{12... | collective-permute-start | bytes 196616 | tf_op jit(solution)/shard_map/ppermute | solution.py:546
  101.6 0.9 collective-permute-start.14
  102.5 0.8 collective-permute-done.12
  103.4 1.5 %collective-permute-done.13 = f32[128,128]{1,0:T(8,128)S(1)} collective-permute-done((f32[128,128]{1,0:T(8,128)S(1)}, f32[128,128]{1,0:T(8,128)S(1)}, u32[]{:S(2)}, u32[]{:S(2)}) %collective-permute-start.13) | collective-permute-done | bytes 65568 | tf_op jit(solution)/shard_map/ppermute | solution.py:546
  104.9 0.9 collective-permute-done.14
  105.7 0.6 add_add_fusion
  106.4 5.4 %all-to-all-done.2 = bf16[32,64,256]{2,1,0:T(8,128)(2,1)S(1)} async-done(((bf16[32,64,256]{2,1,0:T(8,128)(2,1)}), bf16[32,64,256]{2,1,0:T(8,128)(2,1)S(1)}, u32[]{:S(2)}, u32[]{:S(2)}) %all-to-all-start.2) | async-done | bytes 1048608 | tf_op jit(solution)/shard_map/all_to_all | solution.py:381
  111.8 8.0 %all-to-all-start.3 = ((f32[32,4,128]{2,1,0:T(4,128)}), f32[32,4,128]{2,1,0:T(4,128)S(1)}, u32[]{:S(2)}, u32[]{:S(2)}) async-start(f32[32,4,128]{2,1,0:T(4,128)} %bitcast.27), calls=%async_computation.3 | async-start | bytes 131072 | tf_op jit(solution)/shard_map/all_to_all | solution.py:554
  119.8 2.0 %collect.1 = bf16[1024,256]{1,0:T(8,128)(2,1)} custom-call(f32[1024,128]{1,0:T(8,128)S(1)} %copy-done.2, bf16[2048,256]{1,0:T(8,128)(2,1)S(1)} %bitcast.45), custom_call_target="tpu_custom_call" | custom-call | flops 1073741824 | bytes 2097152 | tf_op jit(solution)/shard_map/collect/pallas_call | solution.py:518
  121.8 6.9 %all-to-all-done.3 = f32[32,4,128]{2,1,0:T(4,128)S(1)} async-done(((f32[32,4,128]{2,1,0:T(4,128)}), f32[32,4,128]{2,1,0:T(4,128)S(1)}, u32[]{:S(2)}, u32[]{:S(2)}) %all-to-all-start.3) | async-done | bytes 65568 | tf_op jit(solution)/shard_map/all_to_all | solution.py:554
  128.8 17.7 %all_to_all.25 = bf16[128,4,128]{2,1,0:T(4,128)(2,1)S(1)} all-to-all(bf16[128,4,128]{2,1,0:T(4,128)(2,1)S(1)} %broadcast_in_dim.24), channel_id=1, replica_groups=mesh['y'=4,'z'=8,'x'=4,'core'=2] {'x','y','z'}, dimensions={0} | all-to-all | bytes 262144 | tf_op jit(solution)/shard_map/all_to_all | solution.py:564
  146.5 3.7 %collective-permute-start.15 = (bf16[512,128]{1,0:T(8,128)(2,1)S(1)}, bf16[512,128]{1,0:T(8,128)(2,1)S(1)}, u32[]{:S(2)}, u32[]{:S(2)}) collective-permute-start(bf16[512,128]{1,0:T(8,128)(2,1)S(1)} %bitcast.51), channel_id=1, source_target_pairs={{0,1},{1,0},{2,3},{3,2},{4,5},{5,4},{6,7},{7,6},{8,9},{9,8},{10,11... | collective-permute-start | bytes 393224 | tf_op jit(solution)/shard_map/ppermute | solution.py:533
  150.1 1.0 collective-permute-done.15
  151.2 0.8 maximum_convert_fusion
  (46 shorter events, 0.3 us)
Async XLA Ops:
  0.6 16.7 %copy-start.6 = (s32[1,1,8]{2,1,0:T(1,128)S(1)}, s32[1,1,8]{2,1,0:T(1,128)}, u32[]{:S(2)}) copy-start(s32[1,1,8]{2,1,0:T(1,128)} %param.17) | copy-start | bytes 100
  0.6 16.7 %copy-start.5 = (s32[1,1,8,64]{3,2,1,0:T(8,128)S(1)}, s32[1,1,8,64]{3,2,1,0:T(8,128)}, u32[]{:S(2)}) copy-start(s32[1,1,8,64]{3,2,1,0:T(8,128)} %param.16) | copy-start | bytes 6148
  5.1 28.9 %copy-start = (bf16[2,1024,256]{2,1,0:T(8,128)(2,1)S(1)}, bf16[2,1024,256]{2,1,0:T(8,128)(2,1)}, u32[]{:S(2)}) copy-start(bf16[2,1024,256]{2,1,0:T(8,128)(2,1)} %history_ref.1) | copy-start | bytes 3145732
  5.1 36.8 %all-to-all-start = ((bf16[32,64,256]{2,1,0:T(8,128)(2,1)}), bf16[32,64,256]{2,1,0:T(8,128)(2,1)S(1)}, u32[]{:S(2)}, u32[]{:S(2)}) async-start(bf16[32,64,256]{2,1,0:T(8,128)(2,1)} %bitcast.50), calls=%async_computation | async-start | bytes 2097152 | tf_op jit(solution)/shard_map/all_to_all | solution.py:381
  17.5 14.6 %collective-permute-start = (s32[2,64]{1,0:T(2,128)S(1)}, s32[2,64]{1,0:T(2,128)S(1)}, u32[]{:S(2)}, u32[]{:S(2)}) collective-permute-start(s32[2,64]{1,0:T(2,128)S(1)} %get-tuple-element.72), channel_id=1, source_target_pairs={{0,2},{2,4},{4,6},{6,0},{1,3},{3,5},{5,7},{7,1},{8,10},{10,12},{12... | collective-permute-start | bytes 1544 | tf_op jit(solution)/shard_map/ppermute | solution.py:439
  18.8 13.4 %collective-permute-start.1 = (s32[2,64]{1,0:T(2,128)S(1)}, s32[2,64]{1,0:T(2,128)S(1)}, u32[]{:S(2)}, u32[]{:S(2)}) collective-permute-start(s32[2,64]{1,0:T(2,128)S(1)} %get-tuple-element.71), channel_id=1, source_target_pairs={{0,4},{2,6},{4,0},{6,2},{1,5},{3,7},{5,1},{7,3},{8,12},{10,14},{12... | collective-permute-start | bytes 1544 | tf_op jit(solution)/shard_map/ppermute | solution.py:439
  21.2 10.9 %collective-permute-start.2 = (s32[2,64]{1,0:T(2,128)S(1)}, s32[2,64]{1,0:T(2,128)S(1)}, u32[]{:S(2)}, u32[]{:S(2)}) collective-permute-start(s32[2,64]{1,0:T(2,128)S(1)} %get-tuple-element.73), channel_id=1, source_target_pairs={{0,6},{2,0},{4,2},{6,4},{1,7},{3,1},{5,3},{7,5},{8,14},{10,8},{12,... | collective-permute-start | bytes 1544 | tf_op jit(solution)/shard_map/ppermute | solution.py:439
  32.2 1.7 %collective-permute-start.3 = (s32[4,64]{1,0:T(4,128)S(1)}, s32[4,64]{1,0:T(4,128)S(1)}, u32[]{:S(2)}, u32[]{:S(2)}) collective-permute-start(s32[4,64]{1,0:T(4,128)S(1)} %bitcast.56), channel_id=1, source_target_pairs={{0,1},{1,0},{2,3},{3,2},{4,5},{5,4},{6,7},{7,6},{8,9},{9,8},{10,11... | collective-permute-start | bytes 3080 | tf_op jit(solution)/shard_map/ppermute | solution.py:533
  34.8 29.3 %copy-start.1 = (bf16[256,256]{1,0:T(8,128)(2,1)}, bf16[256,256]{1,0:T(8,128)(2,1)S(1)}, u32[]{:S(2)}) copy-start(bf16[256,256]{1,0:T(8,128)(2,1)S(1)} %get-tuple-element.41.refs_5_) | copy-start | bytes 393220
  42.0 1.0 copy-start.4
  42.9 34.3 %all-to-all-start.1 = ((bf16[32,64,256]{2,1,0:T(8,128)(2,1)}), bf16[32,64,256]{2,1,0:T(8,128)(2,1)S(1)}, u32[]{:S(2)}, u32[]{:S(2)}) async-start(bf16[32,64,256]{2,1,0:T(8,128)(2,1)} %bitcast.49), calls=%async_computation.1 | async-start | bytes 2097152 | tf_op jit(solution)/shard_map/all_to_all | solution.py:381
  51.5 6.6 %collective-permute-start.6 = (bf16[256,256]{1,0:T(8,128)(2,1)S(1)}, bf16[256,256]{1,0:T(8,128)(2,1)S(1)}, u32[]{:S(2)}, u32[]{:S(2)}) collective-permute-start(bf16[256,256]{1,0:T(8,128)(2,1)S(1)} %get-tuple-element.44), channel_id=1, source_target_pairs={{0,2},{2,4},{4,6},{6,0},{1,3},{3,5},{5,7},{7,1},{8,10},{10,12},{12... | collective-permute-start | bytes 393224 | tf_op jit(solution)/shard_map/ppermute | solution.py:439
  52.8 6.8 %collective-permute-start.4 = (bf16[256,256]{1,0:T(8,128)(2,1)S(1)}, bf16[256,256]{1,0:T(8,128)(2,1)S(1)}, u32[]{:S(2)}, u32[]{:S(2)}) collective-permute-start(bf16[256,256]{1,0:T(8,128)(2,1)S(1)} %get-tuple-element.42), channel_id=1, source_target_pairs={{0,6},{2,0},{4,2},{6,4},{1,7},{3,1},{5,3},{7,5},{8,14},{10,8},{12,... | collective-permute-start | bytes 393224 | tf_op jit(solution)/shard_map/ppermute | solution.py:439
  54.3 7.0 %collective-permute-start.5 = (bf16[256,256]{1,0:T(8,128)(2,1)S(1)}, bf16[256,256]{1,0:T(8,128)(2,1)S(1)}, u32[]{:S(2)}, u32[]{:S(2)}) collective-permute-start(bf16[256,256]{1,0:T(8,128)(2,1)S(1)} %get-tuple-element.43), channel_id=1, source_target_pairs={{0,4},{2,6},{4,0},{6,2},{1,5},{3,7},{5,1},{7,3},{8,12},{10,14},{12... | collective-permute-start | bytes 393224 | tf_op jit(solution)/shard_map/ppermute | solution.py:439
  55.8 7.2 %collective-permute-start.7 = (bf16[256,256]{1,0:T(8,128)(2,1)S(1)}, bf16[256,256]{1,0:T(8,128)(2,1)S(1)}, u32[]{:S(2)}, u32[]{:S(2)}) collective-permute-start(bf16[256,256]{1,0:T(8,128)(2,1)S(1)} %get-tuple-element.41.refs_5_), channel_id=1, source_target_pairs={{0,1},{1,0},{2,3},{3,2},{4,5},{5,4},{6,7},{7,6},{8,9},{9,8},{10,11... | collective-permute-start | bytes 393224 | tf_op jit(solution)/shard_map/ppermute | solution.py:533
  58.1 5.9 %copy-start.7 = (bf16[256,256]{1,0:T(8,128)(2,1)}, bf16[256,256]{1,0:T(8,128)(2,1)S(1)}, u32[]{:S(2)}) copy-start(bf16[256,256]{1,0:T(8,128)(2,1)S(1)} %collective-permute-done.6.refs_8_) | copy-start | bytes 393220
  58.1 4.9 %collective-permute-start.10 = (bf16[256,256]{1,0:T(8,128)(2,1)S(1)}, bf16[256,256]{1,0:T(8,128)(2,1)S(1)}, u32[]{:S(2)}, u32[]{:S(2)}) collective-permute-start(bf16[256,256]{1,0:T(8,128)(2,1)S(1)} %collective-permute-done.6.refs_8_), channel_id=1, source_target_pairs={{0,1},{1,0},{2,3},{3,2},{4,5},{5,4},{6,7},{7,6},{8,9},{9,8},{10,11... | collective-permute-start | bytes 393224 | tf_op jit(solution)/shard_map/ppermute | solution.py:533
  59.6 4.4 %copy-start.8 = (bf16[256,256]{1,0:T(8,128)(2,1)}, bf16[256,256]{1,0:T(8,128)(2,1)S(1)}, u32[]{:S(2)}) copy-start(bf16[256,256]{1,0:T(8,128)(2,1)S(1)} %collective-permute-done.4.refs_6_) | copy-start | bytes 393220
  59.6 3.5 %collective-permute-start.8 = (bf16[256,256]{1,0:T(8,128)(2,1)S(1)}, bf16[256,256]{1,0:T(8,128)(2,1)S(1)}, u32[]{:S(2)}, u32[]{:S(2)}) collective-permute-start(bf16[256,256]{1,0:T(8,128)(2,1)S(1)} %collective-permute-done.4.refs_6_), channel_id=1, source_target_pairs={{0,1},{1,0},{2,3},{3,2},{4,5},{5,4},{6,7},{7,6},{8,9},{9,8},{10,11... | collective-permute-start | bytes 393224 | tf_op jit(solution)/shard_map/ppermute | solution.py:533
  61.3 2.7 %copy-start.9 = (bf16[256,256]{1,0:T(8,128)(2,1)}, bf16[256,256]{1,0:T(8,128)(2,1)S(1)}, u32[]{:S(2)}) copy-start(bf16[256,256]{1,0:T(8,128)(2,1)S(1)} %collective-permute-done.5.refs_7_) | copy-start | bytes 393220
  61.3 2.7 %collective-permute-start.9 = (bf16[256,256]{1,0:T(8,128)(2,1)S(1)}, bf16[256,256]{1,0:T(8,128)(2,1)S(1)}, u32[]{:S(2)}, u32[]{:S(2)}) collective-permute-start(bf16[256,256]{1,0:T(8,128)(2,1)S(1)} %collective-permute-done.5.refs_7_), channel_id=1, source_target_pairs={{0,1},{1,0},{2,3},{3,2},{4,5},{5,4},{6,7},{7,6},{8,9},{9,8},{10,11... | collective-permute-start | bytes 393224 | tf_op jit(solution)/shard_map/ppermute | solution.py:533
  63.1 1.0 copy-start.10
  63.1 1.0 copy-start.11
  63.1 1.0 copy-start.12
  64.0 0.6 copy-start.13
  77.3 9.3 %copy-start.3 = (bf16[32,64,256]{2,1,0:T(8,128)(2,1)}, bf16[32,64,256]{2,1,0:T(8,128)(2,1)S(1)}, u32[]{:S(2)}) copy-start(bf16[32,64,256]{2,1,0:T(8,128)(2,1)S(1)} %all-to-all-done.1) | copy-start | bytes 3145732
  77.3 34.5 %all-to-all-start.2 = ((bf16[32,64,256]{2,1,0:T(8,128)(2,1)}), bf16[32,64,256]{2,1,0:T(8,128)(2,1)S(1)}, u32[]{:S(2)}, u32[]{:S(2)}) async-start(bf16[32,64,256]{2,1,0:T(8,128)(2,1)} %bitcast.48), calls=%async_computation.2 | async-start | bytes 2097152 | tf_op jit(solution)/shard_map/all_to_all | solution.py:381
  86.6 33.2 %copy-start.2 = (f32[1024,128]{1,0:T(8,128)S(1)}, f32[1024,128]{1,0:T(8,128)}, u32[]{:S(2)}) copy-start(f32[1024,128]{1,0:T(8,128)} %get-tuple-element.54.column_ref) | copy-start | bytes 1572868
  95.3 2.1 %collective-permute-start.11 = (f32[512,128]{1,0:T(8,128)}, f32[512,128]{1,0:T(8,128)S(1)}, u32[]{:S(2)}, u32[]{:S(2)}) collective-permute-start(f32[512,128]{1,0:T(8,128)} %get-tuple-element.51), channel_id=1, source_target_pairs={{0,1},{1,0},{2,3},{3,2},{4,5},{5,4},{6,7},{7,6},{8,9},{9,8},{10,11... | collective-permute-start | bytes 786440 | tf_op jit(solution)/shard_map/ppermute | solution.py:533
  98.4 4.9 %collective-permute-start.12 = (f32[128,128]{1,0:T(8,128)S(1)}, f32[128,128]{1,0:T(8,128)S(1)}, u32[]{:S(2)}, u32[]{:S(2)}) collective-permute-start(f32[128,128]{1,0:T(8,128)S(1)} %get-tuple-element.60), channel_id=1, source_target_pairs={{0,2},{2,4},{4,6},{6,0},{1,3},{3,5},{5,7},{7,1},{8,10},{10,12},{12... | collective-permute-start | bytes 196616 | tf_op jit(solution)/shard_map/ppermute | solution.py:546
  99.0 5.9 %collective-permute-start.13 = (f32[128,128]{1,0:T(8,128)S(1)}, f32[128,128]{1,0:T(8,128)S(1)}, u32[]{:S(2)}, u32[]{:S(2)}) collective-permute-start(f32[128,128]{1,0:T(8,128)S(1)} %get-tuple-element.62), channel_id=1, source_target_pairs={{0,4},{2,6},{4,0},{6,2},{1,5},{3,7},{5,1},{7,3},{8,12},{10,14},{12... | collective-permute-start | bytes 196616 | tf_op jit(solution)/shard_map/ppermute | solution.py:546
  101.6 4.1 %collective-permute-start.14 = (f32[128,128]{1,0:T(8,128)S(1)}, f32[128,128]{1,0:T(8,128)S(1)}, u32[]{:S(2)}, u32[]{:S(2)}) collective-permute-start(f32[128,128]{1,0:T(8,128)S(1)} %get-tuple-element.61), channel_id=1, source_target_pairs={{0,6},{2,0},{4,2},{6,4},{1,7},{3,1},{5,3},{7,5},{8,14},{10,8},{12,... | collective-permute-start | bytes 196616 | tf_op jit(solution)/shard_map/ppermute | solution.py:546
  111.8 16.9 %all-to-all-start.3 = ((f32[32,4,128]{2,1,0:T(4,128)}), f32[32,4,128]{2,1,0:T(4,128)S(1)}, u32[]{:S(2)}, u32[]{:S(2)}) async-start(f32[32,4,128]{2,1,0:T(4,128)} %bitcast.27), calls=%async_computation.3 | async-start | bytes 131072 | tf_op jit(solution)/shard_map/all_to_all | solution.py:554
  146.5 4.7 %collective-permute-start.15 = (bf16[512,128]{1,0:T(8,128)(2,1)S(1)}, bf16[512,128]{1,0:T(8,128)(2,1)S(1)}, u32[]{:S(2)}, u32[]{:S(2)}) collective-permute-start(bf16[512,128]{1,0:T(8,128)(2,1)S(1)} %bitcast.51), channel_id=1, source_target_pairs={{0,1},{1,0},{2,3},{3,2},{4,5},{5,4},{6,7},{7,6},{8,9},{9,8},{10,11... | collective-permute-start | bytes 393224 | tf_op jit(solution)/shard_map/ppermute | solution.py:533

commit v4 on v3

--- a/solution.py
+++ b/solution.py
@@ -513,7 +513,7 @@
         cost_estimate=cost(2 * work * (work + 3 * width) * width, 20 * MIB),
         name="backward",
     )(core.reshape(1).astype(jnp.int32), in_hbm(ws_cot), weights, adjacency, mixed, slopes)
-    grads = reduce_rows(kept + swap_cores(given))
+    grads = reduce_rows(reduce_rows(kept + swap_cores(given), "x"), "y")
     grads, returned = lax.optimization_barrier((grads, returned))
     second_out = pl.pallas_call(
         collect_body,
@@ -524,7 +524,7 @@
         cost_estimate=cost(2 * work * rows_here * width, 2 * MIB),
         name="collect",
     )(column, returned)
-    mine = sum_wide(grads, n_wide)
+    mine = jnp.sum(from_all(grads, "z"), axis=0).astype(BF16)
     mine, second_out = lax.optimization_barrier((mine, second_out))
     return (second_out, spread(mine))
 
@@ -533,48 +533,38 @@
     return lax.ppermute(value, "core", [(0, 1), (1, 0)])
 
 
-def reduce_rows(kept):
-    size = lax.axis_size("x")
-    quarter = kept.shape[0] // size
-    x = lax.axis_index("x")
+def reduce_rows(kept, axis):
+    size = lax.axis_size(axis)
+    share = kept.shape[0] // size
+    here = lax.axis_index(axis)
 
     def rows_of(index):
-        return lax.dynamic_slice_in_dim(kept, lax.rem(index, size) * quarter, quarter, axis=0)
-
-    total = rows_of(x)
+        return lax.dynamic_slice_in_dim(kept, lax.rem(index, size) * share, share, axis=0)
+
+    total = rows_of(here)
     for k in range(1, size):
         total = total + lax.ppermute(
-            rows_of(x + k), "x", [(i, (i + k) % size) for i in range(size)]
+            rows_of(here + k), axis, [(i, (i + k) % size) for i in range(size)]
         )
     return total
 
 
-def sum_wide(part, n_wide):
-    rows, lanes = part.shape
-    parts = lax.all_to_all(
-        part.reshape(n_wide, rows // n_wide, lanes), WIDE, split_axis=0, concat_axis=0, tiled=True
-    )
-    return jnp.sum(parts, axis=0, keepdims=True).astype(BF16)
+def from_all(value, axes):
+    value = jnp.broadcast_to(value[None], (lax.axis_size(axes),) + value.shape)
+    return lax.all_to_all(value, axes, split_axis=0, concat_axis=0, tiled=True)
 
 
 def spread(mine):
-    _, some, lanes = mine.shape
-    every = ("x",) + WIDE
-    n_every = lax.axis_size(every)
-    own = lax.all_to_all(
-        jnp.broadcast_to(mine, (n_every, some, lanes)),
-        every,
-        split_axis=0,
-        concat_axis=0,
-        tiled=True,
-    ).reshape(n_every * some, lanes)
+    parts = from_all(mine, ("x", "y"))
+    own = parts.reshape(-1, parts.shape[-1])
     other = swap_cores(own)
     core = lax.axis_index("core")
     both = [jnp.where(core == 0, own, other), jnp.where(core == 0, other, own)]
-    width = math.isqrt(n_every * some * lanes)
+    rows, lanes = own.shape
+    width = math.isqrt(rows * lanes)
     return jnp.stack(
         [
-            jnp.concatenate([one[i : i + width] for i in range(0, n_every * some, width)], axis=1)
+            jnp.concatenate([one[i : i + width] for i in range(0, rows, width)], axis=1)
             for one in both
         ]
     ).astype(F32)

time: 153 us -> 148 us (0.967)
  starting transfers between devices: 63.1 us -> 71.1 us
  blocking collectives: 17.7 us -> 11.2 us
  waiting for transfers between devices: 27.5 us -> 21.8 us
    all_to_all x3, waiting for transfers between devices: 12.6 us -> 5.82 us  [to_owners(): lax.all_to_all(value, WIDE, split_axis=0, concat_axis=0, tiled=True)]
    all_to_all x1, blocking collectives: 17.7 us -> 11.2 us  [from_all(): return lax.all_to_all(value, axes, split_axis=0, concat_axis=0, tiled=True)]
    ppermute x3 -> x6, starting transfers between devices: 4.1 us -> 9.23 us  [reduce_rows(): lax.ppermute(rows_of(here + k), axis, [(i, (i + k) % size) for i in range...]
    ppermute x7, starting transfers between devices: 11.7 us -> 16.4 us  [swap_cores(): return lax.ppermute(value, 'core', [(0, 1), (1, 0)])]
    ppermute x3 -> x6, waiting for transfers between devices: 3.21 us -> 5.25 us  [reduce_rows(): lax.ppermute(rows_of(here + k), axis, [(i, (i + k) % size) for i in range...]
    all_to_all x1, starting transfers between devices: 7.96 us -> 6.29 us  [from_all(): return lax.all_to_all(value, axes, split_axis=0, concat_axis=0, tiled=True)]
  transfers between devices with their start and end apart: 20 -> 23, of which waited for: 11 -> 12; matrix products, arithmetic and copies ran while one was open for 1% -> 1% of each run, Pallas kernels for 22% -> 22%
where the time goes in v4:
time: 148 us; the launch traced here: 147 us
  starting transfers between devices  71.1 us (48%)
  Pallas kernels  36.8 us (25%)
  waiting for transfers between devices  21.8 us (15%)
  blocking collectives  11.2 us (8%)
  local copies, waits for them, and re-layouts  2.57 us (2%)
  other arithmetic  2.02 us (1%)
  between operations  1.66 us (1%)
    all_to_all x3, starting transfers between devices, to_owners(): lax.all_to_all(value, WIDE, split_axis=0, concat_axis=0, tiled=True)  30.1 us
    ppermute x7, starting transfers between devices, swap_cores(): return lax.ppermute(value, 'core', [(0, 1), (1, 0)])  16.4 us
    pallas_call x1, Pallas kernels, local(): pl.pallas_call(lambda *refs: forward_body(size, *refs), out_shape=(pltpu....  12.6 us
    all_to_all x1, blocking collectives, from_all(): return lax.all_to_all(value, axes, split_axis=0, concat_axis=0, tiled=True)  11.2 us
    ppermute x6, starting transfers between devices, reduce_rows(): lax.ppermute(rows_of(here + k), axis, [(i, (i + k) % size) for i in range...  9.23 us
    ppermute x6, starting transfers between devices, shift(): return lax.ppermute(value, 'x', [(i, (i + by) % size) for i in range(size)])  9.19 us
    pallas_call x1, Pallas kernels, local(): pl.pallas_call(backward_body, out_shape=(jax.ShapeDtypeStruct((width * wi...  8.71 us
    pallas_call x1, Pallas kernels, local(): pl.pallas_call(prepare_body, out_shape=(pltpu.HBM((work, work + halo), BF...  8.24 us
  transfers between devices with their start and end apart: 23, of which 12 were waited for; matrix products, arithmetic and copies ran while one was open for 1% of the time, Pallas kernels for 22%

profile of v4, /device:TPU:1, one launch (start us, length us, event | category | flops | bytes accessed | tf_op | source)
XLA Modules:
  0.0 147.2 jit_solution(4809421056852588800)
XLA Ops:
  0.7 4.5 %route.1 = (bf16[2048,256]{1,0:T(8,128)(2,1)}, s32[1,1024]{1,0:T(1,128)}) custom-call(s32[1,1024]{1,0:T(1,128)} %bitcast.59, bf16[1024,256]{1,0:T(8,128)(2,1)} %refs_1_.1), custom_call_target="tpu_custom_call" | custom-call | flops 1073741824 | bytes 2097152 | tf_op jit(solution)/shard_map/route/pallas_call | solution.py:385
  5.1 12.2 %all-to-all-start = ((bf16[32,64,256]{2,1,0:T(8,128)(2,1)}), bf16[32,64,256]{2,1,0:T(8,128)(2,1)S(1)}, u32[]{:S(2)}, u32[]{:S(2)}) async-start(bf16[32,64,256]{2,1,0:T(8,128)(2,1)} %bitcast.47), calls=%async_computation | async-start | bytes 2097152 | tf_op jit(solution)/shard_map/all_to_all | solution.py:381
  17.5 1.3 collective-permute-start
  18.7 2.5 %collective-permute-start.1 = (s32[2,64]{1,0:T(2,128)S(1)}, s32[2,64]{1,0:T(2,128)S(1)}, u32[]{:S(2)}, u32[]{:S(2)}) collective-permute-start(s32[2,64]{1,0:T(2,128)S(1)} %get-tuple-element.74), channel_id=1, source_target_pairs={{0,4},{2,6},{4,0},{6,2},{1,5},{3,7},{5,1},{7,3},{8,12},{10,14},{12... | collective-permute-start | bytes 1544 | tf_op jit(solution)/shard_map/ppermute | solution.py:439
  21.2 1.2 collective-permute-start.2
  23.0 8.2 %prepare.1 = (bf16[2048,2560]{1,0:T(8,128)(2,1)}, bf16[2048,256]{1,0:T(8,128)(2,1)}, f32[1024,128]{1,0:T(8,128)}) custom-call(s32[96]{0:T(128)} %bitcast.60, s32[96]{0:T(128)} %bitcast.61, s32[1]{0:T(128)} %bitcast.41.count_ref, s32[1,1024]{1,0:T(1,128)} %get-tuple-element.30.place_ref, bf16[96,128,128]{2,1,0:T(8,128)(2,1)} %bitcast.58, ...), custom_call_target="tpu_custom_call" | custom-call | flops 1073741824 | bytes 20971520 | tf_op jit(solution)/shard_map/prepare/pallas_call | solution.py:405
  31.3 3.0 %collective-permute-start.3 = (s32[4,64]{1,0:T(4,128)S(1)}, s32[4,64]{1,0:T(4,128)S(1)}, u32[]{:S(2)}, u32[]{:S(2)}) collective-permute-start(s32[4,64]{1,0:T(4,128)S(1)} %bitcast.52), channel_id=1, source_target_pairs={{0,1},{1,0},{2,3},{3,2},{4,5},{5,4},{6,7},{7,6},{8,9},{9,8},{10,11... | collective-permute-start | bytes 3080 | tf_op jit(solution)/shard_map/ppermute | solution.py:533
  34.4 0.8 collective-permute-done.3
  35.3 0.1 broadcast_in_dim.26.ids_ref
  35.4 0.7 pick.1
  36.1 5.8 %all-to-all-done = bf16[32,64,256]{2,1,0:T(8,128)(2,1)S(1)} async-done(((bf16[32,64,256]{2,1,0:T(8,128)(2,1)}), bf16[32,64,256]{2,1,0:T(8,128)(2,1)S(1)}, u32[]{:S(2)}, u32[]{:S(2)}) %all-to-all-start) | async-done | bytes 1048608 | tf_op jit(solution)/shard_map/all_to_all | solution.py:381
  42.0 1.0 copy-done.4
  42.9 8.6 %all-to-all-start.1 = ((bf16[32,64,256]{2,1,0:T(8,128)(2,1)}), bf16[32,64,256]{2,1,0:T(8,128)(2,1)S(1)}, u32[]{:S(2)}, u32[]{:S(2)}) async-start(bf16[32,64,256]{2,1,0:T(8,128)(2,1)} %bitcast.46), calls=%async_computation.1 | async-start | bytes 2097152 | tf_op jit(solution)/shard_map/all_to_all | solution.py:381
  51.5 1.3 collective-permute-start.6
  52.8 1.5 collective-permute-start.4
  54.3 1.5 %collective-permute-start.5 = (bf16[256,256]{1,0:T(8,128)(2,1)S(1)}, bf16[256,256]{1,0:T(8,128)(2,1)S(1)}, u32[]{:S(2)}, u32[]{:S(2)}) collective-permute-start(bf16[256,256]{1,0:T(8,128)(2,1)S(1)} %get-tuple-element.43), channel_id=1, source_target_pairs={{0,4},{2,6},{4,0},{6,2},{1,5},{3,7},{5,1},{7,3},{8,12},{10,14},{12... | collective-permute-start | bytes 393224 | tf_op jit(solution)/shard_map/ppermute | solution.py:439
  55.8 2.3 %collective-permute-start.7 = (bf16[256,256]{1,0:T(8,128)(2,1)S(1)}, bf16[256,256]{1,0:T(8,128)(2,1)S(1)}, u32[]{:S(2)}, u32[]{:S(2)}) collective-permute-start(bf16[256,256]{1,0:T(8,128)(2,1)S(1)} %get-tuple-element.41.refs_5_), channel_id=1, source_target_pairs={{0,1},{1,0},{2,3},{3,2},{4,5},{5,4},{6,7},{7,6},{8,9},{9,8},{10,11... | collective-permute-start | bytes 393224 | tf_op jit(solution)/shard_map/ppermute | solution.py:533
  58.1 1.5 collective-permute-start.10
  59.6 1.0 collective-permute-start.8
  60.6 0.7 collective-permute-done.5.refs_7_
  61.3 1.7 %collective-permute-start.9 = (bf16[256,256]{1,0:T(8,128)(2,1)S(1)}, bf16[256,256]{1,0:T(8,128)(2,1)S(1)}, u32[]{:S(2)}, u32[]{:S(2)}) collective-permute-start(bf16[256,256]{1,0:T(8,128)(2,1)S(1)} %collective-permute-done.5.refs_7_), channel_id=1, source_target_pairs={{0,1},{1,0},{2,3},{3,2},{4,5},{5,4},{6,7},{7,6},{8,9},{9,8},{10,11... | collective-permute-start | bytes 393224 | tf_op jit(solution)/shard_map/ppermute | solution.py:533
  63.1 0.9 collective-permute-done.9.refs_11_
  64.1 0.6 copy-done.13
  64.7 12.6 %forward.1 = (bf16[2048,256]{1,0:T(8,128)(2,1)}, bf16[2,2048,256]{2,1,0:T(8,128)(2,1)}, f32[2,2048,256]{2,1,0:T(8,128)}) custom-call(s32[1]{0:T(128)} %bitcast.1.refs_0_, s32[1]{0:T(128)} %bitcast.refs_1_.core_ref, bf16[2048,256]{1,0:T(8,128)(2,1)} %bitcast.45, bf16[2,256,256]{2,1,0:T(8,128)(2,1)} %w_hbm.1, ...), custom_call_target="tpu_custom_call" | custom-call | flops 5905580032 | bytes 25165824 | tf_op jit(solution)/shard_map/forward/pallas_call | solution.py:461
  77.3 9.3 %all-to-all-start.2 = ((bf16[32,64,256]{2,1,0:T(8,128)(2,1)}), bf16[32,64,256]{2,1,0:T(8,128)(2,1)S(1)}, u32[]{:S(2)}, u32[]{:S(2)}) async-start(bf16[32,64,256]{2,1,0:T(8,128)(2,1)} %bitcast.44), calls=%async_computation.2 | async-start | bytes 2097152 | tf_op jit(solution)/shard_map/all_to_all | solution.py:381
  86.6 8.7 %backward.1 = (f32[512,128]{1,0:T(8,128)}, f32[512,128]{1,0:T(8,128)}) custom-call(s32[1]{0:T(128)} %bitcast.refs_1_.core_ref, bf16[2048,256]{1,0:T(8,128)(2,1)} %bitcast.43, bf16[2,256,256]{2,1,0:T(8,128)(2,1)} %w_hbm.1, bf16[2048,2560]{1,0:T(8,128)(2,1)} %get-tuple-element.40.refs_4_.adj_hbm, bf16[2,2048,256]{2,1,0:T(8,128)(2,1)} %get-tuple-element.48.m_hbm, ...), custom_call_target="tpu_custom_call" | custom-call | flops 2952790016 | bytes 20971520 | tf_op jit(solution)/shard_map/backward/pallas_call | solution.py:498
  95.4 0.7 collective-permute-start.11
  96.1 1.4 collective-permute-done.11
  97.5 1.0 add.67
  98.5 0.6 collective-permute-start.12
  99.1 2.6 %collective-permute-start.13 = (f32[128,128]{1,0:T(8,128)S(1)}, f32[128,128]{1,0:T(8,128)S(1)}, u32[]{:S(2)}, u32[]{:S(2)}) collective-permute-start(f32[128,128]{1,0:T(8,128)S(1)} %get-tuple-element.62), channel_id=1, source_target_pairs={{0,4},{2,6},{4,0},{6,2},{1,5},{3,7},{5,1},{7,3},{8,12},{10,14},{12... | collective-permute-start | bytes 196616 | tf_op jit(solution)/shard_map/ppermute | solution.py:546
  101.7 0.9 collective-permute-start.14
  102.5 0.9 collective-permute-done.12
  103.4 1.5 %collective-permute-done.13 = f32[128,128]{1,0:T(8,128)S(1)} collective-permute-done((f32[128,128]{1,0:T(8,128)S(1)}, f32[128,128]{1,0:T(8,128)S(1)}, u32[]{:S(2)}, u32[]{:S(2)}) %collective-permute-start.13) | collective-permute-done | bytes 65568 | tf_op jit(solution)/shard_map/ppermute | solution.py:546
  104.9 0.9 collective-permute-done.14
  105.8 1.6 %collective-permute-start.15 = (f32[32,128]{1,0:T(8,128)S(1)}, f32[32,128]{1,0:T(8,128)S(1)}, u32[]{:S(2)}, u32[]{:S(2)}) collective-permute-start(f32[32,128]{1,0:T(8,128)S(1)} %get-tuple-element.67), channel_id=1, source_target_pairs={{0,64},{64,128},{128,192},{192,0},{1,65},{65,129},{129,193},{193,1... | collective-permute-start | bytes 49160 | tf_op jit(solution)/shard_map/ppermute | solution.py:546
  107.4 2.4 %collective-permute-start.16 = (f32[32,128]{1,0:T(8,128)S(1)}, f32[32,128]{1,0:T(8,128)S(1)}, u32[]{:S(2)}, u32[]{:S(2)}) collective-permute-start(f32[32,128]{1,0:T(8,128)S(1)} %get-tuple-element.69), channel_id=1, source_target_pairs={{0,128},{64,192},{128,0},{192,64},{1,129},{65,193},{129,1},{193,65... | collective-permute-start | bytes 49160 | tf_op jit(solution)/shard_map/ppermute | solution.py:546
  109.9 1.1 collective-permute-start.17
  111.0 1.1 collective-permute-done.16
  112.1 0.9 collective-permute-done.17
  113.0 0.7 broadcast_in_dim.27
  113.7 6.3 %all-to-all-start.3 = ((f32[8,32,128]{2,1,0:T(8,128)}), f32[8,32,128]{2,1,0:T(8,128)S(1)}, u32[]{:S(2)}, u32[]{:S(2)}) async-start(f32[8,32,128]{2,1,0:T(8,128)} %broadcast_in_dim.27), calls=%async_computation.3 | async-start | bytes 262144 | tf_op jit(solution)/shard_map/all_to_all | solution.py:554
  120.0 2.1 %collect.1 = bf16[1024,256]{1,0:T(8,128)(2,1)} custom-call(f32[1024,128]{1,0:T(8,128)S(1)} %copy-done.2, bf16[2048,256]{1,0:T(8,128)(2,1)S(1)} %bitcast.42), custom_call_target="tpu_custom_call" | custom-call | flops 1073741824 | bytes 2097152 | tf_op jit(solution)/shard_map/collect/pallas_call | solution.py:518
  122.0 5.9 %all-to-all-done.3 = f32[8,32,128]{2,1,0:T(8,128)S(1)} async-done(((f32[8,32,128]{2,1,0:T(8,128)}), f32[8,32,128]{2,1,0:T(8,128)S(1)}, u32[]{:S(2)}, u32[]{:S(2)}) %all-to-all-start.3) | async-done | bytes 131104 | tf_op jit(solution)/shard_map/all_to_all | solution.py:554
  127.9 11.2 %all_to_all.25 = bf16[16,32,128]{2,1,0:T(8,128)(2,1)S(1)} all-to-all(bf16[16,32,128]{2,1,0:T(8,128)(2,1)S(1)} %broadcast_in_dim.28), channel_id=1, replica_groups=mesh['y'=4,'z'=8,'x'=4,'core'=2] {'x','y'}, dimensions={0} | all-to-all | bytes 262144 | tf_op jit(solution)/shard_map/all_to_all | solution.py:554
  139.2 6.1 %collective-permute-start.18 = (bf16[512,128]{1,0:T(8,128)(2,1)S(1)}, bf16[512,128]{1,0:T(8,128)(2,1)S(1)}, u32[]{:S(2)}, u32[]{:S(2)}) collective-permute-start(bf16[512,128]{1,0:T(8,128)(2,1)S(1)} %bitcast.48), channel_id=1, source_target_pairs={{0,1},{1,0},{2,3},{3,2},{4,5},{5,4},{6,7},{7,6},{8,9},{9,8},{10,11... | collective-permute-start | bytes 393224 | tf_op jit(solution)/shard_map/ppermute | solution.py:533
  145.3 1.0 collective-permute-done.18
  146.4 0.8 maximum_convert_fusion
  (55 shorter events, 0.5 us)
Async XLA Ops:
  0.6 16.7 %copy-start.6 = (s32[1,1,8]{2,1,0:T(1,128)S(1)}, s32[1,1,8]{2,1,0:T(1,128)}, u32[]{:S(2)}) copy-start(s32[1,1,8]{2,1,0:T(1,128)} %param.17) | copy-start | bytes 100
  0.6 16.7 %copy-start.5 = (s32[1,1,8,64]{3,2,1,0:T(8,128)S(1)}, s32[1,1,8,64]{3,2,1,0:T(8,128)}, u32[]{:S(2)}) copy-start(s32[1,1,8,64]{3,2,1,0:T(8,128)} %param.16) | copy-start | bytes 6148
  5.1 30.3 %copy-start = (bf16[2,1024,256]{2,1,0:T(8,128)(2,1)S(1)}, bf16[2,1024,256]{2,1,0:T(8,128)(2,1)}, u32[]{:S(2)}) copy-start(bf16[2,1024,256]{2,1,0:T(8,128)(2,1)} %history_ref.1) | copy-start | bytes 3145732
  5.1 36.8 %all-to-all-start = ((bf16[32,64,256]{2,1,0:T(8,128)(2,1)}), bf16[32,64,256]{2,1,0:T(8,128)(2,1)S(1)}, u32[]{:S(2)}, u32[]{:S(2)}) async-start(bf16[32,64,256]{2,1,0:T(8,128)(2,1)} %bitcast.47), calls=%async_computation | async-start | bytes 2097152 | tf_op jit(solution)/shard_map/all_to_all | solution.py:381
  17.5 13.8 %collective-permute-start = (s32[2,64]{1,0:T(2,128)S(1)}, s32[2,64]{1,0:T(2,128)S(1)}, u32[]{:S(2)}, u32[]{:S(2)}) collective-permute-start(s32[2,64]{1,0:T(2,128)S(1)} %get-tuple-element.75), channel_id=1, source_target_pairs={{0,2},{2,4},{4,6},{6,0},{1,3},{3,5},{5,7},{7,1},{8,10},{10,12},{12... | collective-permute-start | bytes 1544 | tf_op jit(solution)/shard_map/ppermute | solution.py:439
  18.7 12.5 %collective-permute-start.1 = (s32[2,64]{1,0:T(2,128)S(1)}, s32[2,64]{1,0:T(2,128)S(1)}, u32[]{:S(2)}, u32[]{:S(2)}) collective-permute-start(s32[2,64]{1,0:T(2,128)S(1)} %get-tuple-element.74), channel_id=1, source_target_pairs={{0,4},{2,6},{4,0},{6,2},{1,5},{3,7},{5,1},{7,3},{8,12},{10,14},{12... | collective-permute-start | bytes 1544 | tf_op jit(solution)/shard_map/ppermute | solution.py:439
  21.2 10.1 %collective-permute-start.2 = (s32[2,64]{1,0:T(2,128)S(1)}, s32[2,64]{1,0:T(2,128)S(1)}, u32[]{:S(2)}, u32[]{:S(2)}) collective-permute-start(s32[2,64]{1,0:T(2,128)S(1)} %get-tuple-element.76), channel_id=1, source_target_pairs={{0,6},{2,0},{4,2},{6,4},{1,7},{3,1},{5,3},{7,5},{8,14},{10,8},{12,... | collective-permute-start | bytes 1544 | tf_op jit(solution)/shard_map/ppermute | solution.py:439
  31.3 3.9 %collective-permute-start.3 = (s32[4,64]{1,0:T(4,128)S(1)}, s32[4,64]{1,0:T(4,128)S(1)}, u32[]{:S(2)}, u32[]{:S(2)}) collective-permute-start(s32[4,64]{1,0:T(4,128)S(1)} %bitcast.52), channel_id=1, source_target_pairs={{0,1},{1,0},{2,3},{3,2},{4,5},{5,4},{6,7},{7,6},{8,9},{9,8},{10,11... | collective-permute-start | bytes 3080 | tf_op jit(solution)/shard_map/ppermute | solution.py:533
  36.1 27.9 %copy-start.1 = (bf16[256,256]{1,0:T(8,128)(2,1)}, bf16[256,256]{1,0:T(8,128)(2,1)S(1)}, u32[]{:S(2)}) copy-start(bf16[256,256]{1,0:T(8,128)(2,1)S(1)} %get-tuple-element.41.refs_5_) | copy-start | bytes 393220
  42.0 1.0 copy-start.4
  42.9 34.4 %all-to-all-start.1 = ((bf16[32,64,256]{2,1,0:T(8,128)(2,1)}), bf16[32,64,256]{2,1,0:T(8,128)(2,1)S(1)}, u32[]{:S(2)}, u32[]{:S(2)}) async-start(bf16[32,64,256]{2,1,0:T(8,128)(2,1)} %bitcast.46), calls=%async_computation.1 | async-start | bytes 2097152 | tf_op jit(solution)/shard_map/all_to_all | solution.py:381
  51.5 6.6 %collective-permute-start.6 = (bf16[256,256]{1,0:T(8,128)(2,1)S(1)}, bf16[256,256]{1,0:T(8,128)(2,1)S(1)}, u32[]{:S(2)}, u32[]{:S(2)}) collective-permute-start(bf16[256,256]{1,0:T(8,128)(2,1)S(1)} %get-tuple-element.44), channel_id=1, source_target_pairs={{0,2},{2,4},{4,6},{6,0},{1,3},{3,5},{5,7},{7,1},{8,10},{10,12},{12... | collective-permute-start | bytes 393224 | tf_op jit(solution)/shard_map/ppermute | solution.py:439
  52.8 6.8 %collective-permute-start.4 = (bf16[256,256]{1,0:T(8,128)(2,1)S(1)}, bf16[256,256]{1,0:T(8,128)(2,1)S(1)}, u32[]{:S(2)}, u32[]{:S(2)}) collective-permute-start(bf16[256,256]{1,0:T(8,128)(2,1)S(1)} %get-tuple-element.42), channel_id=1, source_target_pairs={{0,6},{2,0},{4,2},{6,4},{1,7},{3,1},{5,3},{7,5},{8,14},{10,8},{12,... | collective-permute-start | bytes 393224 | tf_op jit(solution)/shard_map/ppermute | solution.py:439
  54.3 7.0 %collective-permute-start.5 = (bf16[256,256]{1,0:T(8,128)(2,1)S(1)}, bf16[256,256]{1,0:T(8,128)(2,1)S(1)}, u32[]{:S(2)}, u32[]{:S(2)}) collective-permute-start(bf16[256,256]{1,0:T(8,128)(2,1)S(1)} %get-tuple-element.43), channel_id=1, source_target_pairs={{0,4},{2,6},{4,0},{6,2},{1,5},{3,7},{5,1},{7,3},{8,12},{10,14},{12... | collective-permute-start | bytes 393224 | tf_op jit(solution)/shard_map/ppermute | solution.py:439
  55.8 7.2 %collective-permute-start.7 = (bf16[256,256]{1,0:T(8,128)(2,1)S(1)}, bf16[256,256]{1,0:T(8,128)(2,1)S(1)}, u32[]{:S(2)}, u32[]{:S(2)}) collective-permute-start(bf16[256,256]{1,0:T(8,128)(2,1)S(1)} %get-tuple-element.41.refs_5_), channel_id=1, source_target_pairs={{0,1},{1,0},{2,3},{3,2},{4,5},{5,4},{6,7},{7,6},{8,9},{9,8},{10,11... | collective-permute-start | bytes 393224 | tf_op jit(solution)/shard_map/ppermute | solution.py:533
  58.1 5.9 %copy-start.7 = (bf16[256,256]{1,0:T(8,128)(2,1)}, bf16[256,256]{1,0:T(8,128)(2,1)S(1)}, u32[]{:S(2)}) copy-start(bf16[256,256]{1,0:T(8,128)(2,1)S(1)} %collective-permute-done.6.refs_8_) | copy-start | bytes 393220
  58.1 4.9 %collective-permute-start.10 = (bf16[256,256]{1,0:T(8,128)(2,1)S(1)}, bf16[256,256]{1,0:T(8,128)(2,1)S(1)}, u32[]{:S(2)}, u32[]{:S(2)}) collective-permute-start(bf16[256,256]{1,0:T(8,128)(2,1)S(1)} %collective-permute-done.6.refs_8_), channel_id=1, source_target_pairs={{0,1},{1,0},{2,3},{3,2},{4,5},{5,4},{6,7},{7,6},{8,9},{9,8},{10,11... | collective-permute-start | bytes 393224 | tf_op jit(solution)/shard_map/ppermute | solution.py:533
  59.6 4.4 %copy-start.8 = (bf16[256,256]{1,0:T(8,128)(2,1)}, bf16[256,256]{1,0:T(8,128)(2,1)S(1)}, u32[]{:S(2)}) copy-start(bf16[256,256]{1,0:T(8,128)(2,1)S(1)} %collective-permute-done.4.refs_6_) | copy-start | bytes 393220
  59.6 3.5 %collective-permute-start.8 = (bf16[256,256]{1,0:T(8,128)(2,1)S(1)}, bf16[256,256]{1,0:T(8,128)(2,1)S(1)}, u32[]{:S(2)}, u32[]{:S(2)}) collective-permute-start(bf16[256,256]{1,0:T(8,128)(2,1)S(1)} %collective-permute-done.4.refs_6_), channel_id=1, source_target_pairs={{0,1},{1,0},{2,3},{3,2},{4,5},{5,4},{6,7},{7,6},{8,9},{9,8},{10,11... | collective-permute-start | bytes 393224 | tf_op jit(solution)/shard_map/ppermute | solution.py:533
  61.3 2.7 %copy-start.9 = (bf16[256,256]{1,0:T(8,128)(2,1)}, bf16[256,256]{1,0:T(8,128)(2,1)S(1)}, u32[]{:S(2)}) copy-start(bf16[256,256]{1,0:T(8,128)(2,1)S(1)} %collective-permute-done.5.refs_7_) | copy-start | bytes 393220
  61.3 2.7 %collective-permute-start.9 = (bf16[256,256]{1,0:T(8,128)(2,1)S(1)}, bf16[256,256]{1,0:T(8,128)(2,1)S(1)}, u32[]{:S(2)}, u32[]{:S(2)}) collective-permute-start(bf16[256,256]{1,0:T(8,128)(2,1)S(1)} %collective-permute-done.5.refs_7_), channel_id=1, source_target_pairs={{0,1},{1,0},{2,3},{3,2},{4,5},{5,4},{6,7},{7,6},{8,9},{9,8},{10,11... | collective-permute-start | bytes 393224 | tf_op jit(solution)/shard_map/ppermute | solution.py:533
  63.0 1.0 copy-start.10
  63.0 1.0 copy-start.11
  63.1 1.0 copy-start.12
  64.0 0.6 copy-start.13
  77.3 9.3 %copy-start.3 = (bf16[32,64,256]{2,1,0:T(8,128)(2,1)}, bf16[32,64,256]{2,1,0:T(8,128)(2,1)S(1)}, u32[]{:S(2)}) copy-start(bf16[32,64,256]{2,1,0:T(8,128)(2,1)S(1)} %all-to-all-done.1) | copy-start | bytes 3145732
  77.3 35.7 %all-to-all-start.2 = ((bf16[32,64,256]{2,1,0:T(8,128)(2,1)}), bf16[32,64,256]{2,1,0:T(8,128)(2,1)S(1)}, u32[]{:S(2)}, u32[]{:S(2)}) async-start(bf16[32,64,256]{2,1,0:T(8,128)(2,1)} %bitcast.44), calls=%async_computation.2 | async-start | bytes 2097152 | tf_op jit(solution)/shard_map/all_to_all | solution.py:381
  86.6 33.3 %copy-start.2 = (f32[1024,128]{1,0:T(8,128)S(1)}, f32[1024,128]{1,0:T(8,128)}, u32[]{:S(2)}) copy-start(f32[1024,128]{1,0:T(8,128)} %get-tuple-element.54.column_ref) | copy-start | bytes 1572868
  95.4 2.1 %collective-permute-start.11 = (f32[512,128]{1,0:T(8,128)}, f32[512,128]{1,0:T(8,128)S(1)}, u32[]{:S(2)}, u32[]{:S(2)}) collective-permute-start(f32[512,128]{1,0:T(8,128)} %get-tuple-element.51), channel_id=1, source_target_pairs={{0,1},{1,0},{2,3},{3,2},{4,5},{5,4},{6,7},{7,6},{8,9},{9,8},{10,11... | collective-permute-start | bytes 786440 | tf_op jit(solution)/shard_map/ppermute | solution.py:533
  98.5 4.9 %collective-permute-start.12 = (f32[128,128]{1,0:T(8,128)S(1)}, f32[128,128]{1,0:T(8,128)S(1)}, u32[]{:S(2)}, u32[]{:S(2)}) collective-permute-start(f32[128,128]{1,0:T(8,128)S(1)} %get-tuple-element.60), channel_id=1, source_target_pairs={{0,2},{2,4},{4,6},{6,0},{1,3},{3,5},{5,7},{7,1},{8,10},{10,12},{12... | collective-permute-start | bytes 196616 | tf_op jit(solution)/shard_map/ppermute | solution.py:546
  99.1 5.9 %collective-permute-start.13 = (f32[128,128]{1,0:T(8,128)S(1)}, f32[128,128]{1,0:T(8,128)S(1)}, u32[]{:S(2)}, u32[]{:S(2)}) collective-permute-start(f32[128,128]{1,0:T(8,128)S(1)} %get-tuple-element.62), channel_id=1, source_target_pairs={{0,4},{2,6},{4,0},{6,2},{1,5},{3,7},{5,1},{7,3},{8,12},{10,14},{12... | collective-permute-start | bytes 196616 | tf_op jit(solution)/shard_map/ppermute | solution.py:546
  101.7 4.1 %collective-permute-start.14 = (f32[128,128]{1,0:T(8,128)S(1)}, f32[128,128]{1,0:T(8,128)S(1)}, u32[]{:S(2)}, u32[]{:S(2)}) collective-permute-start(f32[128,128]{1,0:T(8,128)S(1)} %get-tuple-element.61), channel_id=1, source_target_pairs={{0,6},{2,0},{4,2},{6,4},{1,7},{3,1},{5,3},{7,5},{8,14},{10,8},{12,... | collective-permute-start | bytes 196616 | tf_op jit(solution)/shard_map/ppermute | solution.py:546
  105.8 5.2 %collective-permute-start.15 = (f32[32,128]{1,0:T(8,128)S(1)}, f32[32,128]{1,0:T(8,128)S(1)}, u32[]{:S(2)}, u32[]{:S(2)}) collective-permute-start(f32[32,128]{1,0:T(8,128)S(1)} %get-tuple-element.67), channel_id=1, source_target_pairs={{0,64},{64,128},{128,192},{192,0},{1,65},{65,129},{129,193},{193,1... | collective-permute-start | bytes 49160 | tf_op jit(solution)/shard_map/ppermute | solution.py:546
  107.4 4.7 %collective-permute-start.16 = (f32[32,128]{1,0:T(8,128)S(1)}, f32[32,128]{1,0:T(8,128)S(1)}, u32[]{:S(2)}, u32[]{:S(2)}) collective-permute-start(f32[32,128]{1,0:T(8,128)S(1)} %get-tuple-element.69), channel_id=1, source_target_pairs={{0,128},{64,192},{128,0},{192,64},{1,129},{65,193},{129,1},{193,65... | collective-permute-start | bytes 49160 | tf_op jit(solution)/shard_map/ppermute | solution.py:546
  109.9 3.1 %collective-permute-start.17 = (f32[32,128]{1,0:T(8,128)S(1)}, f32[32,128]{1,0:T(8,128)S(1)}, u32[]{:S(2)}, u32[]{:S(2)}) collective-permute-start(f32[32,128]{1,0:T(8,128)S(1)} %get-tuple-element.68), channel_id=1, source_target_pairs={{0,192},{64,0},{128,64},{192,128},{1,193},{65,1},{129,65},{193,129... | collective-permute-start | bytes 49160 | tf_op jit(solution)/shard_map/ppermute | solution.py:546
  113.7 14.2 %all-to-all-start.3 = ((f32[8,32,128]{2,1,0:T(8,128)}), f32[8,32,128]{2,1,0:T(8,128)S(1)}, u32[]{:S(2)}, u32[]{:S(2)}) async-start(f32[8,32,128]{2,1,0:T(8,128)} %broadcast_in_dim.27), calls=%async_computation.3 | async-start | bytes 262144 | tf_op jit(solution)/shard_map/all_to_all | solution.py:554
  139.2 7.1 %collective-permute-start.18 = (bf16[512,128]{1,0:T(8,128)(2,1)S(1)}, bf16[512,128]{1,0:T(8,128)(2,1)S(1)}, u32[]{:S(2)}, u32[]{:S(2)}) collective-permute-start(bf16[512,128]{1,0:T(8,128)(2,1)S(1)} %bitcast.48), channel_id=1, source_target_pairs={{0,1},{1,0},{2,3},{3,2},{4,5},{5,4},{6,7},{7,6},{8,9},{9,8},{10,11... | collective-permute-start | bytes 393224 | tf_op jit(solution)/shard_map/ppermute | solution.py:533

commit v5 on v4

--- a/solution.py
+++ b/solution.py
@@ -55,12 +55,15 @@
     return (slots == place).astype(F32)
 
 
-def route_body(n_wide, own_ref, x_hbm, send_hbm, place_ref, x_all, send, load_sem, send_sem):
-    load = pltpu.make_async_copy(x_hbm, x_all, load_sem)
+def route_body(n_wide, own_hbm, x_hbm, send_hbm, place_hbm, own_all, place_all, x_all, send, load_sem, send_sem):
+    first = pltpu.make_async_copy(own_hbm, own_all, load_sem.at[0])
+    first.start()
+    load = pltpu.make_async_copy(x_hbm, x_all, load_sem.at[1])
     load.start()
-    rows_here = own_ref.shape[1]
+    rows_here = own_all.shape[1]
     blocks = rows_here // 128
-    own = own_ref[...]
+    first.wait()
+    own = own_all[...]
     hot = (own == lax.broadcasted_iota(jnp.int32, (n_wide, rows_here), 0)).astype(F32)
     hot_b = hot.astype(BF16)
     lower = lax.broadcasted_iota(jnp.int32, (128, 128), 0)
@@ -75,14 +78,15 @@
         ranks.append(jnp.sum(seen * hot[:, part], axis=0, keepdims=True))
         before = before + jnp.sum(hot[:, part], axis=1, keepdims=True)
     rank = jnp.concatenate(ranks, axis=1)
-    place_ref[...] = own * CAP + rank.astype(jnp.int32)
+    place_all[...] = own * CAP + rank.astype(jnp.int32)
+    stores = [pltpu.make_async_copy(place_all, place_hbm, load_sem.at[2])]
+    stores[0].start()
     by_rank = (rank == lax.broadcasted_iota(jnp.int32, (CAP, rows_here), 0).astype(F32)).astype(F32)
     by_rank = by_rank.astype(BF16)
     slot = lax.broadcasted_iota(jnp.int32, (CAP, 1), 0).astype(F32)
     load.wait()
     peers = 8
     step = peers * CAP
-    stores = []
     for c in range(n_wide // peers):
         part = pl.ds(c * step, step)
         group = range(c * peers, (c + 1) * peers)
@@ -97,15 +101,11 @@
 
 
 def prepare_body(
-    rows_ref, cols_ref, count_ref, place_ref, vals_hbm, cot_hbm, adj_hbm, send_hbm, column_ref,
-    adj, vals, cot, send, head, following, row_head, row_next, load_sem, adj_sem, send_sem,
+    rows_ref, cols_ref, count_ref, place_ref, vals, cot_hbm, adj_hbm, send_hbm, column_ref,
+    adj, cot, send, head, following, row_head, row_next, load_sem, adj_sem, send_sem,
 ):
-    loads = (
-        pltpu.make_async_copy(vals_hbm, vals, load_sem.at[0]),
-        pltpu.make_async_copy(cot_hbm, cot, load_sem.at[1]),
-    )
-    for load in loads:
-        load.start()
+    load = pltpu.make_async_copy(cot_hbm, cot, load_sem)
+    load.start()
     count = count_ref[0]
     n_rows, wide = adj.shape[0] // TILE, adj.shape[1] // TILE
     for r in range(n_rows):
@@ -128,7 +128,6 @@
         return carry
 
     lax.fori_loop(0, count, chain, 0)
-    loads[0].wait()
 
     def row_copy(r):
         part = pl.ds(pl.multiple_of(r * TILE, TILE), TILE)
@@ -159,7 +158,7 @@
         return carry
 
     lax.fori_loop(0, n_rows, fill, 0)
-    loads[1].wait()
+    load.wait()
     place = place_ref[...]
     step = 512
     stores = []
@@ -386,14 +385,16 @@
         lambda *refs: route_body(n_wide, *refs),
         out_shape=(
             pltpu.HBM((work, width), BF16),
-            jax.ShapeDtypeStruct((1, rows_here), jnp.int32),
+            pltpu.HBM((1, rows_here), jnp.int32),
         ),
-        in_specs=vmem(1) + [anywhere],
-        out_specs=(anywhere, vmem(1)[0]),
+        in_specs=[anywhere] * 2,
+        out_specs=(anywhere,) * 2,
         scratch_shapes=[
+            pltpu.VMEM((1, rows_here), jnp.int32),
+            pltpu.VMEM((1, rows_here), jnp.int32),
             pltpu.VMEM((rows_here, width), BF16),
             pltpu.VMEM((work, width), BF16),
-            pltpu.SemaphoreType.DMA,
+            pltpu.SemaphoreType.DMA((3,)),
             pltpu.SemaphoreType.DMA((work // 512,)),
         ],
         compiler_params=params(56),
@@ -409,22 +410,21 @@
             pltpu.HBM((work, width), BF16),
             pltpu.HBM((rows_here, 128), F32),
         ),
-        in_specs=smem(3) + vmem(1) + [anywhere] * 2,
+        in_specs=smem(3) + vmem(2) + [anywhere],
         out_specs=(anywhere, anywhere, vmem(1)[0]),
         scratch_shapes=[
             pltpu.VMEM((work, work + halo), BF16),
-            pltpu.VMEM((slots, TILE, TILE), BF16),
             pltpu.VMEM((rows_here, width), BF16),
             pltpu.VMEM((work, width), BF16),
             pltpu.SMEM(((work // TILE) * ((work + halo) // TILE),), jnp.int32),
             pltpu.SMEM((slots,), jnp.int32),
             pltpu.SMEM((work // TILE,), jnp.int32),
             pltpu.SMEM((slots,), jnp.int32),
-            pltpu.SemaphoreType.DMA((2,)),
+            pltpu.SemaphoreType.DMA,
             pltpu.SemaphoreType.DMA((work // TILE,)),
             pltpu.SemaphoreType.DMA((work // 512,)),
         ],
-        compiler_params=params(56),
+        compiler_params=params(40),
         cost_estimate=cost(2 * work * rows_here * width, 20 * MIB),
         name="prepare",
     )(tile_rows[0, 0], tile_cols[0, 0], tile_count[0], place, tile_vals[0, 0], cotangent)

time: 148 us -> 146 us (0.986)
  Pallas kernels: 36.8 us -> 34 us
  local copies, waits for them, and re-layouts: 2.57 us -> 4.58 us
    unnamed x28 -> x36, local copies, waits for them, and re-layouts: 1.62 us -> 3.62 us
    pallas_call x1, Pallas kernels: 8.24 us -> 6.57 us  [local(): pl.pallas_call(prepare_body, out_shape=(pltpu.HBM((work, work + halo), BF...]
  transfers between devices with their start and end apart: 23 -> 23, of which waited for: 12 -> 12; matrix products, arithmetic and copies ran while one was open for 1% -> 1% of each run, Pallas kernels for 22% -> 21%
where the time goes in v5:
time: 146 us; the launch traced here: 145 us
  starting transfers between devices  70 us (48%)
  Pallas kernels  34 us (23%)
  waiting for transfers between devices  21.6 us (15%)
  blocking collectives  11.2 us (8%)
  local copies, waits for them, and re-layouts  4.58 us (3%)
  other arithmetic  2.02 us (1%)
  between operations  1.71 us (1%)
    all_to_all x3, starting transfers between devices, to_owners(): lax.all_to_all(value, WIDE, split_axis=0, concat_axis=0, tiled=True)  30.1 us
    ppermute x7, starting transfers between devices, swap_cores(): return lax.ppermute(value, 'core', [(0, 1), (1, 0)])  15.3 us
    pallas_call x1, Pallas kernels, local(): pl.pallas_call(lambda *refs: forward_body(size, *refs), out_shape=(pltpu....  12.6 us
    all_to_all x1, blocking collectives, from_all(): return lax.all_to_all(value, axes, split_axis=0, concat_axis=0, tiled=True)  11.2 us
    ppermute x6, starting transfers between devices, reduce_rows(): lax.ppermute(rows_of(here + k), axis, [(i, (i + k) % size) for i in range...  9.21 us
    ppermute x6, starting transfers between devices, shift(): return lax.ppermute(value, 'x', [(i, (i + by) % size) for i in range(size)])  9.18 us
    pallas_call x1, Pallas kernels, local(): pl.pallas_call(backward_body, out_shape=(jax.ShapeDtypeStruct((width * wi...  8.69 us
    pallas_call x1, Pallas kernels, local(): pl.pallas_call(prepare_body, out_shape=(pltpu.HBM((work, work + halo), BF...  6.57 us
  transfers between devices with their start and end apart: 23, of which 12 were waited for; matrix products, arithmetic and copies ran while one was open for 1% of the time, Pallas kernels for 21%

profile of v5, /device:TPU:1, one launch (start us, length us, event | category | flops | bytes accessed | tf_op | source)
XLA Modules:
  0.0 145.1 jit_solution(3179087029748743164)
XLA Ops:
  0.7 3.4 %route.1 = (bf16[2048,256]{1,0:T(8,128)(2,1)}, s32[1,1024]{1,0:T(1,128)}) custom-call(s32[1,1024]{1,0:T(1,128)} %bitcast.60, bf16[1024,256]{1,0:T(8,128)(2,1)} %refs_1_.1), custom_call_target="tpu_custom_call" | custom-call | flops 1073741824 | bytes 2097152 | tf_op jit(solution)/shard_map/route/pallas_call | solution.py:384
  4.1 12.2 %all-to-all-start = ((bf16[32,64,256]{2,1,0:T(8,128)(2,1)}), bf16[32,64,256]{2,1,0:T(8,128)(2,1)}, u32[]{:S(2)}, u32[]{:S(2)}) async-start(bf16[32,64,256]{2,1,0:T(8,128)(2,1)} %bitcast.49), calls=%async_computation | async-start | bytes 2097152 | tf_op jit(solution)/shard_map/all_to_all | solution.py:380
  16.4 1.3 collective-permute-start
  17.7 2.4 %collective-permute-start.1 = (s32[2,64]{1,0:T(2,128)S(1)}, s32[2,64]{1,0:T(2,128)S(1)}, u32[]{:S(2)}, u32[]{:S(2)}) collective-permute-start(s32[2,64]{1,0:T(2,128)S(1)} %get-tuple-element.74), channel_id=1, source_target_pairs={{0,4},{2,6},{4,0},{6,2},{1,5},{3,7},{5,1},{7,3},{8,12},{10,14},{12... | collective-permute-start | bytes 1544 | tf_op jit(solution)/shard_map/ppermute | solution.py:439
  20.1 1.2 collective-permute-start.2
  22.0 1.0 copy-done.2
  23.0 0.7 copy-done.7
  23.7 6.6 %prepare.1 = (bf16[2048,2560]{1,0:T(8,128)(2,1)}, bf16[2048,256]{1,0:T(8,128)(2,1)}, f32[1024,128]{1,0:T(8,128)}) custom-call(s32[96]{0:T(128)S(1)} %bitcast.44, s32[96]{0:T(128)S(1)} %bitcast.45, s32[1]{0:T(128)} %bitcast.41.count_ref, s32[1,1024]{1,0:T(1,128)S(1)} %copy-done.7, bf16[96,128,128]{2,1,0:T(8,128)(2,1)S(1)} %bitcast.43, ...), custom_call_target="tpu_custom_call" | custom-call | flops 1073741824 | bytes 20971520 | tf_op jit(solution)/shard_map/prepare/pallas_call | solution.py:406
  30.3 1.9 %collective-permute-start.3 = (s32[4,64]{1,0:T(4,128)S(1)}, s32[4,64]{1,0:T(4,128)S(1)}, u32[]{:S(2)}, u32[]{:S(2)}) collective-permute-start(s32[4,64]{1,0:T(4,128)S(1)} %bitcast.54), channel_id=1, source_target_pairs={{0,1},{1,0},{2,3},{3,2},{4,5},{5,4},{6,7},{7,6},{8,9},{9,8},{10,11... | collective-permute-start | bytes 3080 | tf_op jit(solution)/shard_map/ppermute | solution.py:533
  32.2 0.8 collective-permute-done.3
  33.3 1.2 copy-done.1
  34.5 0.7 pick.1
  35.2 5.6 %all-to-all-done = bf16[32,64,256]{2,1,0:T(8,128)(2,1)} async-done(((bf16[32,64,256]{2,1,0:T(8,128)(2,1)}), bf16[32,64,256]{2,1,0:T(8,128)(2,1)}, u32[]{:S(2)}, u32[]{:S(2)}) %all-to-all-start) | async-done | bytes 1048608 | tf_op jit(solution)/shard_map/all_to_all | solution.py:380
  40.8 8.6 %all-to-all-start.1 = ((bf16[32,64,256]{2,1,0:T(8,128)(2,1)}), bf16[32,64,256]{2,1,0:T(8,128)(2,1)S(1)}, u32[]{:S(2)}, u32[]{:S(2)}) async-start(bf16[32,64,256]{2,1,0:T(8,128)(2,1)} %bitcast.48), calls=%async_computation.1 | async-start | bytes 2097152 | tf_op jit(solution)/shard_map/all_to_all | solution.py:380
  49.4 1.3 collective-permute-start.6
  50.7 1.5 %collective-permute-start.4 = (bf16[256,256]{1,0:T(8,128)(2,1)S(1)}, bf16[256,256]{1,0:T(8,128)(2,1)S(1)}, u32[]{:S(2)}, u32[]{:S(2)}) collective-permute-start(bf16[256,256]{1,0:T(8,128)(2,1)S(1)} %get-tuple-element.42), channel_id=1, source_target_pairs={{0,6},{2,0},{4,2},{6,4},{1,7},{3,1},{5,3},{7,5},{8,14},{10,8},{12,... | collective-permute-start | bytes 393224 | tf_op jit(solution)/shard_map/ppermute | solution.py:439
  52.2 1.5 %collective-permute-start.5 = (bf16[256,256]{1,0:T(8,128)(2,1)S(1)}, bf16[256,256]{1,0:T(8,128)(2,1)S(1)}, u32[]{:S(2)}, u32[]{:S(2)}) collective-permute-start(bf16[256,256]{1,0:T(8,128)(2,1)S(1)} %get-tuple-element.43), channel_id=1, source_target_pairs={{0,4},{2,6},{4,0},{6,2},{1,5},{3,7},{5,1},{7,3},{8,12},{10,14},{12... | collective-permute-start | bytes 393224 | tf_op jit(solution)/shard_map/ppermute | solution.py:439
  53.7 2.3 %collective-permute-start.7 = (bf16[256,256]{1,0:T(8,128)(2,1)S(1)}, bf16[256,256]{1,0:T(8,128)(2,1)S(1)}, u32[]{:S(2)}, u32[]{:S(2)}) collective-permute-start(bf16[256,256]{1,0:T(8,128)(2,1)S(1)} %get-tuple-element.41.refs_5_), channel_id=1, source_target_pairs={{0,1},{1,0},{2,3},{3,2},{4,5},{5,4},{6,7},{7,6},{8,9},{9,8},{10,11... | collective-permute-start | bytes 393224 | tf_op jit(solution)/shard_map/ppermute | solution.py:533
  56.0 1.5 %collective-permute-start.10 = (bf16[256,256]{1,0:T(8,128)(2,1)S(1)}, bf16[256,256]{1,0:T(8,128)(2,1)S(1)}, u32[]{:S(2)}, u32[]{:S(2)}) collective-permute-start(bf16[256,256]{1,0:T(8,128)(2,1)S(1)} %collective-permute-done.6.refs_8_), channel_id=1, source_target_pairs={{0,1},{1,0},{2,3},{3,2},{4,5},{5,4},{6,7},{7,6},{8,9},{9,8},{10,11... | collective-permute-start | bytes 393224 | tf_op jit(solution)/shard_map/ppermute | solution.py:533
  57.5 1.0 collective-permute-start.8
  58.5 0.7 collective-permute-done.5.refs_7_
  59.2 1.7 %collective-permute-start.9 = (bf16[256,256]{1,0:T(8,128)(2,1)S(1)}, bf16[256,256]{1,0:T(8,128)(2,1)S(1)}, u32[]{:S(2)}, u32[]{:S(2)}) collective-permute-start(bf16[256,256]{1,0:T(8,128)(2,1)S(1)} %collective-permute-done.5.refs_7_), channel_id=1, source_target_pairs={{0,1},{1,0},{2,3},{3,2},{4,5},{5,4},{6,7},{7,6},{8,9},{9,8},{10,11... | collective-permute-start | bytes 393224 | tf_op jit(solution)/shard_map/ppermute | solution.py:533
  61.0 0.9 collective-permute-done.9.refs_11_
  62.0 0.6 copy-done.17
  62.6 12.6 %forward.1 = (bf16[2048,256]{1,0:T(8,128)(2,1)}, bf16[2,2048,256]{2,1,0:T(8,128)(2,1)}, f32[2,2048,256]{2,1,0:T(8,128)}) custom-call(s32[1]{0:T(128)} %bitcast.1.refs_0_, s32[1]{0:T(128)} %bitcast.refs_1_.core_ref, bf16[2048,256]{1,0:T(8,128)(2,1)} %bitcast.8.refs_2_, bf16[2,256,256]{2,1,0:T(8,128)(2,1)} %w_hbm.1, ...), custom_call_target="tpu_custom_call" | custom-call | flops 5905580032 | bytes 25165824 | tf_op jit(solution)/shard_map/forward/pallas_call | solution.py:461
  75.2 9.3 %all-to-all-start.2 = ((bf16[32,64,256]{2,1,0:T(8,128)(2,1)}), bf16[32,64,256]{2,1,0:T(8,128)(2,1)S(1)}, u32[]{:S(2)}, u32[]{:S(2)}) async-start(bf16[32,64,256]{2,1,0:T(8,128)(2,1)} %bitcast.47), calls=%async_computation.2 | async-start | bytes 2097152 | tf_op jit(solution)/shard_map/all_to_all | solution.py:380
  84.6 8.7 %backward.1 = (f32[512,128]{1,0:T(8,128)}, f32[512,128]{1,0:T(8,128)}) custom-call(s32[1]{0:T(128)} %bitcast.refs_1_.core_ref, bf16[2048,256]{1,0:T(8,128)(2,1)} %bitcast.46, bf16[2,256,256]{2,1,0:T(8,128)(2,1)} %w_hbm.1, bf16[2048,2560]{1,0:T(8,128)(2,1)} %get-tuple-element.40.refs_4_.adj_hbm, bf16[2,2048,256]{2,1,0:T(8,128)(2,1)} %get-tuple-element.48.m_hbm, ...), custom_call_target="tpu_custom_call" | custom-call | flops 2952790016 | bytes 20971520 | tf_op jit(solution)/shard_map/backward/pallas_call | solution.py:498
  93.3 0.7 collective-permute-start.11
  94.0 1.4 collective-permute-done.11
  95.4 1.0 add.67
  96.9 2.6 %collective-permute-start.13 = (f32[128,128]{1,0:T(8,128)S(1)}, f32[128,128]{1,0:T(8,128)S(1)}, u32[]{:S(2)}, u32[]{:S(2)}) collective-permute-start(f32[128,128]{1,0:T(8,128)S(1)} %get-tuple-element.62), channel_id=1, source_target_pairs={{0,4},{2,6},{4,0},{6,2},{1,5},{3,7},{5,1},{7,3},{8,12},{10,14},{12... | collective-permute-start | bytes 196616 | tf_op jit(solution)/shard_map/ppermute | solution.py:546
  99.6 0.9 collective-permute-start.14
  100.4 0.9 collective-permute-done.12
  101.3 1.5 %collective-permute-done.13 = f32[128,128]{1,0:T(8,128)S(1)} collective-permute-done((f32[128,128]{1,0:T(8,128)S(1)}, f32[128,128]{1,0:T(8,128)S(1)}, u32[]{:S(2)}, u32[]{:S(2)}) %collective-permute-start.13) | collective-permute-done | bytes 65568 | tf_op jit(solution)/shard_map/ppermute | solution.py:546
  102.8 0.9 collective-permute-done.14
  103.7 1.6 %collective-permute-start.15 = (f32[32,128]{1,0:T(8,128)S(1)}, f32[32,128]{1,0:T(8,128)S(1)}, u32[]{:S(2)}, u32[]{:S(2)}) collective-permute-start(f32[32,128]{1,0:T(8,128)S(1)} %get-tuple-element.67), channel_id=1, source_target_pairs={{0,64},{64,128},{128,192},{192,0},{1,65},{65,129},{129,193},{193,1... | collective-permute-start | bytes 49160 | tf_op jit(solution)/shard_map/ppermute | solution.py:546
  105.3 2.4 %collective-permute-start.16 = (f32[32,128]{1,0:T(8,128)S(1)}, f32[32,128]{1,0:T(8,128)S(1)}, u32[]{:S(2)}, u32[]{:S(2)}) collective-permute-start(f32[32,128]{1,0:T(8,128)S(1)} %get-tuple-element.69), channel_id=1, source_target_pairs={{0,128},{64,192},{128,0},{192,64},{1,129},{65,193},{129,1},{193,65... | collective-permute-start | bytes 49160 | tf_op jit(solution)/shard_map/ppermute | solution.py:546
  107.7 1.1 collective-permute-start.17
  108.9 1.1 collective-permute-done.16
  110.0 0.9 collective-permute-done.17
  110.9 0.7 broadcast_in_dim.27
  111.6 6.3 %all-to-all-start.3 = ((f32[8,32,128]{2,1,0:T(8,128)}), f32[8,32,128]{2,1,0:T(8,128)S(1)}, u32[]{:S(2)}, u32[]{:S(2)}) async-start(f32[8,32,128]{2,1,0:T(8,128)} %broadcast_in_dim.27), calls=%async_computation.3 | async-start | bytes 262144 | tf_op jit(solution)/shard_map/all_to_all | solution.py:554
  117.9 2.0 %collect.1 = bf16[1024,256]{1,0:T(8,128)(2,1)} custom-call(f32[1024,128]{1,0:T(8,128)S(1)} %copy-done.6, bf16[2048,256]{1,0:T(8,128)(2,1)S(1)} %bitcast.42), custom_call_target="tpu_custom_call" | custom-call | flops 1073741824 | bytes 2097152 | tf_op jit(solution)/shard_map/collect/pallas_call | solution.py:518
  119.9 5.9 %all-to-all-done.3 = f32[8,32,128]{2,1,0:T(8,128)S(1)} async-done(((f32[8,32,128]{2,1,0:T(8,128)}), f32[8,32,128]{2,1,0:T(8,128)S(1)}, u32[]{:S(2)}, u32[]{:S(2)}) %all-to-all-start.3) | async-done | bytes 131104 | tf_op jit(solution)/shard_map/all_to_all | solution.py:554
  125.8 11.2 %all_to_all.25 = bf16[16,32,128]{2,1,0:T(8,128)(2,1)S(1)} all-to-all(bf16[16,32,128]{2,1,0:T(8,128)(2,1)S(1)} %broadcast_in_dim.28), channel_id=1, replica_groups=mesh['y'=4,'z'=8,'x'=4,'core'=2] {'x','y'}, dimensions={0} | all-to-all | bytes 262144 | tf_op jit(solution)/shard_map/all_to_all | solution.py:554
  137.0 6.2 %collective-permute-start.18 = (bf16[512,128]{1,0:T(8,128)(2,1)S(1)}, bf16[512,128]{1,0:T(8,128)(2,1)S(1)}, u32[]{:S(2)}, u32[]{:S(2)}) collective-permute-start(bf16[512,128]{1,0:T(8,128)(2,1)S(1)} %bitcast.50), channel_id=1, source_target_pairs={{0,1},{1,0},{2,3},{3,2},{4,5},{5,4},{6,7},{7,6},{8,9},{9,8},{10,11... | collective-permute-start | bytes 393224 | tf_op jit(solution)/shard_map/ppermute | solution.py:533
  143.2 1.0 collective-permute-done.18
  144.3 0.8 maximum_convert_fusion
  (63 shorter events, 1.2 us)
Async XLA Ops:
  0.6 15.6 %copy-start.10 = (s32[1,1,8]{2,1,0:T(1,128)S(1)}, s32[1,1,8]{2,1,0:T(1,128)}, u32[]{:S(2)}) copy-start(s32[1,1,8]{2,1,0:T(1,128)} %param.17) | copy-start | bytes 100
  0.6 15.6 %copy-start.9 = (s32[1,1,8,64]{3,2,1,0:T(8,128)S(1)}, s32[1,1,8,64]{3,2,1,0:T(8,128)}, u32[]{:S(2)}) copy-start(s32[1,1,8,64]{3,2,1,0:T(8,128)} %param.16) | copy-start | bytes 6148
  0.7 21.3 %copy-start.4 = (s32[1,1,96]{2,1,0:T(1,128)S(1)}, s32[1,1,96]{2,1,0:T(1,128)}, u32[]{:S(2)}) copy-start(s32[1,1,96]{2,1,0:T(1,128)} %param.18) | copy-start | bytes 1156
  0.7 21.3 %copy-start.5 = (s32[1,1,96]{2,1,0:T(1,128)S(1)}, s32[1,1,96]{2,1,0:T(1,128)}, u32[]{:S(2)}) copy-start(s32[1,1,96]{2,1,0:T(1,128)} %param.19) | copy-start | bytes 1156
  0.7 21.3 %copy-start = (bf16[1,1,96,128,128]{4,3,2,1,0:T(8,128)(2,1)S(1)}, bf16[1,1,96,128,128]{4,3,2,1,0:T(8,128)(2,1)}, u32[]{:S(2)}) copy-start(bf16[1,1,96,128,128]{4,3,2,1,0:T(8,128)(2,1)} %param.21) | copy-start | bytes 9437188
  4.1 36.8 %all-to-all-start = ((bf16[32,64,256]{2,1,0:T(8,128)(2,1)}), bf16[32,64,256]{2,1,0:T(8,128)(2,1)}, u32[]{:S(2)}, u32[]{:S(2)}) async-start(bf16[32,64,256]{2,1,0:T(8,128)(2,1)} %bitcast.49), calls=%async_computation | async-start | bytes 2097152 | tf_op jit(solution)/shard_map/all_to_all | solution.py:380
  16.4 13.9 %collective-permute-start = (s32[2,64]{1,0:T(2,128)S(1)}, s32[2,64]{1,0:T(2,128)S(1)}, u32[]{:S(2)}, u32[]{:S(2)}) collective-permute-start(s32[2,64]{1,0:T(2,128)S(1)} %get-tuple-element.75), channel_id=1, source_target_pairs={{0,2},{2,4},{4,6},{6,0},{1,3},{3,5},{5,7},{7,1},{8,10},{10,12},{12... | collective-permute-start | bytes 1544 | tf_op jit(solution)/shard_map/ppermute | solution.py:439
  17.7 12.6 %collective-permute-start.1 = (s32[2,64]{1,0:T(2,128)S(1)}, s32[2,64]{1,0:T(2,128)S(1)}, u32[]{:S(2)}, u32[]{:S(2)}) collective-permute-start(s32[2,64]{1,0:T(2,128)S(1)} %get-tuple-element.74), channel_id=1, source_target_pairs={{0,4},{2,6},{4,0},{6,2},{1,5},{3,7},{5,1},{7,3},{8,12},{10,14},{12... | collective-permute-start | bytes 1544 | tf_op jit(solution)/shard_map/ppermute | solution.py:439
  20.1 10.2 %collective-permute-start.2 = (s32[2,64]{1,0:T(2,128)S(1)}, s32[2,64]{1,0:T(2,128)S(1)}, u32[]{:S(2)}, u32[]{:S(2)}) collective-permute-start(s32[2,64]{1,0:T(2,128)S(1)} %get-tuple-element.76), channel_id=1, source_target_pairs={{0,6},{2,0},{4,2},{6,4},{1,7},{3,1},{5,3},{7,5},{8,14},{10,8},{12,... | collective-permute-start | bytes 1544 | tf_op jit(solution)/shard_map/ppermute | solution.py:439
  21.9 1.0 copy-start.2
  23.0 0.7 copy-start.7
  30.3 2.7 %collective-permute-start.3 = (s32[4,64]{1,0:T(4,128)S(1)}, s32[4,64]{1,0:T(4,128)S(1)}, u32[]{:S(2)}, u32[]{:S(2)}) collective-permute-start(s32[4,64]{1,0:T(4,128)S(1)} %bitcast.54), channel_id=1, source_target_pairs={{0,1},{1,0},{2,3},{3,2},{4,5},{5,4},{6,7},{7,6},{8,9},{9,8},{10,11... | collective-permute-start | bytes 3080 | tf_op jit(solution)/shard_map/ppermute | solution.py:533
  33.3 1.2 copy-start.1
  35.2 26.7 %copy-start.3 = (bf16[256,256]{1,0:T(8,128)(2,1)}, bf16[256,256]{1,0:T(8,128)(2,1)S(1)}, u32[]{:S(2)}) copy-start(bf16[256,256]{1,0:T(8,128)(2,1)S(1)} %get-tuple-element.41.refs_5_) | copy-start | bytes 393220
  40.8 34.4 %all-to-all-start.1 = ((bf16[32,64,256]{2,1,0:T(8,128)(2,1)}), bf16[32,64,256]{2,1,0:T(8,128)(2,1)S(1)}, u32[]{:S(2)}, u32[]{:S(2)}) async-start(bf16[32,64,256]{2,1,0:T(8,128)(2,1)} %bitcast.48), calls=%async_computation.1 | async-start | bytes 2097152 | tf_op jit(solution)/shard_map/all_to_all | solution.py:380
  49.4 6.6 %collective-permute-start.6 = (bf16[256,256]{1,0:T(8,128)(2,1)S(1)}, bf16[256,256]{1,0:T(8,128)(2,1)S(1)}, u32[]{:S(2)}, u32[]{:S(2)}) collective-permute-start(bf16[256,256]{1,0:T(8,128)(2,1)S(1)} %get-tuple-element.44), channel_id=1, source_target_pairs={{0,2},{2,4},{4,6},{6,0},{1,3},{3,5},{5,7},{7,1},{8,10},{10,12},{12... | collective-permute-start | bytes 393224 | tf_op jit(solution)/shard_map/ppermute | solution.py:439
  50.7 6.8 %collective-permute-start.4 = (bf16[256,256]{1,0:T(8,128)(2,1)S(1)}, bf16[256,256]{1,0:T(8,128)(2,1)S(1)}, u32[]{:S(2)}, u32[]{:S(2)}) collective-permute-start(bf16[256,256]{1,0:T(8,128)(2,1)S(1)} %get-tuple-element.42), channel_id=1, source_target_pairs={{0,6},{2,0},{4,2},{6,4},{1,7},{3,1},{5,3},{7,5},{8,14},{10,8},{12,... | collective-permute-start | bytes 393224 | tf_op jit(solution)/shard_map/ppermute | solution.py:439
  52.2 7.0 %collective-permute-start.5 = (bf16[256,256]{1,0:T(8,128)(2,1)S(1)}, bf16[256,256]{1,0:T(8,128)(2,1)S(1)}, u32[]{:S(2)}, u32[]{:S(2)}) collective-permute-start(bf16[256,256]{1,0:T(8,128)(2,1)S(1)} %get-tuple-element.43), channel_id=1, source_target_pairs={{0,4},{2,6},{4,0},{6,2},{1,5},{3,7},{5,1},{7,3},{8,12},{10,14},{12... | collective-permute-start | bytes 393224 | tf_op jit(solution)/shard_map/ppermute | solution.py:439
  53.7 7.2 %collective-permute-start.7 = (bf16[256,256]{1,0:T(8,128)(2,1)S(1)}, bf16[256,256]{1,0:T(8,128)(2,1)S(1)}, u32[]{:S(2)}, u32[]{:S(2)}) collective-permute-start(bf16[256,256]{1,0:T(8,128)(2,1)S(1)} %get-tuple-element.41.refs_5_), channel_id=1, source_target_pairs={{0,1},{1,0},{2,3},{3,2},{4,5},{5,4},{6,7},{7,6},{8,9},{9,8},{10,11... | collective-permute-start | bytes 393224 | tf_op jit(solution)/shard_map/ppermute | solution.py:533
  56.0 5.9 %copy-start.11 = (bf16[256,256]{1,0:T(8,128)(2,1)}, bf16[256,256]{1,0:T(8,128)(2,1)S(1)}, u32[]{:S(2)}) copy-start(bf16[256,256]{1,0:T(8,128)(2,1)S(1)} %collective-permute-done.6.refs_8_) | copy-start | bytes 393220
  56.0 4.9 %collective-permute-start.10 = (bf16[256,256]{1,0:T(8,128)(2,1)S(1)}, bf16[256,256]{1,0:T(8,128)(2,1)S(1)}, u32[]{:S(2)}, u32[]{:S(2)}) collective-permute-start(bf16[256,256]{1,0:T(8,128)(2,1)S(1)} %collective-permute-done.6.refs_8_), channel_id=1, source_target_pairs={{0,1},{1,0},{2,3},{3,2},{4,5},{5,4},{6,7},{7,6},{8,9},{9,8},{10,11... | collective-permute-start | bytes 393224 | tf_op jit(solution)/shard_map/ppermute | solution.py:533
  57.5 4.4 %copy-start.12 = (bf16[256,256]{1,0:T(8,128)(2,1)}, bf16[256,256]{1,0:T(8,128)(2,1)S(1)}, u32[]{:S(2)}) copy-start(bf16[256,256]{1,0:T(8,128)(2,1)S(1)} %collective-permute-done.4.refs_6_) | copy-start | bytes 393220
  57.5 3.5 %collective-permute-start.8 = (bf16[256,256]{1,0:T(8,128)(2,1)S(1)}, bf16[256,256]{1,0:T(8,128)(2,1)S(1)}, u32[]{:S(2)}, u32[]{:S(2)}) collective-permute-start(bf16[256,256]{1,0:T(8,128)(2,1)S(1)} %collective-permute-done.4.refs_6_), channel_id=1, source_target_pairs={{0,1},{1,0},{2,3},{3,2},{4,5},{5,4},{6,7},{7,6},{8,9},{9,8},{10,11... | collective-permute-start | bytes 393224 | tf_op jit(solution)/shard_map/ppermute | solution.py:533
  59.2 2.7 %copy-start.13 = (bf16[256,256]{1,0:T(8,128)(2,1)}, bf16[256,256]{1,0:T(8,128)(2,1)S(1)}, u32[]{:S(2)}) copy-start(bf16[256,256]{1,0:T(8,128)(2,1)S(1)} %collective-permute-done.5.refs_7_) | copy-start | bytes 393220
  59.2 2.7 %collective-permute-start.9 = (bf16[256,256]{1,0:T(8,128)(2,1)S(1)}, bf16[256,256]{1,0:T(8,128)(2,1)S(1)}, u32[]{:S(2)}, u32[]{:S(2)}) collective-permute-start(bf16[256,256]{1,0:T(8,128)(2,1)S(1)} %collective-permute-done.5.refs_7_), channel_id=1, source_target_pairs={{0,1},{1,0},{2,3},{3,2},{4,5},{5,4},{6,7},{7,6},{8,9},{9,8},{10,11... | collective-permute-start | bytes 393224 | tf_op jit(solution)/shard_map/ppermute | solution.py:533
  60.9 1.0 copy-start.14
  61.0 1.0 copy-start.15
  61.0 1.0 copy-start.16
  61.9 0.7 copy-start.17
  75.2 9.3 %copy-start.8 = (bf16[32,64,256]{2,1,0:T(8,128)(2,1)}, bf16[32,64,256]{2,1,0:T(8,128)(2,1)S(1)}, u32[]{:S(2)}) copy-start(bf16[32,64,256]{2,1,0:T(8,128)(2,1)S(1)} %all-to-all-done.1) | copy-start | bytes 3145732
  75.2 35.7 %all-to-all-start.2 = ((bf16[32,64,256]{2,1,0:T(8,128)(2,1)}), bf16[32,64,256]{2,1,0:T(8,128)(2,1)S(1)}, u32[]{:S(2)}, u32[]{:S(2)}) async-start(bf16[32,64,256]{2,1,0:T(8,128)(2,1)} %bitcast.47), calls=%async_computation.2 | async-start | bytes 2097152 | tf_op jit(solution)/shard_map/all_to_all | solution.py:380
  84.5 33.3 %copy-start.6 = (f32[1024,128]{1,0:T(8,128)S(1)}, f32[1024,128]{1,0:T(8,128)}, u32[]{:S(2)}) copy-start(f32[1024,128]{1,0:T(8,128)} %get-tuple-element.54.column_ref) | copy-start | bytes 1572868
  93.3 2.1 %collective-permute-start.11 = (f32[512,128]{1,0:T(8,128)}, f32[512,128]{1,0:T(8,128)S(1)}, u32[]{:S(2)}, u32[]{:S(2)}) collective-permute-start(f32[512,128]{1,0:T(8,128)} %get-tuple-element.51), channel_id=1, source_target_pairs={{0,1},{1,0},{2,3},{3,2},{4,5},{5,4},{6,7},{7,6},{8,9},{9,8},{10,11... | collective-permute-start | bytes 786440 | tf_op jit(solution)/shard_map/ppermute | solution.py:533
  96.4 4.9 %collective-permute-start.12 = (f32[128,128]{1,0:T(8,128)S(1)}, f32[128,128]{1,0:T(8,128)S(1)}, u32[]{:S(2)}, u32[]{:S(2)}) collective-permute-start(f32[128,128]{1,0:T(8,128)S(1)} %get-tuple-element.60), channel_id=1, source_target_pairs={{0,2},{2,4},{4,6},{6,0},{1,3},{3,5},{5,7},{7,1},{8,10},{10,12},{12... | collective-permute-start | bytes 196616 | tf_op jit(solution)/shard_map/ppermute | solution.py:546
  96.9 5.9 %collective-permute-start.13 = (f32[128,128]{1,0:T(8,128)S(1)}, f32[128,128]{1,0:T(8,128)S(1)}, u32[]{:S(2)}, u32[]{:S(2)}) collective-permute-start(f32[128,128]{1,0:T(8,128)S(1)} %get-tuple-element.62), channel_id=1, source_target_pairs={{0,4},{2,6},{4,0},{6,2},{1,5},{3,7},{5,1},{7,3},{8,12},{10,14},{12... | collective-permute-start | bytes 196616 | tf_op jit(solution)/shard_map/ppermute | solution.py:546
  99.6 4.1 %collective-permute-start.14 = (f32[128,128]{1,0:T(8,128)S(1)}, f32[128,128]{1,0:T(8,128)S(1)}, u32[]{:S(2)}, u32[]{:S(2)}) collective-permute-start(f32[128,128]{1,0:T(8,128)S(1)} %get-tuple-element.61), channel_id=1, source_target_pairs={{0,6},{2,0},{4,2},{6,4},{1,7},{3,1},{5,3},{7,5},{8,14},{10,8},{12,... | collective-permute-start | bytes 196616 | tf_op jit(solution)/shard_map/ppermute | solution.py:546
  103.7 5.2 %collective-permute-start.15 = (f32[32,128]{1,0:T(8,128)S(1)}, f32[32,128]{1,0:T(8,128)S(1)}, u32[]{:S(2)}, u32[]{:S(2)}) collective-permute-start(f32[32,128]{1,0:T(8,128)S(1)} %get-tuple-element.67), channel_id=1, source_target_pairs={{0,64},{64,128},{128,192},{192,0},{1,65},{65,129},{129,193},{193,1... | collective-permute-start | bytes 49160 | tf_op jit(solution)/shard_map/ppermute | solution.py:546
  105.3 4.7 %collective-permute-start.16 = (f32[32,128]{1,0:T(8,128)S(1)}, f32[32,128]{1,0:T(8,128)S(1)}, u32[]{:S(2)}, u32[]{:S(2)}) collective-permute-start(f32[32,128]{1,0:T(8,128)S(1)} %get-tuple-element.69), channel_id=1, source_target_pairs={{0,128},{64,192},{128,0},{192,64},{1,129},{65,193},{129,1},{193,65... | collective-permute-start | bytes 49160 | tf_op jit(solution)/shard_map/ppermute | solution.py:546
  107.7 3.2 %collective-permute-start.17 = (f32[32,128]{1,0:T(8,128)S(1)}, f32[32,128]{1,0:T(8,128)S(1)}, u32[]{:S(2)}, u32[]{:S(2)}) collective-permute-start(f32[32,128]{1,0:T(8,128)S(1)} %get-tuple-element.68), channel_id=1, source_target_pairs={{0,192},{64,0},{128,64},{192,128},{1,193},{65,1},{129,65},{193,129... | collective-permute-start | bytes 49160 | tf_op jit(solution)/shard_map/ppermute | solution.py:546
  111.6 14.2 %all-to-all-start.3 = ((f32[8,32,128]{2,1,0:T(8,128)}), f32[8,32,128]{2,1,0:T(8,128)S(1)}, u32[]{:S(2)}, u32[]{:S(2)}) async-start(f32[8,32,128]{2,1,0:T(8,128)} %broadcast_in_dim.27), calls=%async_computation.3 | async-start | bytes 262144 | tf_op jit(solution)/shard_map/all_to_all | solution.py:554
  137.0 7.2 %collective-permute-start.18 = (bf16[512,128]{1,0:T(8,128)(2,1)S(1)}, bf16[512,128]{1,0:T(8,128)(2,1)S(1)}, u32[]{:S(2)}, u32[]{:S(2)}) collective-permute-start(bf16[512,128]{1,0:T(8,128)(2,1)S(1)} %bitcast.50), channel_id=1, source_target_pairs={{0,1},{1,0},{2,3},{3,2},{4,5},{5,4},{6,7},{7,6},{8,9},{9,8},{10,11... | collective-permute-start | bytes 393224 | tf_op jit(solution)/shard_map/ppermute | solution.py:533

commit v6 on v5

--- a/solution.py
+++ b/solution.py
@@ -293,25 +293,26 @@
     step = 512
     blocks = work // step
     parts = [pl.ds(b * step, step) for b in range(blocks)]
-    pairs = [
-        (s_hbm.at[1], s_all.at[1]),
-        (cot_hbm, cot),
-        (m_hbm.at[1], m_all.at[1]),
-        (w_hbm, w),
-    ]
-    pairs += [(adj_hbm.at[:, parts[0]], adj.at[:, parts[0]])]
-    pairs += [(s_hbm.at[0], s_all.at[0]), (m_hbm.at[0], m_all.at[0])]
-    pairs += [(adj_hbm.at[:, part], adj.at[:, part]) for part in parts[1:]]
+    pairs = [(w_hbm.at[1], w.at[1])]
+    for part in parts:
+        pairs.append((s_hbm.at[1, part], s_all.at[1, part]))
+        pairs.append((cot_hbm.at[part], cot.at[part]))
+        pairs.append((m_hbm.at[1, part], m_all.at[1, part]))
+    for part in parts:
+        pairs.append((adj_hbm.at[:, part], adj.at[:, part]))
+        pairs.append((s_hbm.at[0, part], s_all.at[0, part]))
+        pairs.append((m_hbm.at[0, part], m_all.at[0, part]))
     loads = [
         pltpu.make_async_copy(here, there, load_sem.at[i]) for i, (here, there) in enumerate(pairs)
     ]
     for load in loads:
         load.start()
-    for load in loads[:4]:
-        load.wait()
+    loads[0].wait()
     beta = BETAS[1]
     total = jnp.zeros((width, width), F32)
-    for part in parts:
+    for b, part in enumerate(parts):
+        for load in loads[1 + 3 * b : 4 + 3 * b]:
+            load.wait()
         grad_two = cot[part, :].astype(F32) * s_all[1, part, :]
         grad_two_b = grad_two.astype(BF16)
         total = total + dot_rows(m_all[1, part, :], grad_two_b)
@@ -323,7 +324,7 @@
     second = BETAS[1] * total
     total = jnp.zeros((width, width), F32)
     for b, part in enumerate(parts):
-        for load in loads[4:7] if b == 0 else loads[6 + b : 7 + b]:
+        for load in loads[1 + 3 * (blocks + b) : 4 + 3 * (blocks + b)]:
             load.wait()
         back = jnp.transpose(dot(turned[...], adj[:, part]))
         grad_one = (1.0 - ALPHA) * back * s_all[0, part, :]
@@ -507,7 +508,7 @@
             pltpu.VMEM((2, work, width), BF16),
             pltpu.VMEM((2, work, width), F32),
             pltpu.VMEM((width, work), BF16),
-            pltpu.SemaphoreType.DMA((10,)),
+            pltpu.SemaphoreType.DMA((25,)),
         ],
         compiler_params=params(56),
         cost_estimate=cost(2 * work * (work + 3 * width) * width, 20 * MIB),

time: 146 us -> 145 us (level)
  transfers between devices with their start and end apart: 23 -> 23, of which waited for: 12 -> 13; matrix products, arithmetic and copies ran while one was open for 1% -> 1% of each run, Pallas kernels for 21% -> 21%
where the time goes in v6:
time: 145 us
  starting transfers between devices  69.3 us (48%)
  Pallas kernels  34 us (23%)
  waiting for transfers between devices  21.7 us (15%)
  blocking collectives  11.2 us (8%)
  local copies, waits for them, and re-layouts  4.58 us (3%)
  other arithmetic  2.02 us (1%)
  between operations  1.71 us (1%)
    all_to_all x3, starting transfers between devices, to_owners(): lax.all_to_all(value, WIDE, split_axis=0, concat_axis=0, tiled=True)  30.1 us
    ppermute x7, starting transfers between devices, swap_cores(): return lax.ppermute(value, 'core', [(0, 1), (1, 0)])  14.9 us
    pallas_call x1, Pallas kernels, local(): pl.pallas_call(lambda *refs: forward_body(size, *refs), out_shape=(pltpu....  12.6 us
    all_to_all x1, blocking collectives, from_all(): return lax.all_to_all(value, axes, split_axis=0, concat_axis=0, tiled=True)  11.2 us
    ppermute x6, starting transfers between devices, shift(): return lax.ppermute(value, 'x', [(i, (i + by) % size) for i in range(size)])  9.18 us
    ppermute x6, starting transfers between devices, reduce_rows(): lax.ppermute(rows_of(here + k), axis, [(i, (i + k) % size) for i in range...  8.94 us
    pallas_call x1, Pallas kernels, local(): pl.pallas_call(backward_body, out_shape=(jax.ShapeDtypeStruct((width * wi...  8.1 us
    pallas_call x1, Pallas kernels, local(): pl.pallas_call(prepare_body, out_shape=(pltpu.HBM((work, work + halo), BF...  7.18 us
  transfers between devices with their start and end apart: 23, of which 13 were waited for; matrix products, arithmetic and copies ran while one was open for 1% of the time, Pallas kernels for 21%

profile of v6, /device:TPU:1, one launch (start us, length us, event | category | flops | bytes accessed | tf_op | source)
XLA Modules:
  0.0 144.5 jit_solution(10333473471160770492)
XLA Ops:
  0.7 3.4 %route.1 = (bf16[2048,256]{1,0:T(8,128)(2,1)}, s32[1,1024]{1,0:T(1,128)}) custom-call(s32[1,1024]{1,0:T(1,128)} %bitcast.60, bf16[1024,256]{1,0:T(8,128)(2,1)} %refs_1_.1), custom_call_target="tpu_custom_call" | custom-call | flops 1073741824 | bytes 2097152 | tf_op jit(solution)/shard_map/route/pallas_call | solution.py:385
  4.1 12.2 %all-to-all-start = ((bf16[32,64,256]{2,1,0:T(8,128)(2,1)}), bf16[32,64,256]{2,1,0:T(8,128)(2,1)}, u32[]{:S(2)}, u32[]{:S(2)}) async-start(bf16[32,64,256]{2,1,0:T(8,128)(2,1)} %bitcast.49), calls=%async_computation | async-start | bytes 2097152 | tf_op jit(solution)/shard_map/all_to_all | solution.py:381
  16.4 1.3 collective-permute-start
  17.7 2.4 %collective-permute-start.1 = (s32[2,64]{1,0:T(2,128)S(1)}, s32[2,64]{1,0:T(2,128)S(1)}, u32[]{:S(2)}, u32[]{:S(2)}) collective-permute-start(s32[2,64]{1,0:T(2,128)S(1)} %get-tuple-element.74), channel_id=1, source_target_pairs={{0,4},{2,6},{4,0},{6,2},{1,5},{3,7},{5,1},{7,3},{8,12},{10,14},{12... | collective-permute-start | bytes 1544 | tf_op jit(solution)/shard_map/ppermute | solution.py:440
  20.1 1.2 collective-permute-start.2
  22.0 1.0 copy-done.2
  23.0 0.7 copy-done.7
  23.7 7.2 %prepare.1 = (bf16[2048,2560]{1,0:T(8,128)(2,1)}, bf16[2048,256]{1,0:T(8,128)(2,1)}, f32[1024,128]{1,0:T(8,128)}) custom-call(s32[96]{0:T(128)S(1)} %bitcast.44, s32[96]{0:T(128)S(1)} %bitcast.45, s32[1]{0:T(128)} %bitcast.41.count_ref, s32[1,1024]{1,0:T(1,128)S(1)} %copy-done.7, bf16[96,128,128]{2,1,0:T(8,128)(2,1)S(1)} %bitcast.43, ...), custom_call_target="tpu_custom_call" | custom-call | flops 1073741824 | bytes 20971520 | tf_op jit(solution)/shard_map/prepare/pallas_call | solution.py:407
  30.9 1.3 collective-permute-start.3
  32.2 0.8 collective-permute-done.3
  33.3 1.2 copy-done.1
  34.5 0.7 pick.1
  35.2 5.6 %all-to-all-done = bf16[32,64,256]{2,1,0:T(8,128)(2,1)} async-done(((bf16[32,64,256]{2,1,0:T(8,128)(2,1)}), bf16[32,64,256]{2,1,0:T(8,128)(2,1)}, u32[]{:S(2)}, u32[]{:S(2)}) %all-to-all-start) | async-done | bytes 1048608 | tf_op jit(solution)/shard_map/all_to_all | solution.py:381
  40.8 8.6 %all-to-all-start.1 = ((bf16[32,64,256]{2,1,0:T(8,128)(2,1)}), bf16[32,64,256]{2,1,0:T(8,128)(2,1)S(1)}, u32[]{:S(2)}, u32[]{:S(2)}) async-start(bf16[32,64,256]{2,1,0:T(8,128)(2,1)} %bitcast.48), calls=%async_computation.1 | async-start | bytes 2097152 | tf_op jit(solution)/shard_map/all_to_all | solution.py:381
  49.4 1.3 collective-permute-start.6
  50.7 1.5 %collective-permute-start.4 = (bf16[256,256]{1,0:T(8,128)(2,1)S(1)}, bf16[256,256]{1,0:T(8,128)(2,1)S(1)}, u32[]{:S(2)}, u32[]{:S(2)}) collective-permute-start(bf16[256,256]{1,0:T(8,128)(2,1)S(1)} %get-tuple-element.42), channel_id=1, source_target_pairs={{0,6},{2,0},{4,2},{6,4},{1,7},{3,1},{5,3},{7,5},{8,14},{10,8},{12,... | collective-permute-start | bytes 393224 | tf_op jit(solution)/shard_map/ppermute | solution.py:440
  52.2 1.5 %collective-permute-start.5 = (bf16[256,256]{1,0:T(8,128)(2,1)S(1)}, bf16[256,256]{1,0:T(8,128)(2,1)S(1)}, u32[]{:S(2)}, u32[]{:S(2)}) collective-permute-start(bf16[256,256]{1,0:T(8,128)(2,1)S(1)} %get-tuple-element.43), channel_id=1, source_target_pairs={{0,4},{2,6},{4,0},{6,2},{1,5},{3,7},{5,1},{7,3},{8,12},{10,14},{12... | collective-permute-start | bytes 393224 | tf_op jit(solution)/shard_map/ppermute | solution.py:440
  53.7 2.3 %collective-permute-start.7 = (bf16[256,256]{1,0:T(8,128)(2,1)S(1)}, bf16[256,256]{1,0:T(8,128)(2,1)S(1)}, u32[]{:S(2)}, u32[]{:S(2)}) collective-permute-start(bf16[256,256]{1,0:T(8,128)(2,1)S(1)} %get-tuple-element.41.refs_5_), channel_id=1, source_target_pairs={{0,1},{1,0},{2,3},{3,2},{4,5},{5,4},{6,7},{7,6},{8,9},{9,8},{10,11... | collective-permute-start | bytes 393224 | tf_op jit(solution)/shard_map/ppermute | solution.py:534
  56.0 1.5 %collective-permute-start.10 = (bf16[256,256]{1,0:T(8,128)(2,1)S(1)}, bf16[256,256]{1,0:T(8,128)(2,1)S(1)}, u32[]{:S(2)}, u32[]{:S(2)}) collective-permute-start(bf16[256,256]{1,0:T(8,128)(2,1)S(1)} %collective-permute-done.6.refs_8_), channel_id=1, source_target_pairs={{0,1},{1,0},{2,3},{3,2},{4,5},{5,4},{6,7},{7,6},{8,9},{9,8},{10,11... | collective-permute-start | bytes 393224 | tf_op jit(solution)/shard_map/ppermute | solution.py:534
  57.5 1.0 collective-permute-start.8
  58.5 0.7 collective-permute-done.5.refs_7_
  59.2 1.7 %collective-permute-start.9 = (bf16[256,256]{1,0:T(8,128)(2,1)S(1)}, bf16[256,256]{1,0:T(8,128)(2,1)S(1)}, u32[]{:S(2)}, u32[]{:S(2)}) collective-permute-start(bf16[256,256]{1,0:T(8,128)(2,1)S(1)} %collective-permute-done.5.refs_7_), channel_id=1, source_target_pairs={{0,1},{1,0},{2,3},{3,2},{4,5},{5,4},{6,7},{7,6},{8,9},{9,8},{10,11... | collective-permute-start | bytes 393224 | tf_op jit(solution)/shard_map/ppermute | solution.py:534
  61.0 0.9 collective-permute-done.9.refs_11_
  62.0 0.6 copy-done.17
  62.6 12.6 %forward.1 = (bf16[2048,256]{1,0:T(8,128)(2,1)}, bf16[2,2048,256]{2,1,0:T(8,128)(2,1)}, f32[2,2048,256]{2,1,0:T(8,128)}) custom-call(s32[1]{0:T(128)} %bitcast.1.refs_0_, s32[1]{0:T(128)} %bitcast.refs_1_.core_ref, bf16[2048,256]{1,0:T(8,128)(2,1)} %bitcast.8.refs_2_, bf16[2,256,256]{2,1,0:T(8,128)(2,1)} %w_hbm.1, ...), custom_call_target="tpu_custom_call" | custom-call | flops 5905580032 | bytes 25165824 | tf_op jit(solution)/shard_map/forward/pallas_call | solution.py:462
  75.2 9.3 %all-to-all-start.2 = ((bf16[32,64,256]{2,1,0:T(8,128)(2,1)}), bf16[32,64,256]{2,1,0:T(8,128)(2,1)S(1)}, u32[]{:S(2)}, u32[]{:S(2)}) async-start(bf16[32,64,256]{2,1,0:T(8,128)(2,1)} %bitcast.47), calls=%async_computation.2 | async-start | bytes 2097152 | tf_op jit(solution)/shard_map/all_to_all | solution.py:381
  84.6 8.1 %backward.1 = (f32[512,128]{1,0:T(8,128)}, f32[512,128]{1,0:T(8,128)}) custom-call(s32[1]{0:T(128)} %bitcast.refs_1_.core_ref, bf16[2048,256]{1,0:T(8,128)(2,1)} %bitcast.46, bf16[2,256,256]{2,1,0:T(8,128)(2,1)} %w_hbm.1, bf16[2048,2560]{1,0:T(8,128)(2,1)} %get-tuple-element.40.refs_4_.adj_hbm, bf16[2,2048,256]{2,1,0:T(8,128)(2,1)} %get-tuple-element.48.m_hbm, ...), custom_call_target="tpu_custom_call" | custom-call | flops 2952790016 | bytes 20971520 | tf_op jit(solution)/shard_map/backward/pallas_call | solution.py:499
  92.7 0.9 collective-permute-start.11
  93.6 1.4 collective-permute-done.11
  95.0 1.0 add.67
  96.4 2.6 %collective-permute-start.13 = (f32[128,128]{1,0:T(8,128)S(1)}, f32[128,128]{1,0:T(8,128)S(1)}, u32[]{:S(2)}, u32[]{:S(2)}) collective-permute-start(f32[128,128]{1,0:T(8,128)S(1)} %get-tuple-element.62), channel_id=1, source_target_pairs={{0,4},{2,6},{4,0},{6,2},{1,5},{3,7},{5,1},{7,3},{8,12},{10,14},{12... | collective-permute-start | bytes 196616 | tf_op jit(solution)/shard_map/ppermute | solution.py:547
  99.0 0.9 collective-permute-start.14
  99.8 0.9 collective-permute-done.12
  100.7 1.5 %collective-permute-done.13 = f32[128,128]{1,0:T(8,128)S(1)} collective-permute-done((f32[128,128]{1,0:T(8,128)S(1)}, f32[128,128]{1,0:T(8,128)S(1)}, u32[]{:S(2)}, u32[]{:S(2)}) %collective-permute-start.13) | collective-permute-done | bytes 65568 | tf_op jit(solution)/shard_map/ppermute | solution.py:547
  102.2 0.9 collective-permute-done.14
  103.1 1.6 %collective-permute-start.15 = (f32[32,128]{1,0:T(8,128)S(1)}, f32[32,128]{1,0:T(8,128)S(1)}, u32[]{:S(2)}, u32[]{:S(2)}) collective-permute-start(f32[32,128]{1,0:T(8,128)S(1)} %get-tuple-element.67), channel_id=1, source_target_pairs={{0,64},{64,128},{128,192},{192,0},{1,65},{65,129},{129,193},{193,1... | collective-permute-start | bytes 49160 | tf_op jit(solution)/shard_map/ppermute | solution.py:547
  104.7 2.4 %collective-permute-start.16 = (f32[32,128]{1,0:T(8,128)S(1)}, f32[32,128]{1,0:T(8,128)S(1)}, u32[]{:S(2)}, u32[]{:S(2)}) collective-permute-start(f32[32,128]{1,0:T(8,128)S(1)} %get-tuple-element.69), channel_id=1, source_target_pairs={{0,128},{64,192},{128,0},{192,64},{1,129},{65,193},{129,1},{193,65... | collective-permute-start | bytes 49160 | tf_op jit(solution)/shard_map/ppermute | solution.py:547
  107.1 1.1 collective-permute-start.17
  108.6 0.6 collective-permute-done.16
  109.2 1.1 collective-permute-done.17
  110.3 0.7 broadcast_in_dim.27
  111.0 6.3 %all-to-all-start.3 = ((f32[8,32,128]{2,1,0:T(8,128)}), f32[8,32,128]{2,1,0:T(8,128)S(1)}, u32[]{:S(2)}, u32[]{:S(2)}) async-start(f32[8,32,128]{2,1,0:T(8,128)} %broadcast_in_dim.27), calls=%async_computation.3 | async-start | bytes 262144 | tf_op jit(solution)/shard_map/all_to_all | solution.py:555
  117.3 2.1 %collect.1 = bf16[1024,256]{1,0:T(8,128)(2,1)} custom-call(f32[1024,128]{1,0:T(8,128)S(1)} %copy-done.6, bf16[2048,256]{1,0:T(8,128)(2,1)S(1)} %bitcast.42), custom_call_target="tpu_custom_call" | custom-call | flops 1073741824 | bytes 2097152 | tf_op jit(solution)/shard_map/collect/pallas_call | solution.py:519
  119.3 5.9 %all-to-all-done.3 = f32[8,32,128]{2,1,0:T(8,128)S(1)} async-done(((f32[8,32,128]{2,1,0:T(8,128)}), f32[8,32,128]{2,1,0:T(8,128)S(1)}, u32[]{:S(2)}, u32[]{:S(2)}) %all-to-all-start.3) | async-done | bytes 131104 | tf_op jit(solution)/shard_map/all_to_all | solution.py:555
  125.3 11.2 %all_to_all.25 = bf16[16,32,128]{2,1,0:T(8,128)(2,1)S(1)} all-to-all(bf16[16,32,128]{2,1,0:T(8,128)(2,1)S(1)} %broadcast_in_dim.28), channel_id=1, replica_groups=mesh['y'=4,'z'=8,'x'=4,'core'=2] {'x','y'}, dimensions={0} | all-to-all | bytes 262144 | tf_op jit(solution)/shard_map/all_to_all | solution.py:555
  136.5 6.2 %collective-permute-start.18 = (bf16[512,128]{1,0:T(8,128)(2,1)S(1)}, bf16[512,128]{1,0:T(8,128)(2,1)S(1)}, u32[]{:S(2)}, u32[]{:S(2)}) collective-permute-start(bf16[512,128]{1,0:T(8,128)(2,1)S(1)} %bitcast.50), channel_id=1, source_target_pairs={{0,1},{1,0},{2,3},{3,2},{4,5},{5,4},{6,7},{7,6},{8,9},{9,8},{10,11... | collective-permute-start | bytes 393224 | tf_op jit(solution)/shard_map/ppermute | solution.py:534
  142.6 1.0 collective-permute-done.18
  143.7 0.8 maximum_convert_fusion
  (63 shorter events, 1.3 us)
Async XLA Ops:
  0.6 15.6 %copy-start.10 = (s32[1,1,8]{2,1,0:T(1,128)S(1)}, s32[1,1,8]{2,1,0:T(1,128)}, u32[]{:S(2)}) copy-start(s32[1,1,8]{2,1,0:T(1,128)} %param.17) | copy-start | bytes 100
  0.6 15.6 %copy-start.9 = (s32[1,1,8,64]{3,2,1,0:T(8,128)S(1)}, s32[1,1,8,64]{3,2,1,0:T(8,128)}, u32[]{:S(2)}) copy-start(s32[1,1,8,64]{3,2,1,0:T(8,128)} %param.16) | copy-start | bytes 6148
  0.7 21.3 %copy-start.4 = (s32[1,1,96]{2,1,0:T(1,128)S(1)}, s32[1,1,96]{2,1,0:T(1,128)}, u32[]{:S(2)}) copy-start(s32[1,1,96]{2,1,0:T(1,128)} %param.18) | copy-start | bytes 1156
  0.7 21.3 %copy-start.5 = (s32[1,1,96]{2,1,0:T(1,128)S(1)}, s32[1,1,96]{2,1,0:T(1,128)}, u32[]{:S(2)}) copy-start(s32[1,1,96]{2,1,0:T(1,128)} %param.19) | copy-start | bytes 1156
  0.7 21.3 %copy-start = (bf16[1,1,96,128,128]{4,3,2,1,0:T(8,128)(2,1)S(1)}, bf16[1,1,96,128,128]{4,3,2,1,0:T(8,128)(2,1)}, u32[]{:S(2)}) copy-start(bf16[1,1,96,128,128]{4,3,2,1,0:T(8,128)(2,1)} %param.21) | copy-start | bytes 9437188
  4.1 36.8 %all-to-all-start = ((bf16[32,64,256]{2,1,0:T(8,128)(2,1)}), bf16[32,64,256]{2,1,0:T(8,128)(2,1)}, u32[]{:S(2)}, u32[]{:S(2)}) async-start(bf16[32,64,256]{2,1,0:T(8,128)(2,1)} %bitcast.49), calls=%async_computation | async-start | bytes 2097152 | tf_op jit(solution)/shard_map/all_to_all | solution.py:381
  16.4 14.5 %collective-permute-start = (s32[2,64]{1,0:T(2,128)S(1)}, s32[2,64]{1,0:T(2,128)S(1)}, u32[]{:S(2)}, u32[]{:S(2)}) collective-permute-start(s32[2,64]{1,0:T(2,128)S(1)} %get-tuple-element.75), channel_id=1, source_target_pairs={{0,2},{2,4},{4,6},{6,0},{1,3},{3,5},{5,7},{7,1},{8,10},{10,12},{12... | collective-permute-start | bytes 1544 | tf_op jit(solution)/shard_map/ppermute | solution.py:440
  17.7 13.2 %collective-permute-start.1 = (s32[2,64]{1,0:T(2,128)S(1)}, s32[2,64]{1,0:T(2,128)S(1)}, u32[]{:S(2)}, u32[]{:S(2)}) collective-permute-start(s32[2,64]{1,0:T(2,128)S(1)} %get-tuple-element.74), channel_id=1, source_target_pairs={{0,4},{2,6},{4,0},{6,2},{1,5},{3,7},{5,1},{7,3},{8,12},{10,14},{12... | collective-permute-start | bytes 1544 | tf_op jit(solution)/shard_map/ppermute | solution.py:440
  20.1 10.8 %collective-permute-start.2 = (s32[2,64]{1,0:T(2,128)S(1)}, s32[2,64]{1,0:T(2,128)S(1)}, u32[]{:S(2)}, u32[]{:S(2)}) collective-permute-start(s32[2,64]{1,0:T(2,128)S(1)} %get-tuple-element.76), channel_id=1, source_target_pairs={{0,6},{2,0},{4,2},{6,4},{1,7},{3,1},{5,3},{7,5},{8,14},{10,8},{12,... | collective-permute-start | bytes 1544 | tf_op jit(solution)/shard_map/ppermute | solution.py:440
  21.9 1.0 copy-start.2
  23.0 0.7 copy-start.7
  30.9 2.1 %collective-permute-start.3 = (s32[4,64]{1,0:T(4,128)S(1)}, s32[4,64]{1,0:T(4,128)S(1)}, u32[]{:S(2)}, u32[]{:S(2)}) collective-permute-start(s32[4,64]{1,0:T(4,128)S(1)} %bitcast.54), channel_id=1, source_target_pairs={{0,1},{1,0},{2,3},{3,2},{4,5},{5,4},{6,7},{7,6},{8,9},{9,8},{10,11... | collective-permute-start | bytes 3080 | tf_op jit(solution)/shard_map/ppermute | solution.py:534
  33.2 1.2 copy-start.1
  35.2 26.7 %copy-start.3 = (bf16[256,256]{1,0:T(8,128)(2,1)}, bf16[256,256]{1,0:T(8,128)(2,1)S(1)}, u32[]{:S(2)}) copy-start(bf16[256,256]{1,0:T(8,128)(2,1)S(1)} %get-tuple-element.41.refs_5_) | copy-start | bytes 393220
  40.8 34.4 %all-to-all-start.1 = ((bf16[32,64,256]{2,1,0:T(8,128)(2,1)}), bf16[32,64,256]{2,1,0:T(8,128)(2,1)S(1)}, u32[]{:S(2)}, u32[]{:S(2)}) async-start(bf16[32,64,256]{2,1,0:T(8,128)(2,1)} %bitcast.48), calls=%async_computation.1 | async-start | bytes 2097152 | tf_op jit(solution)/shard_map/all_to_all | solution.py:381
  49.4 6.6 %collective-permute-start.6 = (bf16[256,256]{1,0:T(8,128)(2,1)S(1)}, bf16[256,256]{1,0:T(8,128)(2,1)S(1)}, u32[]{:S(2)}, u32[]{:S(2)}) collective-permute-start(bf16[256,256]{1,0:T(8,128)(2,1)S(1)} %get-tuple-element.44), channel_id=1, source_target_pairs={{0,2},{2,4},{4,6},{6,0},{1,3},{3,5},{5,7},{7,1},{8,10},{10,12},{12... | collective-permute-start | bytes 393224 | tf_op jit(solution)/shard_map/ppermute | solution.py:440
  50.7 6.8 %collective-permute-start.4 = (bf16[256,256]{1,0:T(8,128)(2,1)S(1)}, bf16[256,256]{1,0:T(8,128)(2,1)S(1)}, u32[]{:S(2)}, u32[]{:S(2)}) collective-permute-start(bf16[256,256]{1,0:T(8,128)(2,1)S(1)} %get-tuple-element.42), channel_id=1, source_target_pairs={{0,6},{2,0},{4,2},{6,4},{1,7},{3,1},{5,3},{7,5},{8,14},{10,8},{12,... | collective-permute-start | bytes 393224 | tf_op jit(solution)/shard_map/ppermute | solution.py:440
  52.2 7.0 %collective-permute-start.5 = (bf16[256,256]{1,0:T(8,128)(2,1)S(1)}, bf16[256,256]{1,0:T(8,128)(2,1)S(1)}, u32[]{:S(2)}, u32[]{:S(2)}) collective-permute-start(bf16[256,256]{1,0:T(8,128)(2,1)S(1)} %get-tuple-element.43), channel_id=1, source_target_pairs={{0,4},{2,6},{4,0},{6,2},{1,5},{3,7},{5,1},{7,3},{8,12},{10,14},{12... | collective-permute-start | bytes 393224 | tf_op jit(solution)/shard_map/ppermute | solution.py:440
  53.7 7.2 %collective-permute-start.7 = (bf16[256,256]{1,0:T(8,128)(2,1)S(1)}, bf16[256,256]{1,0:T(8,128)(2,1)S(1)}, u32[]{:S(2)}, u32[]{:S(2)}) collective-permute-start(bf16[256,256]{1,0:T(8,128)(2,1)S(1)} %get-tuple-element.41.refs_5_), channel_id=1, source_target_pairs={{0,1},{1,0},{2,3},{3,2},{4,5},{5,4},{6,7},{7,6},{8,9},{9,8},{10,11... | collective-permute-start | bytes 393224 | tf_op jit(solution)/shard_map/ppermute | solution.py:534
  56.0 5.9 %copy-start.11 = (bf16[256,256]{1,0:T(8,128)(2,1)}, bf16[256,256]{1,0:T(8,128)(2,1)S(1)}, u32[]{:S(2)}) copy-start(bf16[256,256]{1,0:T(8,128)(2,1)S(1)} %collective-permute-done.6.refs_8_) | copy-start | bytes 393220
  56.0 4.9 %collective-permute-start.10 = (bf16[256,256]{1,0:T(8,128)(2,1)S(1)}, bf16[256,256]{1,0:T(8,128)(2,1)S(1)}, u32[]{:S(2)}, u32[]{:S(2)}) collective-permute-start(bf16[256,256]{1,0:T(8,128)(2,1)S(1)} %collective-permute-done.6.refs_8_), channel_id=1, source_target_pairs={{0,1},{1,0},{2,3},{3,2},{4,5},{5,4},{6,7},{7,6},{8,9},{9,8},{10,11... | collective-permute-start | bytes 393224 | tf_op jit(solution)/shard_map/ppermute | solution.py:534
  57.5 4.4 %copy-start.12 = (bf16[256,256]{1,0:T(8,128)(2,1)}, bf16[256,256]{1,0:T(8,128)(2,1)S(1)}, u32[]{:S(2)}) copy-start(bf16[256,256]{1,0:T(8,128)(2,1)S(1)} %collective-permute-done.4.refs_6_) | copy-start | bytes 393220
  57.5 3.5 %collective-permute-start.8 = (bf16[256,256]{1,0:T(8,128)(2,1)S(1)}, bf16[256,256]{1,0:T(8,128)(2,1)S(1)}, u32[]{:S(2)}, u32[]{:S(2)}) collective-permute-start(bf16[256,256]{1,0:T(8,128)(2,1)S(1)} %collective-permute-done.4.refs_6_), channel_id=1, source_target_pairs={{0,1},{1,0},{2,3},{3,2},{4,5},{5,4},{6,7},{7,6},{8,9},{9,8},{10,11... | collective-permute-start | bytes 393224 | tf_op jit(solution)/shard_map/ppermute | solution.py:534
  59.2 2.7 %copy-start.13 = (bf16[256,256]{1,0:T(8,128)(2,1)}, bf16[256,256]{1,0:T(8,128)(2,1)S(1)}, u32[]{:S(2)}) copy-start(bf16[256,256]{1,0:T(8,128)(2,1)S(1)} %collective-permute-done.5.refs_7_) | copy-start | bytes 393220
  59.2 2.7 %collective-permute-start.9 = (bf16[256,256]{1,0:T(8,128)(2,1)S(1)}, bf16[256,256]{1,0:T(8,128)(2,1)S(1)}, u32[]{:S(2)}, u32[]{:S(2)}) collective-permute-start(bf16[256,256]{1,0:T(8,128)(2,1)S(1)} %collective-permute-done.5.refs_7_), channel_id=1, source_target_pairs={{0,1},{1,0},{2,3},{3,2},{4,5},{5,4},{6,7},{7,6},{8,9},{9,8},{10,11... | collective-permute-start | bytes 393224 | tf_op jit(solution)/shard_map/ppermute | solution.py:534
  60.9 1.0 copy-start.14
  61.0 1.0 copy-start.15
  61.0 1.0 copy-start.16
  61.9 0.7 copy-start.17
  75.2 9.3 %copy-start.8 = (bf16[32,64,256]{2,1,0:T(8,128)(2,1)}, bf16[32,64,256]{2,1,0:T(8,128)(2,1)S(1)}, u32[]{:S(2)}) copy-start(bf16[32,64,256]{2,1,0:T(8,128)(2,1)S(1)} %all-to-all-done.1) | copy-start | bytes 3145732
  75.2 35.1 %all-to-all-start.2 = ((bf16[32,64,256]{2,1,0:T(8,128)(2,1)}), bf16[32,64,256]{2,1,0:T(8,128)(2,1)S(1)}, u32[]{:S(2)}, u32[]{:S(2)}) async-start(bf16[32,64,256]{2,1,0:T(8,128)(2,1)} %bitcast.47), calls=%async_computation.2 | async-start | bytes 2097152 | tf_op jit(solution)/shard_map/all_to_all | solution.py:381
  84.5 32.7 %copy-start.6 = (f32[1024,128]{1,0:T(8,128)S(1)}, f32[1024,128]{1,0:T(8,128)}, u32[]{:S(2)}) copy-start(f32[1024,128]{1,0:T(8,128)} %get-tuple-element.54.column_ref) | copy-start | bytes 1572868
  92.7 2.3 %collective-permute-start.11 = (f32[512,128]{1,0:T(8,128)}, f32[512,128]{1,0:T(8,128)S(1)}, u32[]{:S(2)}, u32[]{:S(2)}) collective-permute-start(f32[512,128]{1,0:T(8,128)} %get-tuple-element.51), channel_id=1, source_target_pairs={{0,1},{1,0},{2,3},{3,2},{4,5},{5,4},{6,7},{7,6},{8,9},{9,8},{10,11... | collective-permute-start | bytes 786440 | tf_op jit(solution)/shard_map/ppermute | solution.py:534
  96.0 4.7 %collective-permute-start.12 = (f32[128,128]{1,0:T(8,128)S(1)}, f32[128,128]{1,0:T(8,128)S(1)}, u32[]{:S(2)}, u32[]{:S(2)}) collective-permute-start(f32[128,128]{1,0:T(8,128)S(1)} %get-tuple-element.60), channel_id=1, source_target_pairs={{0,2},{2,4},{4,6},{6,0},{1,3},{3,5},{5,7},{7,1},{8,10},{10,12},{12... | collective-permute-start | bytes 196616 | tf_op jit(solution)/shard_map/ppermute | solution.py:547
  96.4 5.8 %collective-permute-start.13 = (f32[128,128]{1,0:T(8,128)S(1)}, f32[128,128]{1,0:T(8,128)S(1)}, u32[]{:S(2)}, u32[]{:S(2)}) collective-permute-start(f32[128,128]{1,0:T(8,128)S(1)} %get-tuple-element.62), channel_id=1, source_target_pairs={{0,4},{2,6},{4,0},{6,2},{1,5},{3,7},{5,1},{7,3},{8,12},{10,14},{12... | collective-permute-start | bytes 196616 | tf_op jit(solution)/shard_map/ppermute | solution.py:547
  99.0 4.1 %collective-permute-start.14 = (f32[128,128]{1,0:T(8,128)S(1)}, f32[128,128]{1,0:T(8,128)S(1)}, u32[]{:S(2)}, u32[]{:S(2)}) collective-permute-start(f32[128,128]{1,0:T(8,128)S(1)} %get-tuple-element.61), channel_id=1, source_target_pairs={{0,6},{2,0},{4,2},{6,4},{1,7},{3,1},{5,3},{7,5},{8,14},{10,8},{12,... | collective-permute-start | bytes 196616 | tf_op jit(solution)/shard_map/ppermute | solution.py:547
  103.1 5.5 %collective-permute-start.15 = (f32[32,128]{1,0:T(8,128)S(1)}, f32[32,128]{1,0:T(8,128)S(1)}, u32[]{:S(2)}, u32[]{:S(2)}) collective-permute-start(f32[32,128]{1,0:T(8,128)S(1)} %get-tuple-element.67), channel_id=1, source_target_pairs={{0,64},{64,128},{128,192},{192,0},{1,65},{65,129},{129,193},{193,1... | collective-permute-start | bytes 49160 | tf_op jit(solution)/shard_map/ppermute | solution.py:547
  104.7 4.5 %collective-permute-start.16 = (f32[32,128]{1,0:T(8,128)S(1)}, f32[32,128]{1,0:T(8,128)S(1)}, u32[]{:S(2)}, u32[]{:S(2)}) collective-permute-start(f32[32,128]{1,0:T(8,128)S(1)} %get-tuple-element.69), channel_id=1, source_target_pairs={{0,128},{64,192},{128,0},{192,64},{1,129},{65,193},{129,1},{193,65... | collective-permute-start | bytes 49160 | tf_op jit(solution)/shard_map/ppermute | solution.py:547
  107.1 3.2 %collective-permute-start.17 = (f32[32,128]{1,0:T(8,128)S(1)}, f32[32,128]{1,0:T(8,128)S(1)}, u32[]{:S(2)}, u32[]{:S(2)}) collective-permute-start(f32[32,128]{1,0:T(8,128)S(1)} %get-tuple-element.68), channel_id=1, source_target_pairs={{0,192},{64,0},{128,64},{192,128},{1,193},{65,1},{129,65},{193,129... | collective-permute-start | bytes 49160 | tf_op jit(solution)/shard_map/ppermute | solution.py:547
  111.0 14.2 %all-to-all-start.3 = ((f32[8,32,128]{2,1,0:T(8,128)}), f32[8,32,128]{2,1,0:T(8,128)S(1)}, u32[]{:S(2)}, u32[]{:S(2)}) async-start(f32[8,32,128]{2,1,0:T(8,128)} %broadcast_in_dim.27), calls=%async_computation.3 | async-start | bytes 262144 | tf_op jit(solution)/shard_map/all_to_all | solution.py:555
  136.5 7.2 %collective-permute-start.18 = (bf16[512,128]{1,0:T(8,128)(2,1)S(1)}, bf16[512,128]{1,0:T(8,128)(2,1)S(1)}, u32[]{:S(2)}, u32[]{:S(2)}) collective-permute-start(bf16[512,128]{1,0:T(8,128)(2,1)S(1)} %bitcast.50), channel_id=1, source_target_pairs={{0,1},{1,0},{2,3},{3,2},{4,5},{5,4},{6,7},{7,6},{8,9},{9,8},{10,11... | collective-permute-start | bytes 393224 | tf_op jit(solution)/shard_map/ppermute | solution.py:534

commit v7 on v6

--- a/solution.py
+++ b/solution.py
@@ -514,7 +514,7 @@
         cost_estimate=cost(2 * work * (work + 3 * width) * width, 20 * MIB),
         name="backward",
     )(core.reshape(1).astype(jnp.int32), in_hbm(ws_cot), weights, adjacency, mixed, slopes)
-    grads = reduce_rows(reduce_rows(kept + swap_cores(given), "x"), "y")
+    grads = sum(reduce_rows(reduce_rows([kept, swap_cores(given)], "x"), "y"))
     grads, returned = lax.optimization_barrier((grads, returned))
     second_out = pl.pallas_call(
         collect_body,
@@ -534,20 +534,21 @@
     return lax.ppermute(value, "core", [(0, 1), (1, 0)])
 
 
-def reduce_rows(kept, axis):
+def reduce_rows(terms, axis):
     size = lax.axis_size(axis)
-    share = kept.shape[0] // size
+    share = terms[0].shape[0] // size
     here = lax.axis_index(axis)
 
     def rows_of(index):
-        return lax.dynamic_slice_in_dim(kept, lax.rem(index, size) * share, share, axis=0)
-
-    total = rows_of(here)
+        start = lax.rem(index, size) * share
+        return sum(lax.dynamic_slice_in_dim(term, start, share, axis=0) for term in terms)
+
+    shares = [rows_of(here)]
     for k in range(1, size):
-        total = total + lax.ppermute(
-            rows_of(here + k), axis, [(i, (i + k) % size) for i in range(size)]
+        shares.append(
+            lax.ppermute(rows_of(here + k), axis, [(i, (i + k) % size) for i in range(size)])
         )
-    return total
+    return shares
 
 
 def from_all(value, axes):

time: 145 us -> 145 us (level)
  starting transfers between devices: 69.3 us -> 71.1 us
    ppermute x7, starting transfers between devices: 14.9 us -> 16.6 us  [swap_cores(): return lax.ppermute(value, 'core', [(0, 1), (1, 0)])]
where the time goes in v7:
time: 145 us; the launch traced here: 144 us
  starting transfers between devices  71.1 us (49%)
  Pallas kernels  33.6 us (23%)
  waiting for transfers between devices  20.3 us (14%)
  blocking collectives  11.2 us (8%)
  local copies, waits for them, and re-layouts  4.54 us (3%)
  other arithmetic  2.01 us (1%)
  between operations  1.69 us (1%)
    all_to_all x3, starting transfers between devices, to_owners(): lax.all_to_all(value, WIDE, split_axis=0, concat_axis=0, tiled=True)  30.1 us
    ppermute x7, starting transfers between devices, swap_cores(): return lax.ppermute(value, 'core', [(0, 1), (1, 0)])  16.6 us
    pallas_call x1, Pallas kernels, local(): pl.pallas_call(lambda *refs: forward_body(size, *refs), out_shape=(pltpu....  12.6 us
    all_to_all x1, blocking collectives, from_all(): return lax.all_to_all(value, axes, split_axis=0, concat_axis=0, tiled=True)  11.2 us
    ppermute x6, starting transfers between devices, shift(): return lax.ppermute(value, 'x', [(i, (i + by) % size) for i in range(size)])  9.18 us
    ppermute x6, starting transfers between devices, reduce_rows(): lax.ppermute(rows_of(here + k), axis, [(i, (i + k) % size) for i in range...  8.94 us
    pallas_call x1, Pallas kernels, local(): pl.pallas_call(backward_body, out_shape=(jax.ShapeDtypeStruct((width * wi...  8.1 us
    pallas_call x1, Pallas kernels, local(): pl.pallas_call(prepare_body, out_shape=(pltpu.HBM((work, work + halo), BF...  6.82 us
  transfers between devices with their start and end apart: 23, of which 13 were waited for; matrix products, arithmetic and copies ran while one was open for 1% of the time, Pallas kernels for 21%

profile of v7, /device:TPU:1, one launch (start us, length us, event | category | flops | bytes accessed | tf_op | source)
XLA Modules:
  0.0 144.5 jit_solution(169460291089992923)
XLA Ops:
  0.7 3.4 %route.1 = (bf16[2048,256]{1,0:T(8,128)(2,1)}, s32[1,1024]{1,0:T(1,128)}) custom-call(s32[1,1024]{1,0:T(1,128)} %bitcast.60, bf16[1024,256]{1,0:T(8,128)(2,1)} %refs_1_.1), custom_call_target="tpu_custom_call" | custom-call | flops 1073741824 | bytes 2097152 | tf_op jit(solution)/shard_map/route/pallas_call | solution.py:385
  4.1 12.2 %all-to-all-start = ((bf16[32,64,256]{2,1,0:T(8,128)(2,1)}), bf16[32,64,256]{2,1,0:T(8,128)(2,1)}, u32[]{:S(2)}, u32[]{:S(2)}) async-start(bf16[32,64,256]{2,1,0:T(8,128)(2,1)} %bitcast.49), calls=%async_computation | async-start | bytes 2097152 | tf_op jit(solution)/shard_map/all_to_all | solution.py:381
  16.4 1.3 collective-permute-start
  17.7 2.4 %collective-permute-start.1 = (s32[2,64]{1,0:T(2,128)S(1)}, s32[2,64]{1,0:T(2,128)S(1)}, u32[]{:S(2)}, u32[]{:S(2)}) collective-permute-start(s32[2,64]{1,0:T(2,128)S(1)} %get-tuple-element.75), channel_id=1, source_target_pairs={{0,4},{2,6},{4,0},{6,2},{1,5},{3,7},{5,1},{7,3},{8,12},{10,14},{12... | collective-permute-start | bytes 1544 | tf_op jit(solution)/shard_map/ppermute | solution.py:440
  20.1 1.2 collective-permute-start.2
  22.0 1.0 copy-done.2
  23.0 0.7 copy-done.7
  23.7 6.8 %prepare.1 = (bf16[2048,2560]{1,0:T(8,128)(2,1)}, bf16[2048,256]{1,0:T(8,128)(2,1)}, f32[1024,128]{1,0:T(8,128)}) custom-call(s32[96]{0:T(128)S(1)} %bitcast.44, s32[96]{0:T(128)S(1)} %bitcast.45, s32[1]{0:T(128)} %bitcast.41.count_ref, s32[1,1024]{1,0:T(1,128)S(1)} %copy-done.7, bf16[96,128,128]{2,1,0:T(8,128)(2,1)S(1)} %bitcast.43, ...), custom_call_target="tpu_custom_call" | custom-call | flops 1073741824 | bytes 20971520 | tf_op jit(solution)/shard_map/prepare/pallas_call | solution.py:407
  30.6 3.0 %collective-permute-start.3 = (s32[4,64]{1,0:T(4,128)S(1)}, s32[4,64]{1,0:T(4,128)S(1)}, u32[]{:S(2)}, u32[]{:S(2)}) collective-permute-start(s32[4,64]{1,0:T(4,128)S(1)} %bitcast.54), channel_id=1, source_target_pairs={{0,1},{1,0},{2,3},{3,2},{4,5},{5,4},{6,7},{7,6},{8,9},{9,8},{10,11... | collective-permute-start | bytes 3080 | tf_op jit(solution)/shard_map/ppermute | solution.py:534
  33.6 0.8 collective-permute-done.3
  34.6 1.2 copy-done.1
  35.9 0.7 pick.1
  36.6 4.2 %all-to-all-done = bf16[32,64,256]{2,1,0:T(8,128)(2,1)} async-done(((bf16[32,64,256]{2,1,0:T(8,128)(2,1)}), bf16[32,64,256]{2,1,0:T(8,128)(2,1)}, u32[]{:S(2)}, u32[]{:S(2)}) %all-to-all-start) | async-done | bytes 1048608 | tf_op jit(solution)/shard_map/all_to_all | solution.py:381
  40.8 8.6 %all-to-all-start.1 = ((bf16[32,64,256]{2,1,0:T(8,128)(2,1)}), bf16[32,64,256]{2,1,0:T(8,128)(2,1)S(1)}, u32[]{:S(2)}, u32[]{:S(2)}) async-start(bf16[32,64,256]{2,1,0:T(8,128)(2,1)} %bitcast.48), calls=%async_computation.1 | async-start | bytes 2097152 | tf_op jit(solution)/shard_map/all_to_all | solution.py:381
  49.4 1.3 collective-permute-start.6
  50.7 1.5 %collective-permute-start.4 = (bf16[256,256]{1,0:T(8,128)(2,1)S(1)}, bf16[256,256]{1,0:T(8,128)(2,1)S(1)}, u32[]{:S(2)}, u32[]{:S(2)}) collective-permute-start(bf16[256,256]{1,0:T(8,128)(2,1)S(1)} %get-tuple-element.42), channel_id=1, source_target_pairs={{0,6},{2,0},{4,2},{6,4},{1,7},{3,1},{5,3},{7,5},{8,14},{10,8},{12,... | collective-permute-start | bytes 393224 | tf_op jit(solution)/shard_map/ppermute | solution.py:440
  52.2 1.5 %collective-permute-start.5 = (bf16[256,256]{1,0:T(8,128)(2,1)S(1)}, bf16[256,256]{1,0:T(8,128)(2,1)S(1)}, u32[]{:S(2)}, u32[]{:S(2)}) collective-permute-start(bf16[256,256]{1,0:T(8,128)(2,1)S(1)} %get-tuple-element.43), channel_id=1, source_target_pairs={{0,4},{2,6},{4,0},{6,2},{1,5},{3,7},{5,1},{7,3},{8,12},{10,14},{12... | collective-permute-start | bytes 393224 | tf_op jit(solution)/shard_map/ppermute | solution.py:440
  53.7 2.3 %collective-permute-start.7 = (bf16[256,256]{1,0:T(8,128)(2,1)S(1)}, bf16[256,256]{1,0:T(8,128)(2,1)S(1)}, u32[]{:S(2)}, u32[]{:S(2)}) collective-permute-start(bf16[256,256]{1,0:T(8,128)(2,1)S(1)} %get-tuple-element.41.refs_5_), channel_id=1, source_target_pairs={{0,1},{1,0},{2,3},{3,2},{4,5},{5,4},{6,7},{7,6},{8,9},{9,8},{10,11... | collective-permute-start | bytes 393224 | tf_op jit(solution)/shard_map/ppermute | solution.py:534
  56.0 1.5 %collective-permute-start.10 = (bf16[256,256]{1,0:T(8,128)(2,1)S(1)}, bf16[256,256]{1,0:T(8,128)(2,1)S(1)}, u32[]{:S(2)}, u32[]{:S(2)}) collective-permute-start(bf16[256,256]{1,0:T(8,128)(2,1)S(1)} %collective-permute-done.6.refs_8_), channel_id=1, source_target_pairs={{0,1},{1,0},{2,3},{3,2},{4,5},{5,4},{6,7},{7,6},{8,9},{9,8},{10,11... | collective-permute-start | bytes 393224 | tf_op jit(solution)/shard_map/ppermute | solution.py:534
  57.5 1.0 collective-permute-start.8
  58.5 0.7 collective-permute-done.5.refs_7_
  59.2 1.7 %collective-permute-start.9 = (bf16[256,256]{1,0:T(8,128)(2,1)S(1)}, bf16[256,256]{1,0:T(8,128)(2,1)S(1)}, u32[]{:S(2)}, u32[]{:S(2)}) collective-permute-start(bf16[256,256]{1,0:T(8,128)(2,1)S(1)} %collective-permute-done.5.refs_7_), channel_id=1, source_target_pairs={{0,1},{1,0},{2,3},{3,2},{4,5},{5,4},{6,7},{7,6},{8,9},{9,8},{10,11... | collective-permute-start | bytes 393224 | tf_op jit(solution)/shard_map/ppermute | solution.py:534
  61.0 0.9 collective-permute-done.9.refs_11_
  62.0 0.6 copy-done.17
  62.6 12.6 %forward.1 = (bf16[2048,256]{1,0:T(8,128)(2,1)}, bf16[2,2048,256]{2,1,0:T(8,128)(2,1)}, f32[2,2048,256]{2,1,0:T(8,128)}) custom-call(s32[1]{0:T(128)} %bitcast.1.refs_0_, s32[1]{0:T(128)} %bitcast.refs_1_.core_ref, bf16[2048,256]{1,0:T(8,128)(2,1)} %bitcast.8.refs_2_, bf16[2,256,256]{2,1,0:T(8,128)(2,1)} %w_hbm.1, ...), custom_call_target="tpu_custom_call" | custom-call | flops 5905580032 | bytes 25165824 | tf_op jit(solution)/shard_map/forward/pallas_call | solution.py:462
  75.2 9.3 %all-to-all-start.2 = ((bf16[32,64,256]{2,1,0:T(8,128)(2,1)}), bf16[32,64,256]{2,1,0:T(8,128)(2,1)S(1)}, u32[]{:S(2)}, u32[]{:S(2)}) async-start(bf16[32,64,256]{2,1,0:T(8,128)(2,1)} %bitcast.47), calls=%async_computation.2 | async-start | bytes 2097152 | tf_op jit(solution)/shard_map/all_to_all | solution.py:381
  84.6 8.1 %backward.1 = (f32[512,128]{1,0:T(8,128)}, f32[512,128]{1,0:T(8,128)}) custom-call(s32[1]{0:T(128)} %bitcast.refs_1_.core_ref, bf16[2048,256]{1,0:T(8,128)(2,1)} %bitcast.46, bf16[2,256,256]{2,1,0:T(8,128)(2,1)} %w_hbm.1, bf16[2048,2560]{1,0:T(8,128)(2,1)} %get-tuple-element.40.refs_4_.adj_hbm, bf16[2,2048,256]{2,1,0:T(8,128)(2,1)} %get-tuple-element.48.m_hbm, ...), custom_call_target="tpu_custom_call" | custom-call | flops 2952790016 | bytes 20971520 | tf_op jit(solution)/shard_map/backward/pallas_call | solution.py:499
  92.7 0.9 collective-permute-start.11
  93.6 1.4 collective-permute-done.11
  95.0 1.0 dynamic-slice_add_fusion.3
  96.3 2.6 %collective-permute-start.13 = (f32[128,128]{1,0:T(8,128)S(1)}, f32[128,128]{1,0:T(8,128)S(1)}, u32[]{:S(2)}, u32[]{:S(2)}) collective-permute-start(f32[128,128]{1,0:T(8,128)S(1)} %get-tuple-element.60), channel_id=1, source_target_pairs={{0,4},{2,6},{4,0},{6,2},{1,5},{3,7},{5,1},{7,3},{8,12},{10,14},{12... | collective-permute-start | bytes 196616 | tf_op jit(solution)/shard_map/ppermute | solution.py:549
  98.9 0.9 collective-permute-start.14
  99.8 0.9 collective-permute-done.12
  100.7 1.5 %collective-permute-done.13 = f32[128,128]{1,0:T(8,128)S(1)} collective-permute-done((f32[128,128]{1,0:T(8,128)S(1)}, f32[128,128]{1,0:T(8,128)S(1)}, u32[]{:S(2)}, u32[]{:S(2)}) %collective-permute-start.13) | collective-permute-done | bytes 65568 | tf_op jit(solution)/shard_map/ppermute | solution.py:549
  102.2 0.9 collective-permute-done.14
  103.0 1.6 %collective-permute-start.15 = (f32[32,128]{1,0:T(8,128)S(1)}, f32[32,128]{1,0:T(8,128)S(1)}, u32[]{:S(2)}, u32[]{:S(2)}) collective-permute-start(f32[32,128]{1,0:T(8,128)S(1)} %get-tuple-element.64), channel_id=1, source_target_pairs={{0,64},{64,128},{128,192},{192,0},{1,65},{65,129},{129,193},{193,1... | collective-permute-start | bytes 49160 | tf_op jit(solution)/shard_map/ppermute | solution.py:549
  104.6 2.4 %collective-permute-start.16 = (f32[32,128]{1,0:T(8,128)S(1)}, f32[32,128]{1,0:T(8,128)S(1)}, u32[]{:S(2)}, u32[]{:S(2)}) collective-permute-start(f32[32,128]{1,0:T(8,128)S(1)} %get-tuple-element.66), channel_id=1, source_target_pairs={{0,128},{64,192},{128,0},{192,64},{1,129},{65,193},{129,1},{193,65... | collective-permute-start | bytes 49160 | tf_op jit(solution)/shard_map/ppermute | solution.py:549
  107.1 1.1 collective-permute-start.17
  108.6 0.5 collective-permute-done.16
  109.1 1.1 collective-permute-done.17
  110.2 0.7 broadcast_in_dim.27
  110.9 6.3 %all-to-all-start.3 = ((f32[8,32,128]{2,1,0:T(8,128)}), f32[8,32,128]{2,1,0:T(8,128)S(1)}, u32[]{:S(2)}, u32[]{:S(2)}) async-start(f32[8,32,128]{2,1,0:T(8,128)} %broadcast_in_dim.27), calls=%async_computation.3 | async-start | bytes 262144 | tf_op jit(solution)/shard_map/all_to_all | solution.py:556
  117.2 2.0 %collect.1 = bf16[1024,256]{1,0:T(8,128)(2,1)} custom-call(f32[1024,128]{1,0:T(8,128)S(1)} %copy-done.6, bf16[2048,256]{1,0:T(8,128)(2,1)S(1)} %bitcast.42), custom_call_target="tpu_custom_call" | custom-call | flops 1073741824 | bytes 2097152 | tf_op jit(solution)/shard_map/collect/pallas_call | solution.py:519
  119.3 5.9 %all-to-all-done.3 = f32[8,32,128]{2,1,0:T(8,128)S(1)} async-done(((f32[8,32,128]{2,1,0:T(8,128)}), f32[8,32,128]{2,1,0:T(8,128)S(1)}, u32[]{:S(2)}, u32[]{:S(2)}) %all-to-all-start.3) | async-done | bytes 131104 | tf_op jit(solution)/shard_map/all_to_all | solution.py:556
  125.2 11.2 %all_to_all.25 = bf16[16,32,128]{2,1,0:T(8,128)(2,1)S(1)} all-to-all(bf16[16,32,128]{2,1,0:T(8,128)(2,1)S(1)} %broadcast_in_dim.28), channel_id=1, replica_groups=mesh['y'=4,'z'=8,'x'=4,'core'=2] {'x','y'}, dimensions={0} | all-to-all | bytes 262144 | tf_op jit(solution)/shard_map/all_to_all | solution.py:556
  136.4 6.2 %collective-permute-start.18 = (bf16[512,128]{1,0:T(8,128)(2,1)S(1)}, bf16[512,128]{1,0:T(8,128)(2,1)S(1)}, u32[]{:S(2)}, u32[]{:S(2)}) collective-permute-start(bf16[512,128]{1,0:T(8,128)(2,1)S(1)} %bitcast.50), channel_id=1, source_target_pairs={{0,1},{1,0},{2,3},{3,2},{4,5},{5,4},{6,7},{7,6},{8,9},{9,8},{10,11... | collective-permute-start | bytes 393224 | tf_op jit(solution)/shard_map/ppermute | solution.py:534
  142.6 1.0 collective-permute-done.18
  143.6 0.8 maximum_convert_fusion
  (61 shorter events, 1.3 us)
Async XLA Ops:
  0.6 15.6 %copy-start.10 = (s32[1,1,8]{2,1,0:T(1,128)S(1)}, s32[1,1,8]{2,1,0:T(1,128)}, u32[]{:S(2)}) copy-start(s32[1,1,8]{2,1,0:T(1,128)} %param.17) | copy-start | bytes 100
  0.6 15.6 %copy-start.9 = (s32[1,1,8,64]{3,2,1,0:T(8,128)S(1)}, s32[1,1,8,64]{3,2,1,0:T(8,128)}, u32[]{:S(2)}) copy-start(s32[1,1,8,64]{3,2,1,0:T(8,128)} %param.16) | copy-start | bytes 6148
  0.7 21.3 %copy-start.4 = (s32[1,1,96]{2,1,0:T(1,128)S(1)}, s32[1,1,96]{2,1,0:T(1,128)}, u32[]{:S(2)}) copy-start(s32[1,1,96]{2,1,0:T(1,128)} %param.18) | copy-start | bytes 1156
  0.7 21.3 %copy-start.5 = (s32[1,1,96]{2,1,0:T(1,128)S(1)}, s32[1,1,96]{2,1,0:T(1,128)}, u32[]{:S(2)}) copy-start(s32[1,1,96]{2,1,0:T(1,128)} %param.19) | copy-start | bytes 1156
  0.7 21.3 %copy-start = (bf16[1,1,96,128,128]{4,3,2,1,0:T(8,128)(2,1)S(1)}, bf16[1,1,96,128,128]{4,3,2,1,0:T(8,128)(2,1)}, u32[]{:S(2)}) copy-start(bf16[1,1,96,128,128]{4,3,2,1,0:T(8,128)(2,1)} %param.21) | copy-start | bytes 9437188
  4.1 36.8 %all-to-all-start = ((bf16[32,64,256]{2,1,0:T(8,128)(2,1)}), bf16[32,64,256]{2,1,0:T(8,128)(2,1)}, u32[]{:S(2)}, u32[]{:S(2)}) async-start(bf16[32,64,256]{2,1,0:T(8,128)(2,1)} %bitcast.49), calls=%async_computation | async-start | bytes 2097152 | tf_op jit(solution)/shard_map/all_to_all | solution.py:381
  16.4 14.1 %collective-permute-start = (s32[2,64]{1,0:T(2,128)S(1)}, s32[2,64]{1,0:T(2,128)S(1)}, u32[]{:S(2)}, u32[]{:S(2)}) collective-permute-start(s32[2,64]{1,0:T(2,128)S(1)} %get-tuple-element.76), channel_id=1, source_target_pairs={{0,2},{2,4},{4,6},{6,0},{1,3},{3,5},{5,7},{7,1},{8,10},{10,12},{12... | collective-permute-start | bytes 1544 | tf_op jit(solution)/shard_map/ppermute | solution.py:440
  17.7 12.9 %collective-permute-start.1 = (s32[2,64]{1,0:T(2,128)S(1)}, s32[2,64]{1,0:T(2,128)S(1)}, u32[]{:S(2)}, u32[]{:S(2)}) collective-permute-start(s32[2,64]{1,0:T(2,128)S(1)} %get-tuple-element.75), channel_id=1, source_target_pairs={{0,4},{2,6},{4,0},{6,2},{1,5},{3,7},{5,1},{7,3},{8,12},{10,14},{12... | collective-permute-start | bytes 1544 | tf_op jit(solution)/shard_map/ppermute | solution.py:440
  20.1 10.4 %collective-permute-start.2 = (s32[2,64]{1,0:T(2,128)S(1)}, s32[2,64]{1,0:T(2,128)S(1)}, u32[]{:S(2)}, u32[]{:S(2)}) collective-permute-start(s32[2,64]{1,0:T(2,128)S(1)} %get-tuple-element.77), channel_id=1, source_target_pairs={{0,6},{2,0},{4,2},{6,4},{1,7},{3,1},{5,3},{7,5},{8,14},{10,8},{12,... | collective-permute-start | bytes 1544 | tf_op jit(solution)/shard_map/ppermute | solution.py:440
  21.9 1.0 copy-start.2
  23.0 0.7 copy-start.7
  30.6 3.8 %collective-permute-start.3 = (s32[4,64]{1,0:T(4,128)S(1)}, s32[4,64]{1,0:T(4,128)S(1)}, u32[]{:S(2)}, u32[]{:S(2)}) collective-permute-start(s32[4,64]{1,0:T(4,128)S(1)} %bitcast.54), channel_id=1, source_target_pairs={{0,1},{1,0},{2,3},{3,2},{4,5},{5,4},{6,7},{7,6},{8,9},{9,8},{10,11... | collective-permute-start | bytes 3080 | tf_op jit(solution)/shard_map/ppermute | solution.py:534
  34.6 1.2 copy-start.1
  36.6 25.3 %copy-start.3 = (bf16[256,256]{1,0:T(8,128)(2,1)}, bf16[256,256]{1,0:T(8,128)(2,1)S(1)}, u32[]{:S(2)}) copy-start(bf16[256,256]{1,0:T(8,128)(2,1)S(1)} %get-tuple-element.41.refs_5_) | copy-start | bytes 393220
  40.8 34.4 %all-to-all-start.1 = ((bf16[32,64,256]{2,1,0:T(8,128)(2,1)}), bf16[32,64,256]{2,1,0:T(8,128)(2,1)S(1)}, u32[]{:S(2)}, u32[]{:S(2)}) async-start(bf16[32,64,256]{2,1,0:T(8,128)(2,1)} %bitcast.48), calls=%async_computation.1 | async-start | bytes 2097152 | tf_op jit(solution)/shard_map/all_to_all | solution.py:381
  49.4 6.6 %collective-permute-start.6 = (bf16[256,256]{1,0:T(8,128)(2,1)S(1)}, bf16[256,256]{1,0:T(8,128)(2,1)S(1)}, u32[]{:S(2)}, u32[]{:S(2)}) collective-permute-start(bf16[256,256]{1,0:T(8,128)(2,1)S(1)} %get-tuple-element.44), channel_id=1, source_target_pairs={{0,2},{2,4},{4,6},{6,0},{1,3},{3,5},{5,7},{7,1},{8,10},{10,12},{12... | collective-permute-start | bytes 393224 | tf_op jit(solution)/shard_map/ppermute | solution.py:440
  50.7 6.8 %collective-permute-start.4 = (bf16[256,256]{1,0:T(8,128)(2,1)S(1)}, bf16[256,256]{1,0:T(8,128)(2,1)S(1)}, u32[]{:S(2)}, u32[]{:S(2)}) collective-permute-start(bf16[256,256]{1,0:T(8,128)(2,1)S(1)} %get-tuple-element.42), channel_id=1, source_target_pairs={{0,6},{2,0},{4,2},{6,4},{1,7},{3,1},{5,3},{7,5},{8,14},{10,8},{12,... | collective-permute-start | bytes 393224 | tf_op jit(solution)/shard_map/ppermute | solution.py:440
  52.2 7.0 %collective-permute-start.5 = (bf16[256,256]{1,0:T(8,128)(2,1)S(1)}, bf16[256,256]{1,0:T(8,128)(2,1)S(1)}, u32[]{:S(2)}, u32[]{:S(2)}) collective-permute-start(bf16[256,256]{1,0:T(8,128)(2,1)S(1)} %get-tuple-element.43), channel_id=1, source_target_pairs={{0,4},{2,6},{4,0},{6,2},{1,5},{3,7},{5,1},{7,3},{8,12},{10,14},{12... | collective-permute-start | bytes 393224 | tf_op jit(solution)/shard_map/ppermute | solution.py:440
  53.7 7.2 %collective-permute-start.7 = (bf16[256,256]{1,0:T(8,128)(2,1)S(1)}, bf16[256,256]{1,0:T(8,128)(2,1)S(1)}, u32[]{:S(2)}, u32[]{:S(2)}) collective-permute-start(bf16[256,256]{1,0:T(8,128)(2,1)S(1)} %get-tuple-element.41.refs_5_), channel_id=1, source_target_pairs={{0,1},{1,0},{2,3},{3,2},{4,5},{5,4},{6,7},{7,6},{8,9},{9,8},{10,11... | collective-permute-start | bytes 393224 | tf_op jit(solution)/shard_map/ppermute | solution.py:534
  56.0 5.9 %copy-start.11 = (bf16[256,256]{1,0:T(8,128)(2,1)}, bf16[256,256]{1,0:T(8,128)(2,1)S(1)}, u32[]{:S(2)}) copy-start(bf16[256,256]{1,0:T(8,128)(2,1)S(1)} %collective-permute-done.6.refs_8_) | copy-start | bytes 393220
  56.0 4.9 %collective-permute-start.10 = (bf16[256,256]{1,0:T(8,128)(2,1)S(1)}, bf16[256,256]{1,0:T(8,128)(2,1)S(1)}, u32[]{:S(2)}, u32[]{:S(2)}) collective-permute-start(bf16[256,256]{1,0:T(8,128)(2,1)S(1)} %collective-permute-done.6.refs_8_), channel_id=1, source_target_pairs={{0,1},{1,0},{2,3},{3,2},{4,5},{5,4},{6,7},{7,6},{8,9},{9,8},{10,11... | collective-permute-start | bytes 393224 | tf_op jit(solution)/shard_map/ppermute | solution.py:534
  57.5 4.4 %copy-start.12 = (bf16[256,256]{1,0:T(8,128)(2,1)}, bf16[256,256]{1,0:T(8,128)(2,1)S(1)}, u32[]{:S(2)}) copy-start(bf16[256,256]{1,0:T(8,128)(2,1)S(1)} %collective-permute-done.4.refs_6_) | copy-start | bytes 393220
  57.5 3.5 %collective-permute-start.8 = (bf16[256,256]{1,0:T(8,128)(2,1)S(1)}, bf16[256,256]{1,0:T(8,128)(2,1)S(1)}, u32[]{:S(2)}, u32[]{:S(2)}) collective-permute-start(bf16[256,256]{1,0:T(8,128)(2,1)S(1)} %collective-permute-done.4.refs_6_), channel_id=1, source_target_pairs={{0,1},{1,0},{2,3},{3,2},{4,5},{5,4},{6,7},{7,6},{8,9},{9,8},{10,11... | collective-permute-start | bytes 393224 | tf_op jit(solution)/shard_map/ppermute | solution.py:534
  59.2 2.7 %copy-start.13 = (bf16[256,256]{1,0:T(8,128)(2,1)}, bf16[256,256]{1,0:T(8,128)(2,1)S(1)}, u32[]{:S(2)}) copy-start(bf16[256,256]{1,0:T(8,128)(2,1)S(1)} %collective-permute-done.5.refs_7_) | copy-start | bytes 393220
  59.2 2.7 %collective-permute-start.9 = (bf16[256,256]{1,0:T(8,128)(2,1)S(1)}, bf16[256,256]{1,0:T(8,128)(2,1)S(1)}, u32[]{:S(2)}, u32[]{:S(2)}) collective-permute-start(bf16[256,256]{1,0:T(8,128)(2,1)S(1)} %collective-permute-done.5.refs_7_), channel_id=1, source_target_pairs={{0,1},{1,0},{2,3},{3,2},{4,5},{5,4},{6,7},{7,6},{8,9},{9,8},{10,11... | collective-permute-start | bytes 393224 | tf_op jit(solution)/shard_map/ppermute | solution.py:534
  60.9 1.0 copy-start.14
  61.0 1.0 copy-start.15
  61.0 1.0 copy-start.16
  61.9 0.7 copy-start.17
  75.2 9.3 %copy-start.8 = (bf16[32,64,256]{2,1,0:T(8,128)(2,1)}, bf16[32,64,256]{2,1,0:T(8,128)(2,1)S(1)}, u32[]{:S(2)}) copy-start(bf16[32,64,256]{2,1,0:T(8,128)(2,1)S(1)} %all-to-all-done.1) | copy-start | bytes 3145732
  75.2 35.0 %all-to-all-start.2 = ((bf16[32,64,256]{2,1,0:T(8,128)(2,1)}), bf16[32,64,256]{2,1,0:T(8,128)(2,1)S(1)}, u32[]{:S(2)}, u32[]{:S(2)}) async-start(bf16[32,64,256]{2,1,0:T(8,128)(2,1)} %bitcast.47), calls=%async_computation.2 | async-start | bytes 2097152 | tf_op jit(solution)/shard_map/all_to_all | solution.py:381
  84.5 32.7 %copy-start.6 = (f32[1024,128]{1,0:T(8,128)S(1)}, f32[1024,128]{1,0:T(8,128)}, u32[]{:S(2)}) copy-start(f32[1024,128]{1,0:T(8,128)} %get-tuple-element.54.column_ref) | copy-start | bytes 1572868
  92.7 2.3 %collective-permute-start.11 = (f32[512,128]{1,0:T(8,128)}, f32[512,128]{1,0:T(8,128)S(1)}, u32[]{:S(2)}, u32[]{:S(2)}) collective-permute-start(f32[512,128]{1,0:T(8,128)} %get-tuple-element.51), channel_id=1, source_target_pairs={{0,1},{1,0},{2,3},{3,2},{4,5},{5,4},{6,7},{7,6},{8,9},{9,8},{10,11... | collective-permute-start | bytes 786440 | tf_op jit(solution)/shard_map/ppermute | solution.py:534
  96.0 4.7 %collective-permute-start.12 = (f32[128,128]{1,0:T(8,128)S(1)}, f32[128,128]{1,0:T(8,128)S(1)}, u32[]{:S(2)}, u32[]{:S(2)}) collective-permute-start(f32[128,128]{1,0:T(8,128)S(1)} %get-tuple-element.61), channel_id=1, source_target_pairs={{0,2},{2,4},{4,6},{6,0},{1,3},{3,5},{5,7},{7,1},{8,10},{10,12},{12... | collective-permute-start | bytes 196616 | tf_op jit(solution)/shard_map/ppermute | solution.py:549
  96.3 5.9 %collective-permute-start.13 = (f32[128,128]{1,0:T(8,128)S(1)}, f32[128,128]{1,0:T(8,128)S(1)}, u32[]{:S(2)}, u32[]{:S(2)}) collective-permute-start(f32[128,128]{1,0:T(8,128)S(1)} %get-tuple-element.60), channel_id=1, source_target_pairs={{0,4},{2,6},{4,0},{6,2},{1,5},{3,7},{5,1},{7,3},{8,12},{10,14},{12... | collective-permute-start | bytes 196616 | tf_op jit(solution)/shard_map/ppermute | solution.py:549
  98.9 4.1 %collective-permute-start.14 = (f32[128,128]{1,0:T(8,128)S(1)}, f32[128,128]{1,0:T(8,128)S(1)}, u32[]{:S(2)}, u32[]{:S(2)}) collective-permute-start(f32[128,128]{1,0:T(8,128)S(1)} %get-tuple-element.59), channel_id=1, source_target_pairs={{0,6},{2,0},{4,2},{6,4},{1,7},{3,1},{5,3},{7,5},{8,14},{10,8},{12,... | collective-permute-start | bytes 196616 | tf_op jit(solution)/shard_map/ppermute | solution.py:549
  103.0 5.5 %collective-permute-start.15 = (f32[32,128]{1,0:T(8,128)S(1)}, f32[32,128]{1,0:T(8,128)S(1)}, u32[]{:S(2)}, u32[]{:S(2)}) collective-permute-start(f32[32,128]{1,0:T(8,128)S(1)} %get-tuple-element.64), channel_id=1, source_target_pairs={{0,64},{64,128},{128,192},{192,0},{1,65},{65,129},{129,193},{193,1... | collective-permute-start | bytes 49160 | tf_op jit(solution)/shard_map/ppermute | solution.py:549
  104.6 4.5 %collective-permute-start.16 = (f32[32,128]{1,0:T(8,128)S(1)}, f32[32,128]{1,0:T(8,128)S(1)}, u32[]{:S(2)}, u32[]{:S(2)}) collective-permute-start(f32[32,128]{1,0:T(8,128)S(1)} %get-tuple-element.66), channel_id=1, source_target_pairs={{0,128},{64,192},{128,0},{192,64},{1,129},{65,193},{129,1},{193,65... | collective-permute-start | bytes 49160 | tf_op jit(solution)/shard_map/ppermute | solution.py:549
  107.1 3.2 %collective-permute-start.17 = (f32[32,128]{1,0:T(8,128)S(1)}, f32[32,128]{1,0:T(8,128)S(1)}, u32[]{:S(2)}, u32[]{:S(2)}) collective-permute-start(f32[32,128]{1,0:T(8,128)S(1)} %get-tuple-element.65), channel_id=1, source_target_pairs={{0,192},{64,0},{128,64},{192,128},{1,193},{65,1},{129,65},{193,129... | collective-permute-start | bytes 49160 | tf_op jit(solution)/shard_map/ppermute | solution.py:549
  110.9 14.2 %all-to-all-start.3 = ((f32[8,32,128]{2,1,0:T(8,128)}), f32[8,32,128]{2,1,0:T(8,128)S(1)}, u32[]{:S(2)}, u32[]{:S(2)}) async-start(f32[8,32,128]{2,1,0:T(8,128)} %broadcast_in_dim.27), calls=%async_computation.3 | async-start | bytes 262144 | tf_op jit(solution)/shard_map/all_to_all | solution.py:556
  136.4 7.2 %collective-permute-start.18 = (bf16[512,128]{1,0:T(8,128)(2,1)S(1)}, bf16[512,128]{1,0:T(8,128)(2,1)S(1)}, u32[]{:S(2)}, u32[]{:S(2)}) collective-permute-start(bf16[512,128]{1,0:T(8,128)(2,1)S(1)} %bitcast.50), channel_id=1, source_target_pairs={{0,1},{1,0},{2,3},{3,2},{4,5},{5,4},{6,7},{7,6},{8,9},{9,8},{10,11... | collective-permute-start | bytes 393224 | tf_op jit(solution)/shard_map/ppermute | solution.py:534
